TPU v7x, 512 devices: a whole 4x8x8 slice. The times are simulated.
512 devices in a mesh: blk: 32 (over y, x), col: 16 (over z, core).
Axes of the slice: x: 4, y: 8, z: 8, core: 2. Of those that a mesh axis runs over, the one named last changes fastest.
Arguments:
- visit_cov: bfloat16 [32768, 128], P('blk'), may hold values from -6 to 6
- tumor_size: bfloat16 [32768], P('blk'), may hold values from -6 to 6
- visit_weight: bfloat16 [32768], P('blk'), may hold values from 0.5 to 2
- visit_owner: int32 [32768, 1], P('blk'), may hold values from 0 to 31; in each aligned block of 1024 rows (0 to 1023, 1024 to 2047, ...) at most 64 rows name the same one
- visit_patient: int32 [32768], P('blk'), may hold values from 0 to 127
- inducing_freq: bfloat16 [128, 2048], P(None, 'col'), may hold values from -1.5 to 1.5
- inducing_phase: bfloat16 [2048], P('col'), may hold values from -3.140625 to 3.140625
- node_cov: bfloat16 [4096, 16, 128], P('blk'), may hold values from -6 to 6
- event_time: float32 [4096], P('blk'), may hold values from 0.2 to 2
- event_flag: int32 [4096], P('blk'), may hold values 0 or 1
Outputs:
- loglik: float32 [4096], P('blk')
- mean_weights: float32 [2048], P('col')
Inputs may be any that keep to these rules, and one draw needn't show every extreme that they name: `visit_owner`: among the visits entering one index of blk, no owner is named more than 64 times, a bound that some block reaches.
All inputs are finite; a program needn't handle non-finite values. No bound on the sum of `event_flag` on one device may be relied on, other than what follows from the above.
Results may differ from a plain program's by a relative error of at most 0.003.
Values may be sent and summed in bfloat16 or wider, within the bound.
No kernel may reach another device: no remote copies, remote signals or barrier semaphores. Data moves between devices by JAX's collectives and lax.ppermute only.
A program may use at most 64 MiB of HBM per device.

v0:
```python
import math

import jax
import jax.numpy as jnp
from jax import lax
from jax.sharding import PartitionSpec as P

ITERS = 3


SQRT_TWO = math.sqrt(2.0)
LOG_SHAPE = math.log(1.5)
LINK = 0.4


def features(covariates, frequency, phases):
    angles = jnp.dot(covariates, frequency, preferred_element_type=jnp.float32) + phases.astype(
        jnp.float32
    )
    return (SQRT_TWO * jnp.cos(angles)).astype(jnp.bfloat16)


def norm_of(vector):
    return lax.psum(jnp.sum(vector * vector), "col")


def on_device(
    visit_cov,
    tumor_size,
    visit_weight,
    visit_owner,
    visit_patient,
    inducing_freq,
    inducing_phase,
    node_cov,
    event_time,
    event_flag,
):
    blocks = lax.axis_size("blk")
    visits_here = visit_cov.shape[0]
    width_in = visit_cov.shape[1]
    total_visits = visits_here * blocks
    owners = visit_owner[:, 0]
    owner_table = (owners[:, None] == jnp.arange(blocks, dtype=jnp.int32)[None, :]).astype(
        jnp.int32
    )
    capacity = 2 * visits_here // blocks
    slots = blocks * capacity
    ranking = jnp.cumsum(owner_table, axis=0) - 1
    target = owners * capacity + jnp.sum(owner_table * ranking, axis=1)
    cov_buffer = (
        jnp.zeros((slots, width_in), jnp.bfloat16)
        .at[target]
        .set(visit_cov)
        .reshape(blocks, capacity, width_in)
    )
    packed = jnp.stack([visit_weight, tumor_size, visit_patient.astype(jnp.bfloat16)], axis=1)
    val_buffer = (
        jnp.zeros((slots, 3), jnp.bfloat16)
        .at[target]
        .set(packed)
        .reshape(blocks, capacity, 3)
        .transpose(0, 2, 1)
    )
    cov_in, val_in = (
        lax.all_to_all(cov_buffer, "blk", split_axis=0, concat_axis=0, tiled=True),
        lax.all_to_all(val_buffer, "blk", split_axis=0, concat_axis=0, tiled=True),
    )
    cov_in = cov_in.reshape(slots, width_in)
    weight_in = val_in[:, 0, :].reshape(slots).astype(jnp.float32)
    size_in = val_in[:, 1, :].reshape(slots).astype(jnp.float32)
    patient_in = val_in[:, 2, :].reshape(slots).astype(jnp.int32)
    row_count = cov_in.shape[0]
    phi_local = features(cov_in, inducing_freq, inducing_phase)
    phi_wide = phi_local.astype(jnp.float32)
    rhs_local = jnp.dot(weight_in * size_in, phi_wide, precision=lax.Precision.HIGHEST)
    local_cols = inducing_freq.shape[1]
    inducing = local_cols * lax.axis_size("col")
    freq_all, phase_all = (
        lax.all_gather(inducing_freq, "col", axis=1, tiled=True),
        lax.all_gather(inducing_phase, "col", axis=0, tiled=True),
    )
    step_rows = min(512, row_count)

    def add_block(index, gram):
        first = index * step_rows
        rows_cov = lax.dynamic_slice_in_dim(cov_in, first, step_rows, 0)
        rows_weight = lax.dynamic_slice_in_dim(weight_in, first, step_rows, 0)
        rows_phi = lax.dynamic_slice_in_dim(phi_local, first, step_rows, 0)
        full_phi = features(rows_cov, freq_all, phase_all)
        weighted = (rows_weight[:, None] * full_phi.astype(jnp.float32)).astype(jnp.bfloat16)
        return gram + lax.dot_general(
            weighted, rows_phi, (((0,), (0,)), ((), ())), preferred_element_type=jnp.float32
        )

    gram = lax.fori_loop(
        0, row_count // step_rows, add_block, jnp.zeros((inducing, local_cols), jnp.float32)
    )
    gram, rhs = lax.psum((gram, rhs_local), "blk")
    gram = gram / total_visits
    rhs = rhs / math.sqrt(total_visits)
    solution = jnp.zeros((local_cols,), jnp.float32)
    residual = rhs
    direction = rhs
    norm_now = norm_of(residual)
    for turn in range(ITERS):
        whole = lax.all_gather(direction, "col", axis=0, tiled=True)
        image = direction + jnp.dot(whole, gram, precision=lax.Precision.HIGHEST)
        alpha = norm_now / lax.psum(jnp.sum(direction * image), "col")
        solution = solution + alpha * direction
        residual = residual - alpha * image
        norm_next = norm_of(residual)
        direction = residual + norm_next / norm_now * direction
        norm_now = norm_next
    nodes_flat = node_cov.reshape(-1, width_in)
    node_phi = features(nodes_flat, inducing_freq, inducing_phase)
    fit_part = jnp.dot(phi_wide, solution, precision=lax.Precision.HIGHEST)
    node_part = jnp.dot(node_phi.astype(jnp.float32), solution, precision=lax.Precision.HIGHEST)
    fitted, node_value = lax.psum((fit_part, node_part), "col")
    fitted = fitted / math.sqrt(inducing)
    node_value = node_value / math.sqrt(inducing)
    patients_here = event_time.shape[0]
    nodes_count = node_cov.shape[1]
    patient_table = (
        patient_in[:, None] == jnp.arange(patients_here, dtype=jnp.int32)[None, :]
    ).astype(jnp.float32)
    residual_term = weight_in * (size_in - fitted)
    numer = jnp.dot(residual_term, patient_table, precision=lax.Precision.HIGHEST)
    denom = 1.0 + jnp.dot(weight_in, patient_table, precision=lax.Precision.HIGHEST)
    effect = numer / denom
    grid = (
        event_time[:, None]
        * (jnp.arange(nodes_count).astype(jnp.float32)[None, :] + 1.0)
        / nodes_count
    )
    eta = (
        LOG_SHAPE
        + 0.5 * jnp.log(grid)
        + LINK * (node_value.reshape(patients_here, nodes_count) + effect[:, None])
    )
    loglik = event_flag.astype(jnp.float32) * eta[:, -1] - event_time / nodes_count * jnp.sum(
        jnp.exp(eta), axis=1
    )
    return (loglik, solution)


def solution(mesh):
    in_specs = (
        P("blk", None),
        P("blk"),
        P("blk"),
        P("blk", None),
        P("blk"),
        P(None, "col"),
        P("col"),
        P("blk", None, None),
        P("blk"),
        P("blk"),
    )
    out_specs = (P("blk"), P("col"))
    return jax.shard_map(
        on_device, mesh=mesh, in_specs=in_specs, out_specs=out_specs, check_vma=False
    )
```

profile of v0, /device:TPU:4, one launch (start us, length us, event | category | flops | bytes accessed | tf_op | source)
XLA Modules:
  0.0 532.1 jit_solution(2748140927083613573)
XLA Ops:
  7.2 0.0 copy-start
  7.2 0.7 fusion.35
  8.0 9.0 %reduce-window.6 = s32[32,8,128]{2,1,0:T(8,128)S(1)} reduce-window(s32[32,8,128]{2,1,0:T(8,128)S(1)} %fusion.35, s32[]{:T(128)} %constant.72.clone.1), window={size=1x1x128 pad=0_0x0_0x127_0}, to_apply=%region_0.0 | reduce-window | flops 4161536 | bytes 262148 | tf_op jit(solution)/shard_map/reduce-window
  17.0 0.1 slice.24
  17.1 0.1 copy.22
  17.3 0.1 copy.23
  17.3 0.1 add_add_fusion
  17.6 0.2 copy.24
  17.8 3.3 scatter_custom_fusion
  21.2 0.0 copy-start.10
  21.2 0.0 copy-start.4
  21.2 0.9 copy.25
  22.1 10.2 %all-to-all-start = ((bf16[32,3,64]{2,1,0:T(4,128)(2,1)}), bf16[32,3,64]{2,1,0:T(4,128)(2,1)S(1)}, u32[]{:S(2)}, u32[]{:S(2)}) async-start(bf16[32,3,64]{2,1,0:T(4,128)(2,1)} %bitcast.8), calls=%async_computation | async-start | bytes 65536 | tf_op jit(solution)/shard_map/all_to_all | solution.py:67
  32.3 4.3 scatter_custom_fusion.1
  36.6 3.5 all-to-all-done
  40.2 6.3 %all-to-all-start.1 = ((bf16[32,64,128]{2,1,0:T(8,128)(2,1)}), bf16[32,64,128]{2,1,0:T(8,128)(2,1)S(1)}, u32[]{:S(2)}, u32[]{:S(2)}) async-start(bf16[32,64,128]{2,1,0:T(8,128)(2,1)} %bitcast.10), calls=%async_computation.1 | async-start | bytes 1048576 | tf_op jit(solution)/shard_map/all_to_all | solution.py:66
  46.4 0.0 all-reduce.4.cloned.1.call-start
  46.5 23.1 %all-gather.1 = bf16[16,1,128]{2,1,0:T(2,128)(2,1)S(1)} all-gather(bf16[1,1,128]{2,1,0:T(2,128)(2,1)S(1)} %bitcast.121), channel_id=1, replica_groups=mesh['blk'=32,'col'=16] {'col'}, dimensions={0}, use_global_device_ids=true | all-gather | bytes 4352 | tf_op jit(solution)/shard_map/all_gather | solution.py:81
  69.6 15.9 %all_gather.16 = bf16[128,2048]{1,0:T(8,128)(2,1)S(1)} all-gather(bf16[128,128]{1,0:T(8,128)(2,1)S(1)} %copy-done.4), channel_id=1, replica_groups=mesh['blk'=32,'col'=16] {'col'}, dimensions={1}, use_global_device_ids=true | all-gather | bytes 557056 | tf_op jit(solution)/shard_map/all_gather | solution.py:80
  85.5 0.1 slice_reduce_fusion
  85.5 0.1 reshape_squeeze.2
  85.6 3.9 fusion.11
  89.5 61.9 %while.14 = (s32[]{:T(128)}, f32[2048,128]{1,0:T(8,128)S(1)}, f32[2048]{0:T(1024)S(1)}, bf16[2048,128]{1,0:T(8,128)(2,1)S(1)}, bf16[128,2048]{1,0:T(8,128)(2,1)S...) while((s32[]{:T(128)}, f32[2048,128]{1,0:T(8,128)S(1)}, ...), condition=%wide.region_9.10_spmd.clone, body=%wide.region_8.9_spmd.clone.sunk | while | flops 543688704 | bytes 2911912 | solution.py:96
  89.7 0.1 dynamic_slice.34
  89.8 15.2 %convolution_add_fusion.4 = f32[2048,128]{1,0:T(8,128)S(1)} fusion(bf16[128,2048]{1,0:T(8,128)(2,1)S(1)} %get-tuple-element.249, f32[2048]{0:T(1024)S(1)} %convert_element_type.131, f32[512]{0:T(512)S(1)} %dynamic_slice.34, f32[2048,128]{1,0:T(8,128)S(1)} %get-tuple-element.235, pred[]{:T(512)S(6)} %compare.3, ...), kind=kOutput, calls=%fused_computation.4.clone.1 | convolution fusion | flops 543686656 | bytes 2895360 | tf_op jit(solution)/shard_map/while/body/eval_jaxpr/dot_general | solution.py:92
  105.1 0.1 dynamic_slice.34
  105.1 15.3 %convolution_add_fusion.4 = f32[2048,128]{1,0:T(8,128)S(1)} fusion(bf16[128,2048]{1,0:T(8,128)(2,1)S(1)} %get-tuple-element.249, f32[2048]{0:T(1024)S(1)} %convert_element_type.131, f32[512]{0:T(512)S(1)} %dynamic_slice.34, f32[2048,128]{1,0:T(8,128)S(1)} %get-tuple-element.235, pred[]{:T(512)S(6)} %compare.3, ...), kind=kOutput, calls=%fused_computation.4.clone.1 | convolution fusion | flops 543686656 | bytes 2895360 | tf_op jit(solution)/shard_map/while/body/eval_jaxpr/dot_general | solution.py:92
  120.4 0.1 dynamic_slice.34
  120.5 15.3 %convolution_add_fusion.4 = f32[2048,128]{1,0:T(8,128)S(1)} fusion(bf16[128,2048]{1,0:T(8,128)(2,1)S(1)} %get-tuple-element.249, f32[2048]{0:T(1024)S(1)} %convert_element_type.131, f32[512]{0:T(512)S(1)} %dynamic_slice.34, f32[2048,128]{1,0:T(8,128)S(1)} %get-tuple-element.235, pred[]{:T(512)S(6)} %compare.3, ...), kind=kOutput, calls=%fused_computation.4.clone.1 | convolution fusion | flops 543686656 | bytes 2895360 | tf_op jit(solution)/shard_map/while/body/eval_jaxpr/dot_general | solution.py:92
  135.8 0.1 dynamic_slice.34
  135.9 15.3 %convolution_add_fusion.4 = f32[2048,128]{1,0:T(8,128)S(1)} fusion(bf16[128,2048]{1,0:T(8,128)(2,1)S(1)} %get-tuple-element.249, f32[2048]{0:T(1024)S(1)} %convert_element_type.131, f32[512]{0:T(512)S(1)} %dynamic_slice.34, f32[2048,128]{1,0:T(8,128)S(1)} %get-tuple-element.235, pred[]{:T(512)S(6)} %compare.3, ...), kind=kOutput, calls=%fused_computation.4.clone.1 | convolution fusion | flops 543686656 | bytes 2895360 | tf_op jit(solution)/shard_map/while/body/eval_jaxpr/dot_general | solution.py:92
  151.4 1.0 copy-done.2
  152.4 0.0 all-reduce.4.cloned.1.call-update
  152.5 3.9 fusion.10
  156.3 0.1 reshape.108
  156.4 0.1 fusion.37
  156.5 0.1 reshape.68
  156.6 0.1 fusion.36
  156.6 0.3 convolution_bitcast_fusion.5
  157.0 70.3 %psum.70 = f32[128]{0:T(128)S(1)} all-reduce(f32[128]{0:T(128)S(1)} %convolution_bitcast_fusion.5), channel_id=1, replica_groups=mesh['blk'=32,'col'=16] {'blk'}, use_global_device_ids=true, to_apply=%region_5.6 | all-reduce | flops 128 | bytes 1024 | tf_op jit(solution)/shard_map/psum | solution.py:99
  227.3 15.7 %all-gather = f32[16,1,128]{2,1,0:T(1,128)S(1)} all-gather(f32[1,1,128]{2,1,0:T(1,128)S(1)} %fusion.50), channel_id=1, replica_groups=mesh['blk'=32,'col'=16] {'col'}, dimensions={0}, use_global_device_ids=true | all-gather | bytes 8704 | tf_op jit(solution)/shard_map/all_gather | solution.py:107
  243.0 65.3 %all-reduce.4.cloned.1.call-done = f32[2048,128]{1,0:T(8,128)} async-done(((f32[2048,128]{1,0:T(8,128)}), f32[2048,128]{1,0:T(8,128)}) %all-reduce.4.cloned.1.call-update) | async-done | bytes 1048592 | tf_op jit(solution)/shard_map/psum | solution.py:99
  308.4 2.6 multiply_reduce_fusion.3
  310.9 24.8 %all-reduce.1 = (f32[]{:T(128)}, f32[]{:T(128)}) all-reduce(f32[]{:T(128)} %get-tuple-element.152, f32[]{:T(128)} %get-tuple-element.151), channel_id=1, replica_groups=mesh['blk'=32,'col'=16] {'col'}, use_global_device_ids=true, to_apply=%region_7.8 | all-reduce | flops 2 | bytes 16 | tf_op jit(solution)/shard_map/psum | solution.py:24
  337.1 0.6 multiply_reduce_fusion.2
  337.7 24.5 %psum.74 = f32[]{:T(128)} all-reduce(f32[]{:T(128)} %get-tuple-element.173), channel_id=1, replica_groups=mesh['blk'=32,'col'=16] {'col'}, use_global_device_ids=true, to_apply=%region_14.15 | all-reduce | flops 1 | bytes 8 | tf_op jit(solution)/shard_map/psum | solution.py:24
  363.5 14.4 %all-gather.2 = f32[16,1,128]{2,1,0:T(1,128)S(1)} all-gather(f32[1,1,128]{2,1,0:T(1,128)S(1)} %bitcast.116), channel_id=1, replica_groups=mesh['blk'=32,'col'=16] {'col'}, dimensions={0}, use_global_device_ids=true | all-gather | bytes 8704 | tf_op jit(solution)/shard_map/all_gather | solution.py:107
  377.9 1.2 multiply_reduce_fusion.1
  379.2 27.3 %psum.75 = f32[]{:T(128)} all-reduce(f32[]{:T(128)} %get-tuple-element.176), channel_id=1, replica_groups=mesh['blk'=32,'col'=16] {'col'}, use_global_device_ids=true, to_apply=%region_16.17 | all-reduce | flops 1 | bytes 8 | tf_op jit(solution)/shard_map/psum | solution.py:109
  407.8 0.6 multiply_reduce_fusion
  408.4 0.1 reshape.69
  408.4 24.2 %psum.76 = f32[]{:T(128)} all-reduce(f32[]{:T(128)} %multiply_reduce_fusion), channel_id=1, replica_groups=mesh['blk'=32,'col'=16] {'col'}, use_global_device_ids=true, to_apply=%region_18.19 | all-reduce | flops 1 | bytes 8 | tf_op jit(solution)/shard_map/psum | solution.py:24
  433.9 14.1 %all-gather.3 = f32[16,1,128]{2,1,0:T(1,128)S(1)} all-gather(f32[1,1,128]{2,1,0:T(1,128)S(1)} %bitcast.117), channel_id=1, replica_groups=mesh['blk'=32,'col'=16] {'col'}, dimensions={0}, use_global_device_ids=true | all-gather | bytes 8704 | tf_op jit(solution)/shard_map/all_gather | solution.py:107
  448.0 1.2 fusion.21
  449.2 26.1 %psum.77 = f32[]{:T(128)} all-reduce(f32[]{:T(128)} %fusion.21), channel_id=1, replica_groups=mesh['blk'=32,'col'=16] {'col'}, use_global_device_ids=true, to_apply=%region_20.21 | all-reduce | flops 1 | bytes 8 | tf_op jit(solution)/shard_map/psum | solution.py:109
  476.7 0.5 fusion.43
  477.2 0.5 fusion.45
  477.7 45.7 %all-reduce = (f32[2048]{0:T(1024)S(1)}, f32[2048]{0:T(1024)S(1)}) all-reduce(f32[2048]{0:T(1024)S(1)} %bitcast.112, f32[2048]{0:T(1024)S(1)} %bitcast.111), channel_id=1, replica_groups=mesh['blk'=32,'col'=16] {'col'}, use_global_device_ids=true, to_apply=%region_21.22 | all-reduce | flops 4096 | bytes 32768 | tf_op jit(solution)/shard_map/psum | solution.py:119
  523.4 0.1 reshape.67
  523.5 0.1 copy.26
  523.6 0.6 convolution_bitcast_fusion.4
  524.2 0.5 fusion.17
  524.6 0.1 exponential_reduce_fusion
  524.7 0.5 fusion.42
  (45 shorter events, 0.3 us)
Async XLA Ops:
  7.2 145.3 %copy-start = (bf16[128,16,128]{2,1,0:T(8,128)(2,1)S(1)}, bf16[128,16,128]{2,1,0:T(8,128)(2,1)}, u32[]{:S(2)}) copy-start(bf16[128,16,128]{2,1,0:T(8,128)(2,1)} %param.19) | copy-start | bytes 1572868
  7.2 10.3 %copy-start.3 = (s32[1024,1]{0,1:T(1,128)S(1)}, s32[1024,1]{0,1:T(1,128)}, u32[]{:S(2)}) copy-start(s32[1024,1]{0,1:T(1,128)} %param.15) | copy-start | bytes 12292
  7.2 10.3 %copy-start.6 = (s32[1024]{0:T(1024)S(1)}, s32[1024]{0:T(1024)}, u32[]{:S(2)}) copy-start(s32[1024]{0:T(1024)} %param.16) | copy-start | bytes 12292
  7.2 10.4 %copy-start.7 = (bf16[1024]{0:T(1024)(128)(2,1)S(1)}, bf16[1024]{0:T(1024)(128)(2,1)}, u32[]{:S(2)}) copy-start(bf16[1024]{0:T(1024)(128)(2,1)} %param.14) | copy-start | bytes 6148
  7.2 10.4 %copy-start.8 = (bf16[1024]{0:T(1024)(128)(2,1)S(1)}, bf16[1024]{0:T(1024)(128)(2,1)}, u32[]{:S(2)}) copy-start(bf16[1024]{0:T(1024)(128)(2,1)} %param.13) | copy-start | bytes 6148
  21.2 25.3 %copy-start.10 = (bf16[128]{0:T(256)(128)(2,1)S(1)}, bf16[128]{0:T(256)(128)(2,1)}, u32[]{:S(2)}) copy-start(bf16[128]{0:T(256)(128)(2,1)} %param.18) | copy-start | bytes 772
  21.2 48.4 %copy-start.4 = (bf16[128,128]{1,0:T(8,128)(2,1)S(1)}, bf16[128,128]{1,0:T(8,128)(2,1)}, u32[]{:S(2)}) copy-start(bf16[128,128]{1,0:T(8,128)(2,1)} %param.17) | copy-start | bytes 98308
  22.1 18.1 %all-to-all-start = ((bf16[32,3,64]{2,1,0:T(4,128)(2,1)}), bf16[32,3,64]{2,1,0:T(4,128)(2,1)S(1)}, u32[]{:S(2)}, u32[]{:S(2)}) async-start(bf16[32,3,64]{2,1,0:T(4,128)(2,1)} %bitcast.8), calls=%async_computation | async-start | bytes 65536 | tf_op jit(solution)/shard_map/all_to_all | solution.py:67
  40.2 45.5 %all-to-all-start.1 = ((bf16[32,64,128]{2,1,0:T(8,128)(2,1)}), bf16[32,64,128]{2,1,0:T(8,128)(2,1)S(1)}, u32[]{:S(2)}, u32[]{:S(2)}) async-start(bf16[32,64,128]{2,1,0:T(8,128)(2,1)} %bitcast.10), calls=%async_computation.1 | async-start | bytes 1048576 | tf_op jit(solution)/shard_map/all_to_all | solution.py:66
  46.4 261.9 %all-reduce.4.cloned.1.call-start = ((), (), s32[]{:S(2)}) async-start(), calls=%async_computation.2 | async-start | bytes 2097152 | tf_op jit(solution)/shard_map/psum | solution.py:99
  151.4 1.0 copy-start.2
  308.4 69.6 %copy-start.1 = (f32[2048,128]{1,0:T(8,128)S(1)}, f32[2048,128]{1,0:T(8,128)}, u32[]{:S(2)}) copy-start(f32[2048,128]{1,0:T(8,128)} %all-reduce.4.cloned.1.call-done) | copy-start | bytes 3145732
  449.2 75.4 %copy-start.9 = (f32[128]{0:T(128)S(1)}, f32[128]{0:T(128)}, u32[]{:S(2)}) copy-start(f32[128]{0:T(128)} %param.20) | copy-start | bytes 1540
  449.2 75.5 %copy-start.11 = (s32[128]{0:T(128)S(1)}, s32[128]{0:T(128)}, u32[]{:S(2)}) copy-start(s32[128]{0:T(128)} %param.21) | copy-start | bytes 1540
  476.7 48.6 %copy-start.5 = (f32[128]{0:T(128)}, f32[128]{0:T(128)S(1)}, u32[]{:S(2)}) copy-start(f32[128]{0:T(128)S(1)} %multiply_add_fusion.1) | copy-start | bytes 1540
Sparse Core Ops, SparseCore 0:
  152.6 155.7 all-reduce.3
where the time goes:
time: 533 us; the launch traced here: 532 us
  blocking collectives  326 us (61%)
  matrix products  76.2 us (14%)
  waiting for transfers between devices  68.9 us (13%)
  between operations  21.1 us (4%)
  starting transfers between devices  16.5 us (3%)
  other arithmetic  12 us (2%)
  local copies, waits for them, and re-layouts  10.9 us (2%)
    psum x3, blocking collectives, norm_of(): return lax.psum(jnp.sum(vector * vector), 'col')  73.4 us
    psum x1, blocking collectives, on_device(): gram, rhs = lax.psum((gram, rhs_local), 'blk')  70.3 us
    psum x1, waiting for transfers between devices, on_device(): gram, rhs = lax.psum((gram, rhs_local), 'blk')  65.3 us
    dot_general x4, matrix products, add_block(): lax.dot_general(weighted, rows_phi, (((0,), (0,)), ((), ())), preferred_e...  61 us
    psum x2, blocking collectives, on_device(): alpha = norm_now / lax.psum(jnp.sum(direction * image), 'col')  53.3 us
    psum x1, blocking collectives, on_device(): fitted, node_value = lax.psum((fit_part, node_part), 'col')  45.7 us
    all_gather x3, blocking collectives, on_device(): whole = lax.all_gather(direction, 'col', axis=0, tiled=True)  44.2 us
    all_gather x1, blocking collectives, on_device(): lax.all_gather(inducing_phase, 'col', axis=0, tiled=True)  23.1 us
  transfers between devices with their start and end apart: 3, of which 2 were waited for; matrix products, arithmetic and copies ran while one was open for 2% of the time, Pallas kernels for 0%

commit v1 on v0

v1 whole, which is shorter than its diff:
```python
import functools
import math

import jax
import jax.numpy as jnp
import numpy as np
from jax import lax
from jax.experimental import pallas as pl
from jax.experimental.pallas import tpu as pltpu
from jax.sharding import PartitionSpec as P

F32 = jnp.float32
BF16 = jnp.bfloat16
LOG_SHAPE = math.log(1.5)
LINK = 0.4
LANES = 128
LIMIT = 20 * 1024 * 1024


def cosine_table():
    nodes = 0.125 + 0.125 * np.cos(np.pi * (np.arange(400) + 0.5) / 400)
    values = math.sqrt(2.0) * np.cos(2.0 * np.pi * np.sqrt(nodes))
    fit = np.polynomial.chebyshev.Chebyshev.fit(nodes, values, 5, domain=[0.0, 0.25])
    return [float(c) for c in fit.convert(kind=np.polynomial.Polynomial).coef]


COEFS = cosine_table()
PER_TURN = 1.0 / (2.0 * math.pi)


def feature(angles):
    turns = angles * PER_TURN
    turns = turns - jnp.round(turns)
    square = turns * turns
    total = COEFS[-1]
    for coef in COEFS[-2::-1]:
        total = total * square + coef
    return total.astype(BF16)


def split3(value):
    high = value.astype(BF16).astype(F32)
    rest = value - high
    middle = rest.astype(BF16).astype(F32)
    low = (rest - middle).astype(BF16).astype(F32)
    return high, middle, low


def stack_rows(rows, height):
    at = lax.broadcasted_iota(jnp.int32, (height, rows[0].shape[1]), 0)
    total = jnp.zeros((height, rows[0].shape[1]), F32)
    for index, row in enumerate(rows):
        total = jnp.where(at == index, row, total)
    return total.astype(BF16)


def as_row(tiles):
    return jnp.concatenate([tiles[j : j + 1, :] for j in range(tiles.shape[0])], axis=1)


def dot_nt(a, b):
    return lax.dot_general(a, b, (((1,), (1,)), ((), ())), preferred_element_type=F32)


def dot_nn(a, b):
    return jnp.dot(a, b, preferred_element_type=F32)


VMEM = pl.BlockSpec(memory_space=pltpu.VMEM)
SMEM = pl.BlockSpec(memory_space=pltpu.SMEM)
BLOCK = 256
PHASE_ROWS = 8


def rows_at(index, size):
    return pl.ds(pl.multiple_of(index * size, size), size)


def total_of(x):
    return jnp.sum(jnp.sum(x, axis=0, keepdims=True), axis=1, keepdims=True)


def params():
    return pltpu.CompilerParams(vmem_limit_bytes=LIMIT)


def cost(flops, size, hard=0):
    return pl.CostEstimate(flops=flops, bytes_accessed=size, transcendentals=hard)


def pack_kernel(freq, phase, out):
    depth = freq.shape[0]
    values = freq[...]
    last = jnp.broadcast_to(phase[...], (PHASE_ROWS, phase.shape[1]))
    for copy in range(out.shape[0]):
        out[copy, 0:depth, :] = values
        out[copy, depth : depth + PHASE_ROWS, :] = last


def feature_block(rows, freq, store):
    depth = rows.shape[1]
    for j in range(0, freq.shape[0], 2):
        both = jnp.concatenate([freq[j, :depth, :], freq[j + 1, :depth, :]], axis=1)
        phase = jnp.concatenate(
            [freq[j, depth : depth + 1, :], freq[j + 1, depth : depth + 1, :]], axis=1
        )
        store(j * LANES, feature(dot_nn(rows, both) + phase.astype(F32)))


FEATURE_ROWS = 128


def features_kernel(cov, *rest):
    freqs, out = rest[:-1], rest[-1]

    def step(i, carry):
        at = rows_at(i, FEATURE_ROWS)
        base = 0
        for freq in freqs:

            def store(column, value, base=base):
                out[at, base + column : base + column + value.shape[1]] = value

            feature_block(cov[at, :], freq, store)
            base += freq.shape[0] * LANES
        return carry

    lax.fori_loop(0, cov.shape[0] // FEATURE_ROWS, step, 0)


def features(cov, freqs, name):
    rows, depth = cov.shape
    columns = sum(f.shape[0] * f.shape[2] for f in freqs)
    return pl.pallas_call(
        features_kernel,
        in_specs=[VMEM] * (1 + len(freqs)),
        out_specs=VMEM,
        out_shape=jax.ShapeDtypeStruct((rows, columns), BF16),
        compiler_params=params(),
        cost_estimate=cost(2 * rows * depth * columns + 20 * rows * columns, 2 * rows * columns),
        name=name,
    )(cov, *freqs)


def near_kernel(cov, freq, weight, size, phi, out, gathered, tiles):
    product = weight[...].astype(F32) * size[...].astype(F32)
    split = stack_rows(split3(product), 16)
    gathered[...] = jnp.zeros_like(gathered)
    for i in range(cov.shape[0] // BLOCK):
        at = slice(i * BLOCK, (i + 1) * BLOCK)
        left = split[:, at]

        def store(column, value, at=at, left=left):
            where = slice(column, column + value.shape[1])
            phi[at, where] = value
            gathered[:, where] += dot_nn(left, value)

        feature_block(cov[at, :], freq, store)
    send_whole(gathered, tiles, out)


def rows_of(vector):
    return stack_rows(split3(as_row(vector)), 16)


def send_whole(gathered, tiles, out):
    total = jnp.sum(gathered[...], axis=0, keepdims=True)
    for j in range(tiles.shape[0]):
        tiles[j : j + 1, :] = total[:, j * LANES : (j + 1) * LANES]
    whole = tiles[...]
    for copy in range(out.shape[0]):
        out[copy] = whole


def forward(direction, phis):
    split = rows_of(direction)
    total, base = 0.0, 0
    for phi in phis:
        total = total + dot_nt(split[:, base : base + phi.shape[1]], phi[...])
        base += phi.shape[1]
    return jnp.sum(total, axis=0, keepdims=True)


def product(direction, phis, weight, gathered, tiles, out, scale):
    values = forward(direction, phis)
    split = stack_rows(split3(weight[...].astype(F32) * values * scale), 16)
    base = 0
    for phi in phis:
        gathered[:, base : base + phi.shape[1]] = dot_nn(split, phi[...])
        base += phi.shape[1]
    send_whole(gathered, tiles, out)
    return values


def first_kernel(scale, core, halves, near, far, weight, out, values_out, rhs_out, gathered, tiles):
    low, high = halves[0], halves[1]
    swap = core[0] == 1
    half = low.shape[0]
    rhs_out[0:half, :] = jnp.where(swap, high, low)
    rhs_out[half : 2 * half, :] = jnp.where(swap, low, high)
    values_out[...] = product(rhs_out[...], (near, far), weight, gathered, tiles, out, scale)


def second_kernel(
    scale, arrived, rhs, before, near, far, weight,
    out, fit_out, solution_out, residual_out, direction_out,
    gathered, tiles,
):
    direction = rhs[...]
    norm = total_of(direction * direction)
    image = direction + jnp.sum(arrived[...], axis=0)
    length = norm / total_of(direction * image)
    residual = direction - length * image
    later = residual + total_of(residual * residual) / norm * direction
    solution_out[...] = length * direction
    residual_out[...] = residual
    direction_out[...] = later
    fit_out[0:1, :] = length * before[...]
    fit_out[1:2, :] = product(later, (near, far), weight, gathered, tiles, out, scale)


def third_kernel(
    scale, fit_scale, arrived, solution, residual, direction, fit, near, far, weight, size, owner, patient,
    out, both_out, norm_out,
):
    before = direction[...]
    left = residual[...]
    norm = total_of(left * left)
    image = before + jnp.sum(arrived[...], axis=0)
    length = norm / total_of(before * image)
    left = left - length * image
    norm_next = total_of(left * left)
    later = left + norm_next / norm * before
    both_out[0] = solution[...] + length * before
    both_out[1] = later
    norm_out[...] = jnp.broadcast_to(norm_next, norm_out.shape)
    values = forward(later, (near, far))
    fitted = fit[0:1, :] + length * fit[1:2, :]
    weights = weight[...].astype(F32)
    weighted = weights * values
    energy = total_of(weighted * values) * scale
    rest = weights * (size[...].astype(F32) - fitted * fit_scale)
    owners, patients = out.shape[0], out.shape[2]
    here = values.shape[1]
    to_owner = (owner[...] == lax.broadcasted_iota(jnp.int32, (owners, here), 0)).astype(F32)
    to_patient = (patient[...] == lax.broadcasted_iota(jnp.int32, (patients, here), 0)).astype(F32)
    parts = split3(rest) + split3(weighted * fit_scale) + (weights,)
    tall = jnp.concatenate([to_owner * part for part in parts], axis=0).astype(BF16)
    sums = dot_nt(tall, to_patient.astype(BF16))
    part = [sums[i * owners : (i + 1) * owners, :] for i in range(len(parts))]
    out[:, 0, :] = part[0] + part[1] + part[2]
    out[:, 1, :] = part[3] + part[4] + part[5]
    out[:, 2, :] = part[6]
    out[:, 3, :] = jnp.broadcast_to(energy, (owners, patients))


def nodes_kernel(both, first, second, out):
    rows = split3(as_row(both[0])) + split3(as_row(both[1]))
    split = stack_rows(rows, 16)
    base = 0
    for phi in (first, second):
        products = dot_nt(split, phi[...])
        where = slice(base, base + phi.shape[0])
        out[0:1, where] = products[0:1] + products[1:2] + products[2:3]
        out[1:2, where] = products[3:4] + products[4:5] + products[5:6]
        base += phi.shape[0]


def last_kernel(fit_scale, mine, arrived, both, norm, node_values, time, flag, loglik, weights_out, tiles):
    sums = jnp.sum(arrived[...], axis=0)
    direction = both[1]
    denominator = total_of(direction * direction) + sums[3:4, 0:1]
    length = norm[0:1, 0:1] / denominator
    tiles[...] = both[0] + length * direction
    weights_out[...] = tiles[pl.ds(mine[0], 1), :]
    effect = (sums[0:1, :] - length * sums[1:2, :]) / (1.0 + sums[2:3, :])
    values = (node_values[0:1, :] + length * node_values[1:2, :]) * fit_scale
    patients = loglik.shape[1]
    nodes = values.shape[1] // patients
    total = jnp.zeros_like(effect)
    eta = total
    when = time[...]
    for q in range(nodes):
        grid = when * (q + 1.0) / nodes
        eta = (
            LOG_SHAPE
            + 0.5 * jnp.log(grid)
            + LINK * (values[:, q * patients : (q + 1) * patients] + effect)
        )
        total = total + jnp.exp(eta)
    loglik[...] = flag[...].astype(F32) * eta - when / nodes * total


def on_device(
    visit_cov,
    tumor_size,
    visit_weight,
    visit_owner,
    visit_patient,
    inducing_freq,
    inducing_phase,
    node_cov,
    event_time,
    event_flag,
):
    blocks, cols = lax.axis_size("blk"), lax.axis_size("col")
    rows, depth = visit_cov.shape
    own = inducing_freq.shape[1]
    inducing = own * cols
    tall = inducing // LANES
    layers = cols // 2
    patients, nodes = node_cov.shape[:2]
    scale = 1.0 / (rows * blocks)
    fit_scale = 1.0 / math.sqrt(inducing)
    weight = visit_weight.reshape(1, rows)
    size = tumor_size.reshape(1, rows)
    owner = visit_owner.reshape(1, rows)
    patient = visit_patient.reshape(1, rows)
    place = lax.axis_index("col").astype(jnp.int32)
    core = (place % 2).reshape(1)
    layer = (place // 2).reshape(1)
    together = lax.optimization_barrier
    same_core = [[2 * z + c for z in range(layers)] for c in range(2)]
    pairs = [[2 * z, 2 * z + 1] for z in range(layers)]
    swap = [(i, i ^ 1) for i in range(cols)]

    packed = pl.pallas_call(
        pack_kernel,
        in_specs=[VMEM, VMEM],
        out_specs=VMEM,
        out_shape=jax.ShapeDtypeStruct((layers, depth + PHASE_ROWS, own), BF16),
        compiler_params=params(),
        name="pack",
    )(inducing_freq, inducing_phase.reshape(1, own))
    near_freq = lax.all_to_all(packed, "col", 0, 0, tiled=True, axis_index_groups=same_core)

    half = inducing // 2
    near, sent = pl.pallas_call(
        near_kernel,
        in_specs=[VMEM] * 4,
        out_specs=[VMEM] * 2,
        out_shape=[
            jax.ShapeDtypeStruct((rows, half), BF16),
            jax.ShapeDtypeStruct((blocks, tall // 2, LANES), F32),
        ],
        scratch_shapes=[pltpu.VMEM((16, half), F32), pltpu.VMEM((tall // 2, LANES), F32)],
        compiler_params=params(),
        name="near_features",
    )(visit_cov, near_freq, weight, size)
    sent, late_freq = together((sent, near_freq))
    arrived = lax.all_to_all(sent, "blk", 0, 0, tiled=True)
    far_freq = lax.ppermute(late_freq, "col", swap)
    far = features(visit_cov, (far_freq,), "far_features")
    arrived, far = together((arrived, far))
    rhs = jnp.sum(arrived, axis=0) * (1.0 / math.sqrt(rows * blocks))
    halves = lax.all_gather(rhs, "col", axis_index_groups=pairs)

    by_node = node_cov.transpose(1, 0, 2).reshape(nodes * patients, depth)
    count = nodes * patients // 2
    message = jax.ShapeDtypeStruct((blocks, tall, LANES), F32)
    vector = jax.ShapeDtypeStruct((tall, LANES), F32)
    scratch = [pltpu.VMEM((16, inducing), F32), pltpu.VMEM((tall, LANES), F32)]
    work = cost(64 * rows * inducing, 2 * rows * inducing)

    sent, before, rhs = pl.pallas_call(
        functools.partial(first_kernel, scale),
        in_specs=[SMEM] + [VMEM] * 4,
        out_specs=[VMEM] * 3,
        out_shape=[message, jax.ShapeDtypeStruct((1, rows), F32), vector],
        scratch_shapes=scratch,
        compiler_params=params(),
        cost_estimate=work,
        name="first_product",
    )(core, halves, near, far, weight)
    sent, node_cov_now = together((sent, by_node[:count]))
    arrived = lax.all_to_all(sent, "blk", 0, 0, tiled=True)
    node_first = features(node_cov_now, (near_freq, far_freq), "node_features_a")
    arrived, node_first = together((arrived, node_first))

    sent, fit, solution, residual, direction = pl.pallas_call(
        functools.partial(second_kernel, scale),
        in_specs=[VMEM] * 6,
        out_specs=[VMEM] * 5,
        out_shape=[message, jax.ShapeDtypeStruct((2, rows), F32), vector, vector, vector],
        scratch_shapes=scratch,
        compiler_params=params(),
        cost_estimate=work,
        name="second_product",
    )(arrived, rhs, before, near, far, weight)
    sent, node_cov_now = together((sent, by_node[count:]))
    arrived = lax.all_to_all(sent, "blk", 0, 0, tiled=True)
    node_second = features(node_cov_now, (near_freq, far_freq), "node_features_b")
    arrived, node_second = together((arrived, node_second))

    sent, both, norm = pl.pallas_call(
        functools.partial(third_kernel, scale, fit_scale),
        in_specs=[VMEM] * 11,
        out_specs=[VMEM] * 3,
        out_shape=[
            jax.ShapeDtypeStruct((blocks, 4, patients), F32),
            jax.ShapeDtypeStruct((2, tall, LANES), F32),
            jax.ShapeDtypeStruct((8, LANES), F32),
        ],
        compiler_params=params(),
        cost_estimate=work,
        name="third_product",
    )(arrived, solution, residual, direction, fit, near, far, weight, size, owner, patient)
    sent, both = together((sent, both))
    arrived = lax.all_to_all(sent, "blk", 0, 0, tiled=True)
    node_values = pl.pallas_call(
        nodes_kernel,
        in_specs=[VMEM] * 3,
        out_specs=VMEM,
        out_shape=jax.ShapeDtypeStruct((2, 2 * count), F32),
        compiler_params=params(),
        cost_estimate=cost(64 * 2 * count * inducing, 4 * count * inducing),
        name="node_values",
    )(both, node_first, node_second)
    arrived, node_values = together((arrived, node_values))

    loglik, weights = pl.pallas_call(
        functools.partial(last_kernel, fit_scale),
        in_specs=[SMEM] + [VMEM] * 6,
        out_specs=[VMEM, VMEM],
        out_shape=[
            jax.ShapeDtypeStruct((1, patients), F32),
            jax.ShapeDtypeStruct((1, own), F32),
        ],
        scratch_shapes=[pltpu.VMEM((tall, LANES), F32)],
        compiler_params=params(),
        name="last",
    )(
        layer,
        arrived,
        both,
        norm,
        node_values,
        event_time.reshape(1, patients),
        event_flag.reshape(1, patients),
    )
    return loglik.reshape(patients), weights.reshape(own)


def solution(mesh):
    in_specs = (
        P("blk", None),
        P("blk"),
        P("blk"),
        P("blk", None),
        P("blk"),
        P(None, "col"),
        P("col"),
        P("blk", None, None),
        P("blk"),
        P("blk"),
    )
    out_specs = (P("blk"), P("col"))
    return jax.shard_map(
        on_device, mesh=mesh, in_specs=in_specs, out_specs=out_specs, check_vma=False
    )
```

time: 533 us -> 121 us (0.23)
  the two profiles are of different devices: /device:TPU:4 before, /device:TPU:8 now
where the time goes in v1:
time: 121 us; the launch traced here: 120 us
  starting transfers between devices  39.2 us (32%)
  Pallas kernels  30.2 us (25%)
  waiting for transfers between devices  25.7 us (21%)
  local copies, waits for them, and re-layouts  22.7 us (19%)
  blocking collectives  1.79 us (1%)
    all_to_all x4, starting transfers between devices, on_device(): arrived = lax.all_to_all(sent, 'blk', 0, 0, tiled=True)  26.9 us
    unnamed x34, local copies, waits for them, and re-layouts  18.5 us
    all_to_all x4, waiting for transfers between devices, on_device(): arrived = lax.all_to_all(sent, 'blk', 0, 0, tiled=True)  14.9 us
    pallas_call x3, Pallas kernels, features(): pl.pallas_call(features_kernel, in_specs=[VMEM] * (1 + len(freqs)), out_s...  14.4 us
    all_to_all x1, waiting for transfers between devices, on_device(): lax.all_to_all(packed, 'col', 0, 0, tiled=True, axis_index_groups=same_core)  10.9 us
    all_to_all x1, starting transfers between devices, on_device(): lax.all_to_all(packed, 'col', 0, 0, tiled=True, axis_index_groups=same_core)  10.3 us
    pallas_call x1, Pallas kernels, on_device(): pl.pallas_call(near_kernel, in_specs=[VMEM] * 4, out_specs=[VMEM] * 2, ou...  5.24 us
    slice x2, local copies, waits for them, and re-layouts, on_device(): sent, node_cov_now = together((sent, by_node[count:]))  2.78 us
  transfers between devices with their start and end apart: 6, of which 5 were waited for; matrix products, arithmetic and copies ran while one was open for 3% of the time, Pallas kernels for 14%

profile of v1, /device:TPU:8, one launch (start us, length us, event | category | flops | bytes accessed | tf_op | source)
XLA Modules:
  0.0 120.4 jit_solution(2383529342937788492)
XLA Ops:
  0.6 0.0 copy-start.11
  0.6 0.7 copy-done.11
  1.4 0.0 copy-start.14
  1.4 0.7 copy-done.14
  2.0 0.7 pack.1
  2.8 10.3 %all-to-all-start = ((bf16[8,136,128]{2,1,0:T(8,128)(2,1)}), bf16[8,136,128]{2,1,0:T(8,128)(2,1)S(1)}, u32[]{:S(2)}, u32[]{:S(2)}) async-start(bf16[8,136,128]{2,1,0:T(8,128)(2,1)} %pack.1), calls=%async_computation | async-start | bytes 557056 | tf_op jit(solution)/shard_map/all_to_all | solution.py:335
  13.1 0.7 reshape.52.weight
  13.8 0.7 reshape.53.size
  14.5 10.9 %all-to-all-done.freq.rest_0_ = bf16[8,136,128]{2,1,0:T(8,128)(2,1)S(1)} async-done(((bf16[8,136,128]{2,1,0:T(8,128)(2,1)}), bf16[8,136,128]{2,1,0:T(8,128)(2,1)S(1)}, u32[]{:S(2)}, u32[]{:S(2)}) %all-to-all-start) | async-done | bytes 278560 | tf_op jit(solution)/shard_map/all_to_all | solution.py:335
  25.3 0.0 copy-start.8
  25.3 0.9 copy-done.8
  26.3 5.2 %near_features.1 = (bf16[1024,1024]{1,0:T(8,128)(2,1)S(1)}, f32[32,8,128]{2,1,0:T(8,128)}) custom-call(bf16[1024,128]{1,0:T(8,128)(2,1)S(1)} %copy-done.8, bf16[8,136,128]{2,1,0:T(8,128)(2,1)S(1)} %all-to-all-done.freq.rest_0_, bf16[1,1024]{1,0:T(2,128)(2,1)S(1)} %reshape.52.weight, bf16[1,1024]{1,0:T(2,128)(2,1)S(1)} %reshape.53.size), custom_call_target="tpu_custom_call" | custom-call | tf_op jit(solution)/shard_map/near_features/pallas_call | solution.py:338
  31.5 0.0 copy-start
  31.5 1.4 %copy-done = bf16[1024,1024]{1,0:T(8,128)(2,1)} copy-done((bf16[1024,1024]{1,0:T(8,128)(2,1)}, bf16[1024,1024]{1,0:T(8,128)(2,1)S(1)}, u32[]{:S(2)}) %copy-start) | copy-done | bytes 2097176
  32.9 1.9 %collective-permute-start = (bf16[8,136,128]{2,1,0:T(8,128)(2,1)S(1)}, bf16[8,136,128]{2,1,0:T(8,128)(2,1)S(1)}, u32[]{:S(2)}, u32[]{:S(2)}) collective-permute-start(bf16[8,136,128]{2,1,0:T(8,128)(2,1)S(1)} %all-to-all-done.freq.rest_0_), channel_id=1, source_target_pairs={{0,1},{1,0},{2,3},{3,2},{4,5},{5,4},{6,7},{7,6},{8,9},{9,8},{10,11... | collective-permute-start | bytes 835592 | tf_op jit(solution)/shard_map/ppermute | solution.py:352
  34.8 10.2 %all-to-all-start.1 = ((f32[32,8,128]{2,1,0:T(8,128)}), f32[32,8,128]{2,1,0:T(8,128)S(1)}, u32[]{:S(2)}, u32[]{:S(2)}) async-start(f32[32,8,128]{2,1,0:T(8,128)} %get-tuple-element.34), calls=%async_computation.1 | async-start | bytes 262144 | tf_op jit(solution)/shard_map/all_to_all | solution.py:351
  45.0 1.8 %fusion = (bf16[8,128,128]{2,0,1:T(8,128)(2,1)}, bf16[8,128,128]{2,0,1:T(8,128)(2,1)S(1)}) fusion(bf16[16,128,128]{2,0,1:T(8,128)(2,1)} %bitcast.21), kind=kLoop, calls=%fused_computation.1 | loop fusion | bytes 1048576 | tf_op jit(solution)/shard_map/slice | solution.py:390
  46.8 0.0 collective-permute-done.rest_0_.rest_1_
  46.9 0.0 copy-start.9
  46.9 0.9 copy-done.9
  47.8 3.3 %far_features.1.far = bf16[1024,1024]{1,0:T(8,128)(2,1)S(1)} custom-call(bf16[1024,128]{1,0:T(8,128)(2,1)S(1)} %copy-done.9, bf16[8,136,128]{2,1,0:T(8,128)(2,1)S(1)} %collective-permute-done.rest_0_.rest_1_), custom_call_target="tpu_custom_call" | custom-call | flops 289406976 | bytes 2097152 | tf_op jit(solution)/shard_map/far_features/pallas_call | solution.py:134
  51.2 4.1 %all-to-all-done.1 = f32[32,8,128]{2,1,0:T(8,128)S(1)} async-done(((f32[32,8,128]{2,1,0:T(8,128)}), f32[32,8,128]{2,1,0:T(8,128)S(1)}, u32[]{:S(2)}, u32[]{:S(2)}) %all-to-all-start.1) | async-done | bytes 131104 | tf_op jit(solution)/shard_map/all_to_all | solution.py:351
  55.3 1.8 %all-gather = f32[16,128]{1,0:T(8,128)S(1)} all-gather(f32[8,128]{1,0:T(8,128)S(1)} %broadcast_multiply_fusion), channel_id=2, replica_groups={{0,1},{2,3},{4,5},{6,7},{8,9},{10,11},{12,13},{14,15},{16,17},{18,19},{..., dimensions={0}, use_global_device_ids=true | all-gather | bytes 12288 | tf_op jit(solution)/shard_map/all_gather | solution.py:356
  57.1 0.0 copy-start.1
  57.1 1.6 %copy-done.1 = bf16[1024,1024]{1,0:T(8,128)(2,1)S(1)} copy-done((bf16[1024,1024]{1,0:T(8,128)(2,1)S(1)}, bf16[1024,1024]{1,0:T(8,128)(2,1)}, u32[]{:S(2)}) %copy-start.1) | copy-done | bytes 2097176
  58.7 2.5 %first_product.1 = (f32[32,16,128]{2,1,0:T(8,128)}, f32[1,1024]{1,0:T(1,128)S(1)}, f32[16,128]{1,0:T(8,128)S(1)}) custom-call(s32[1]{0:T(128)} %bitcast.1.core, f32[2,8,128]{2,1,0:T(8,128)S(1)} %bitcast.15, bf16[1024,1024]{1,0:T(8,128)(2,1)S(1)} %copy-done.1, bf16[1024,1024]{1,0:T(8,128)(2,1)S(1)} %far_features.1.far, bf16[1,1024]{1,0:T(2,128)(2,1)S(1)} %reshape.52.weight), custom_call_target="tpu_custom_call" | custom-call | flops 134217728 | bytes 4194304 | tf_op jit(solution)/shard_map/first_product/pallas_call | solution.py:365
  61.2 5.7 %all-to-all-start.2 = ((f32[32,16,128]{2,1,0:T(8,128)}), f32[32,16,128]{2,1,0:T(8,128)S(1)}, u32[]{:S(2)}, u32[]{:S(2)}) async-start(f32[32,16,128]{2,1,0:T(8,128)} %get-tuple-element.40), calls=%async_computation.2 | async-start | bytes 524288 | tf_op jit(solution)/shard_map/all_to_all | solution.py:376
  66.9 1.0 copy.13
  67.9 5.5 %node_features_a.1.first = bf16[1024,2048]{1,0:T(8,128)(2,1)S(1)} custom-call(bf16[1024,128]{1,0:T(8,128)(2,1)S(1)} %bitcast.13, bf16[8,136,128]{2,1,0:T(8,128)(2,1)S(1)} %all-to-all-done.freq.rest_0_, bf16[8,136,128]{2,1,0:T(8,128)(2,1)S(1)} %collective-permute-done.rest_0_.rest_1_), custom_call_target="tpu_custom_call" | custom-call | flops 578813952 | bytes 4194304 | tf_op jit(solution)/shard_map/node_features_a/pallas_call | solution.py:134
  73.4 0.0 copy-start.4
  73.4 2.0 %copy-done.4 = bf16[1024,2048]{1,0:T(8,128)(2,1)} copy-done((bf16[1024,2048]{1,0:T(8,128)(2,1)}, bf16[1024,2048]{1,0:T(8,128)(2,1)S(1)}, u32[]{:S(2)}) %copy-start.4) | copy-done | bytes 4194328
  75.3 4.1 %all-to-all-done.2.arrived = f32[32,16,128]{2,1,0:T(8,128)S(1)} async-done(((f32[32,16,128]{2,1,0:T(8,128)}), f32[32,16,128]{2,1,0:T(8,128)S(1)}, u32[]{:S(2)}, u32[]{:S(2)}) %all-to-all-start.2) | async-done | bytes 262176 | tf_op jit(solution)/shard_map/all_to_all | solution.py:376
  79.4 0.0 copy-start.2
  79.4 1.6 %copy-done.2 = bf16[1024,1024]{1,0:T(8,128)(2,1)S(1)} copy-done((bf16[1024,1024]{1,0:T(8,128)(2,1)S(1)}, bf16[1024,1024]{1,0:T(8,128)(2,1)}, u32[]{:S(2)}) %copy-start.2) | copy-done | bytes 2097176
  81.0 0.0 copy-start.12
  81.0 0.0 copy-start.13
  81.0 2.0 %second_product.1 = (f32[32,16,128]{2,1,0:T(8,128)S(1)}, f32[2,1024]{1,0:T(2,128)S(1)}, f32[16,128]{1,0:T(8,128)S(1)}, f32[16,128]{1,0:T(8,128)S(1)}, f32[16,128]{1,0:T(8,128)S(1)}) custom-call(f32[32,16,128]{2,1,0:T(8,128)S(1)} %all-to-all-done.2.arrived, f32[16,128]{1,0:T(8,128)S(1)} %get-tuple-element.43.rhs, f32[1,1024]{1,0:T(1,128)S(1)} %get-tuple-element.44.before, ...), custom_call_target="tpu_custom_call" | custom-call | flops 134217728 | bytes 4194304 | tf_op jit(solution)/shard_map/second_product/pallas_call | solution.py:380
  83.0 0.0 copy-start.10
  83.0 0.7 copy-done.10
  83.7 5.7 %all-to-all-start.3 = ((f32[32,16,128]{2,1,0:T(8,128)}), f32[32,16,128]{2,1,0:T(8,128)S(1)}, u32[]{:S(2)}, u32[]{:S(2)}) async-start(f32[32,16,128]{2,1,0:T(8,128)} %copy-done.10), calls=%async_computation.3 | async-start | bytes 524288 | tf_op jit(solution)/shard_map/all_to_all | solution.py:391
  89.4 5.5 %node_features_b.1.second = bf16[1024,2048]{1,0:T(8,128)(2,1)S(1)} custom-call(bf16[1024,128]{1,0:T(8,128)(2,1)S(1)} %bitcast.14, bf16[8,136,128]{2,1,0:T(8,128)(2,1)S(1)} %all-to-all-done.freq.rest_0_, bf16[8,136,128]{2,1,0:T(8,128)(2,1)S(1)} %collective-permute-done.rest_0_.rest_1_), custom_call_target="tpu_custom_call" | custom-call | flops 578813952 | bytes 4194304 | tf_op jit(solution)/shard_map/node_features_b/pallas_call | solution.py:134
  95.0 0.0 copy-start.6
  95.0 2.0 %copy-done.6 = bf16[1024,2048]{1,0:T(8,128)(2,1)} copy-done((bf16[1024,2048]{1,0:T(8,128)(2,1)}, bf16[1024,2048]{1,0:T(8,128)(2,1)S(1)}, u32[]{:S(2)}) %copy-start.6) | copy-done | bytes 4194328
  97.0 4.4 %all-to-all-done.3.arrived = f32[32,16,128]{2,1,0:T(8,128)S(1)} async-done(((f32[32,16,128]{2,1,0:T(8,128)}), f32[32,16,128]{2,1,0:T(8,128)S(1)}, u32[]{:S(2)}, u32[]{:S(2)}) %all-to-all-start.3) | async-done | bytes 262176 | tf_op jit(solution)/shard_map/all_to_all | solution.py:391
  101.3 0.0 copy-done.12
  101.3 0.0 copy-done.13
  101.3 0.0 copy-start.3
  101.3 1.6 %copy-done.3 = bf16[1024,1024]{1,0:T(8,128)(2,1)S(1)} copy-done((bf16[1024,1024]{1,0:T(8,128)(2,1)S(1)}, bf16[1024,1024]{1,0:T(8,128)(2,1)}, u32[]{:S(2)}) %copy-start.3) | copy-done | bytes 2097176
  102.9 2.4 %third_product.1 = (f32[32,4,128]{2,1,0:T(4,128)}, f32[2,16,128]{2,1,0:T(8,128)S(1)}, f32[8,128]{1,0:T(8,128)S(1)}) custom-call(f32[32,16,128]{2,1,0:T(8,128)S(1)} %all-to-all-done.3.arrived, f32[16,128]{1,0:T(8,128)S(1)} %get-tuple-element.49.solution, f32[16,128]{1,0:T(8,128)S(1)} %get-tuple-element.50.residual, ...), custom_call_target="tpu_custom_call" | custom-call | flops 134217728 | bytes 4194304 | tf_op jit(solution)/shard_map/third_product/pallas_call | solution.py:395
  105.3 5.4 %all-to-all-start.4 = ((f32[32,4,128]{2,1,0:T(4,128)}), f32[32,4,128]{2,1,0:T(4,128)S(1)}, u32[]{:S(2)}, u32[]{:S(2)}) async-start(f32[32,4,128]{2,1,0:T(4,128)} %get-tuple-element.55), calls=%async_computation.4 | async-start | bytes 131072 | tf_op jit(solution)/shard_map/all_to_all | solution.py:409
  110.7 0.0 copy-start.5
  110.7 2.2 %copy-done.5 = bf16[1024,2048]{1,0:T(8,128)(2,1)S(1)} copy-done((bf16[1024,2048]{1,0:T(8,128)(2,1)S(1)}, bf16[1024,2048]{1,0:T(8,128)(2,1)}, u32[]{:S(2)}) %copy-start.5) | copy-done | bytes 4194328
  112.9 0.0 copy-start.7
  112.9 2.2 %copy-done.7 = bf16[1024,2048]{1,0:T(8,128)(2,1)S(1)} copy-done((bf16[1024,2048]{1,0:T(8,128)(2,1)S(1)}, bf16[1024,2048]{1,0:T(8,128)(2,1)}, u32[]{:S(2)}) %copy-start.7) | copy-done | bytes 4194328
  115.1 0.0 copy-start.15
  115.1 0.0 copy-start.16
  115.1 2.3 %node_values.1 = f32[2,2048]{1,0:T(2,128)S(1)} custom-call(f32[2,16,128]{2,1,0:T(8,128)S(1)} %get-tuple-element.56.both, bf16[1024,2048]{1,0:T(8,128)(2,1)S(1)} %copy-done.5, bf16[1024,2048]{1,0:T(8,128)(2,1)S(1)} %copy-done.7), custom_call_target="tpu_custom_call" | custom-call | flops 268435456 | bytes 8388608 | tf_op jit(solution)/shard_map/node_values/pallas_call | solution.py:410
  117.4 2.3 %all-to-all-done.4.arrived = f32[32,4,128]{2,1,0:T(4,128)S(1)} async-done(((f32[32,4,128]{2,1,0:T(4,128)}), f32[32,4,128]{2,1,0:T(4,128)S(1)}, u32[]{:S(2)}, u32[]{:S(2)}) %all-to-all-start.4) | async-done | bytes 65568 | tf_op jit(solution)/shard_map/all_to_all | solution.py:409
  119.7 0.0 copy-done.15
  119.7 0.0 copy-done.16
  119.7 0.7 last.1
  (3 shorter events, 0.1 us)
Async XLA Ops:
  0.6 0.8 copy-start.11
  1.4 0.7 copy-start.14
  2.8 22.5 %all-to-all-start = ((bf16[8,136,128]{2,1,0:T(8,128)(2,1)}), bf16[8,136,128]{2,1,0:T(8,128)(2,1)S(1)}, u32[]{:S(2)}, u32[]{:S(2)}) async-start(bf16[8,136,128]{2,1,0:T(8,128)(2,1)} %pack.1), calls=%async_computation | async-start | bytes 557056 | tf_op jit(solution)/shard_map/all_to_all | solution.py:335
  25.3 1.0 copy-start.8
  31.5 1.4 %copy-start = (bf16[1024,1024]{1,0:T(8,128)(2,1)}, bf16[1024,1024]{1,0:T(8,128)(2,1)S(1)}, u32[]{:S(2)}) copy-start(bf16[1024,1024]{1,0:T(8,128)(2,1)S(1)} %get-tuple-element.37.near) | copy-start | bytes 6291460
  32.9 14.0 %collective-permute-start = (bf16[8,136,128]{2,1,0:T(8,128)(2,1)S(1)}, bf16[8,136,128]{2,1,0:T(8,128)(2,1)S(1)}, u32[]{:S(2)}, u32[]{:S(2)}) collective-permute-start(bf16[8,136,128]{2,1,0:T(8,128)(2,1)S(1)} %all-to-all-done.freq.rest_0_), channel_id=1, source_target_pairs={{0,1},{1,0},{2,3},{3,2},{4,5},{5,4},{6,7},{7,6},{8,9},{9,8},{10,11... | collective-permute-start | bytes 835592 | tf_op jit(solution)/shard_map/ppermute | solution.py:352
  34.8 20.5 %all-to-all-start.1 = ((f32[32,8,128]{2,1,0:T(8,128)}), f32[32,8,128]{2,1,0:T(8,128)S(1)}, u32[]{:S(2)}, u32[]{:S(2)}) async-start(f32[32,8,128]{2,1,0:T(8,128)} %get-tuple-element.34), calls=%async_computation.1 | async-start | bytes 262144 | tf_op jit(solution)/shard_map/all_to_all | solution.py:351
  46.9 1.0 copy-start.9
  57.1 1.6 %copy-start.1 = (bf16[1024,1024]{1,0:T(8,128)(2,1)S(1)}, bf16[1024,1024]{1,0:T(8,128)(2,1)}, u32[]{:S(2)}) copy-start(bf16[1024,1024]{1,0:T(8,128)(2,1)} %copy-done) | copy-start | bytes 6291460
  61.2 18.2 %all-to-all-start.2 = ((f32[32,16,128]{2,1,0:T(8,128)}), f32[32,16,128]{2,1,0:T(8,128)S(1)}, u32[]{:S(2)}, u32[]{:S(2)}) async-start(f32[32,16,128]{2,1,0:T(8,128)} %get-tuple-element.40), calls=%async_computation.2 | async-start | bytes 524288 | tf_op jit(solution)/shard_map/all_to_all | solution.py:376
  73.4 2.0 %copy-start.4 = (bf16[1024,2048]{1,0:T(8,128)(2,1)}, bf16[1024,2048]{1,0:T(8,128)(2,1)S(1)}, u32[]{:S(2)}) copy-start(bf16[1024,2048]{1,0:T(8,128)(2,1)S(1)} %node_features_a.1.first) | copy-start | bytes 12582916
  79.4 1.6 %copy-start.2 = (bf16[1024,1024]{1,0:T(8,128)(2,1)S(1)}, bf16[1024,1024]{1,0:T(8,128)(2,1)}, u32[]{:S(2)}) copy-start(bf16[1024,1024]{1,0:T(8,128)(2,1)} %copy-done) | copy-start | bytes 6291460
  81.0 20.3 %copy-start.12 = (s32[1024,1]{0,1:T(1,128)S(1)}, s32[1024,1]{0,1:T(1,128)}, u32[]{:S(2)}) copy-start(s32[1024,1]{0,1:T(1,128)} %param.13) | copy-start | bytes 12292
  81.0 20.3 %copy-start.13 = (s32[1024]{0:T(1024)S(1)}, s32[1024]{0:T(1024)}, u32[]{:S(2)}) copy-start(s32[1024]{0:T(1024)} %param.14) | copy-start | bytes 12292
  83.0 0.7 copy-start.10
  83.7 17.6 %all-to-all-start.3 = ((f32[32,16,128]{2,1,0:T(8,128)}), f32[32,16,128]{2,1,0:T(8,128)S(1)}, u32[]{:S(2)}, u32[]{:S(2)}) async-start(f32[32,16,128]{2,1,0:T(8,128)} %copy-done.10), calls=%async_computation.3 | async-start | bytes 524288 | tf_op jit(solution)/shard_map/all_to_all | solution.py:391
  95.0 2.0 %copy-start.6 = (bf16[1024,2048]{1,0:T(8,128)(2,1)}, bf16[1024,2048]{1,0:T(8,128)(2,1)S(1)}, u32[]{:S(2)}) copy-start(bf16[1024,2048]{1,0:T(8,128)(2,1)S(1)} %node_features_b.1.second) | copy-start | bytes 12582916
  101.3 1.6 %copy-start.3 = (bf16[1024,1024]{1,0:T(8,128)(2,1)S(1)}, bf16[1024,1024]{1,0:T(8,128)(2,1)}, u32[]{:S(2)}) copy-start(bf16[1024,1024]{1,0:T(8,128)(2,1)} %copy-done) | copy-start | bytes 6291460
  105.3 14.4 %all-to-all-start.4 = ((f32[32,4,128]{2,1,0:T(4,128)}), f32[32,4,128]{2,1,0:T(4,128)S(1)}, u32[]{:S(2)}, u32[]{:S(2)}) async-start(f32[32,4,128]{2,1,0:T(4,128)} %get-tuple-element.55), calls=%async_computation.4 | async-start | bytes 131072 | tf_op jit(solution)/shard_map/all_to_all | solution.py:409
  110.7 2.2 %copy-start.5 = (bf16[1024,2048]{1,0:T(8,128)(2,1)S(1)}, bf16[1024,2048]{1,0:T(8,128)(2,1)}, u32[]{:S(2)}) copy-start(bf16[1024,2048]{1,0:T(8,128)(2,1)} %copy-done.4) | copy-start | bytes 12582916
  112.9 2.2 %copy-start.7 = (bf16[1024,2048]{1,0:T(8,128)(2,1)S(1)}, bf16[1024,2048]{1,0:T(8,128)(2,1)}, u32[]{:S(2)}) copy-start(bf16[1024,2048]{1,0:T(8,128)(2,1)} %copy-done.6) | copy-start | bytes 12582916
  115.1 4.6 %copy-start.15 = (f32[128]{0:T(128)S(1)}, f32[128]{0:T(128)}, u32[]{:S(2)}) copy-start(f32[128]{0:T(128)} %param.18) | copy-start | bytes 1540
  115.1 4.6 %copy-start.16 = (s32[128]{0:T(128)S(1)}, s32[128]{0:T(128)}, u32[]{:S(2)}) copy-start(s32[128]{0:T(128)} %param.19) | copy-start | bytes 1540

commit v2 on v1

--- a/solution.py
+++ b/solution.py
@@ -14,7 +14,7 @@
 LOG_SHAPE = math.log(1.5)
 LINK = 0.4
 LANES = 128
-LIMIT = 20 * 1024 * 1024
+MIB = 1024 * 1024
 
 
 def cosine_table():
@@ -68,7 +68,9 @@
 
 VMEM = pl.BlockSpec(memory_space=pltpu.VMEM)
 SMEM = pl.BlockSpec(memory_space=pltpu.SMEM)
-BLOCK = 256
+HBM = pl.BlockSpec(memory_space=pltpu.HBM)
+PARTS = 4
+SPARE = 9
 PHASE_ROWS = 8
 
 
@@ -80,21 +82,51 @@
     return jnp.sum(jnp.sum(x, axis=0, keepdims=True), axis=1, keepdims=True)
 
 
-def params():
-    return pltpu.CompilerParams(vmem_limit_bytes=LIMIT)
+def params(mebibytes=48):
+    return pltpu.CompilerParams(vmem_limit_bytes=mebibytes * MIB)
 
 
 def cost(flops, size, hard=0):
     return pl.CostEstimate(flops=flops, bytes_accessed=size, transcendentals=hard)
 
 
-def pack_kernel(freq, phase, out):
+def pack_kernel(freq, phase, out, packed, row, sems):
     depth = freq.shape[0]
-    values = freq[...]
-    last = jnp.broadcast_to(phase[...], (PHASE_ROWS, phase.shape[1]))
-    for copy in range(out.shape[0]):
-        out[copy, 0:depth, :] = values
-        out[copy, depth : depth + PHASE_ROWS, :] = last
+    loads = [
+        pltpu.make_async_copy(freq, packed.at[0:depth], sems.at[0]),
+        pltpu.make_async_copy(phase, row, sems.at[1]),
+    ]
+    for load in loads:
+        load.start()
+    for load in loads:
+        load.wait()
+    packed[depth : depth + PHASE_ROWS, :] = jnp.broadcast_to(
+        row[...], (PHASE_ROWS, row.shape[1])
+    )
+    stores = [
+        pltpu.make_async_copy(packed, out.at[copy], sems.at[2 + copy])
+        for copy in range(out.shape[0])
+    ]
+    for store in stores:
+        store.start()
+    for store in stores:
+        store.wait()
+
+
+def stage_kernel(value, out):
+    out[...] = value[...]
+
+
+def stage(value, name):
+    return pl.pallas_call(
+        stage_kernel,
+        in_specs=[VMEM],
+        out_specs=VMEM,
+        out_shape=jax.ShapeDtypeStruct(value.shape, value.dtype),
+        compiler_params=params(),
+        cost_estimate=cost(value.size, 4 * value.size),
+        name=name,
+    )(value)
 
 
 def feature_block(rows, freq, store):
@@ -107,56 +139,62 @@
         store(j * LANES, feature(dot_nn(rows, both) + phase.astype(F32)))
 
 
-FEATURE_ROWS = 128
-
-
-def features_kernel(cov, *rest):
-    freqs, out = rest[:-1], rest[-1]
+FEATURE_ROWS = 256
+
+
+def features_kernel(order, core, cov, freq, out):
+    half = freq.shape[1] * LANES
 
     def step(i, carry):
         at = rows_at(i, FEATURE_ROWS)
-        base = 0
-        for freq in freqs:
-
-            def store(column, value, base=base):
+        for index, other in enumerate(order):
+            source = 1 - core[0] if other else core[0]
+
+            def store(column, value, base=index * half):
                 out[at, base + column : base + column + value.shape[1]] = value
 
-            feature_block(cov[at, :], freq, store)
-            base += freq.shape[0] * LANES
+            feature_block(cov[at, :], freq.at[source], store)
         return carry
 
     lax.fori_loop(0, cov.shape[0] // FEATURE_ROWS, step, 0)
 
 
-def features(cov, freqs, name):
+def features(core, cov, freq, order, name):
     rows, depth = cov.shape
-    columns = sum(f.shape[0] * f.shape[2] for f in freqs)
+    columns = len(order) * freq.shape[1] * LANES
     return pl.pallas_call(
-        features_kernel,
-        in_specs=[VMEM] * (1 + len(freqs)),
+        functools.partial(features_kernel, order),
+        in_specs=[SMEM, VMEM, VMEM],
         out_specs=VMEM,
         out_shape=jax.ShapeDtypeStruct((rows, columns), BF16),
         compiler_params=params(),
         cost_estimate=cost(2 * rows * depth * columns + 20 * rows * columns, 2 * rows * columns),
         name=name,
-    )(cov, *freqs)
-
-
-def near_kernel(cov, freq, weight, size, phi, out, gathered, tiles):
+    )(core, cov, freq)
+
+
+def near_kernel(cov, freq, weight, size, phi_out, out, phi, gathered, tiles, sems):
+    def part(i):
+        at = rows_at(i, FEATURE_ROWS)
+        return pltpu.make_async_copy(phi.at[at], phi_out.at[at], sems.at[i])
+
+    def step(i, carry):
+        at = rows_at(i, FEATURE_ROWS)
+
+        def store(column, value):
+            phi[at, column : column + value.shape[1]] = value
+
+        feature_block(cov[at, :], freq, store)
+        part(i).start()
+        return carry
+
+    steps = cov.shape[0] // FEATURE_ROWS
+    lax.fori_loop(0, steps, step, 0)
     product = weight[...].astype(F32) * size[...].astype(F32)
-    split = stack_rows(split3(product), 16)
-    gathered[...] = jnp.zeros_like(gathered)
-    for i in range(cov.shape[0] // BLOCK):
-        at = slice(i * BLOCK, (i + 1) * BLOCK)
-        left = split[:, at]
-
-        def store(column, value, at=at, left=left):
-            where = slice(column, column + value.shape[1])
-            phi[at, where] = value
-            gathered[:, where] += dot_nn(left, value)
-
-        feature_block(cov[at, :], freq, store)
+    gathered[...] = dot_nn(stack_rows(split3(product), 16), phi[...])
     send_whole(gathered, tiles, out)
+    for i in range(steps):
+        part(i).wait()
 
 
 def rows_of(vector):
@@ -172,40 +210,59 @@
         out[copy] = whole
 
 
-def forward(direction, phis):
+def fetch(near, held, sems):
+    part = held.shape[0] // PARTS
+    copies = []
+    for k in range(PARTS):
+        at = slice(k * part, (k + 1) * part)
+        copy = pltpu.make_async_copy(near.at[at], held.at[at], sems.at[k])
+        copy.start()
+        copies.append((at, copy))
+    return copies
+
+
+def forward(direction, held, copies, far):
     split = rows_of(direction)
-    total, base = 0.0, 0
-    for phi in phis:
-        total = total + dot_nt(split[:, base : base + phi.shape[1]], phi[...])
-        base += phi.shape[1]
-    return jnp.sum(total, axis=0, keepdims=True)
-
-
-def product(direction, phis, weight, gathered, tiles, out, scale):
-    values = forward(direction, phis)
+    half = far.shape[1]
+    total = jnp.sum(dot_nt(split[:, half:], far[...]), axis=0, keepdims=True)
+    values = []
+    for at, copy in copies:
+        copy.wait()
+        part = jnp.sum(dot_nt(split[:, :half], held[at]), axis=0, keepdims=True)
+        values.append(part + total[:, at])
+    return jnp.concatenate(values, axis=1)
+
+
+def product(direction, held, copies, far, weight, gathered, tiles, out, scale):
+    values = forward(direction, held, copies, far)
     split = stack_rows(split3(weight[...].astype(F32) * values * scale), 16)
-    base = 0
-    for phi in phis:
-        gathered[:, base : base + phi.shape[1]] = dot_nn(split, phi[...])
-        base += phi.shape[1]
+    half = far.shape[1]
+    gathered[:, :half] = dot_nn(split, held[...])
+    gathered[:, half:] = dot_nn(split, far[...])
     send_whole(gathered, tiles, out)
     return values
 
 
-def first_kernel(scale, core, halves, near, far, weight, out, values_out, rhs_out, gathered, tiles):
+def first_kernel(
+    scale, core, halves, near, far, weight, out, values_out, rhs_out, gathered, tiles, held, sems
+):
+    copies = fetch(near, held, sems)
     low, high = halves[0], halves[1]
     swap = core[0] == 1
     half = low.shape[0]
     rhs_out[0:half, :] = jnp.where(swap, high, low)
     rhs_out[half : 2 * half, :] = jnp.where(swap, low, high)
-    values_out[...] = product(rhs_out[...], (near, far), weight, gathered, tiles, out, scale)
+    values_out[...] = product(
+        rhs_out[...], held, copies, far, weight, gathered, tiles, out, scale
+    )
 
 
 def second_kernel(
     scale, arrived, rhs, before, near, far, weight,
     out, fit_out, solution_out, residual_out, direction_out,
-    gathered, tiles,
+    gathered, tiles, held, sems,
 ):
+    copies = fetch(near, held, sems)
     direction = rhs[...]
     norm = total_of(direction * direction)
     image = direction + jnp.sum(arrived[...], axis=0)
@@ -216,13 +273,17 @@
     residual_out[...] = residual
     direction_out[...] = later
     fit_out[0:1, :] = length * before[...]
-    fit_out[1:2, :] = product(later, (near, far), weight, gathered, tiles, out, scale)
+    fit_out[1:2, :] = product(
+        later, held, copies, far, weight, gathered, tiles, out, scale
+    )
 
 
 def third_kernel(
     scale, fit_scale, arrived, solution, residual, direction, fit, near, far, weight, size, owner, patient,
     out, both_out, norm_out,
+    held, sems,
 ):
+    copies = fetch(near, held, sems)
     before = direction[...]
     left = residual[...]
     norm = total_of(left * left)
@@ -234,7 +295,7 @@
     both_out[0] = solution[...] + length * before
     both_out[1] = later
     norm_out[...] = jnp.broadcast_to(norm_next, norm_out.shape)
-    values = forward(later, (near, far))
+    values = forward(later, held, copies, far)
     fitted = fit[0:1, :] + length * fit[1:2, :]
     weights = weight[...].astype(F32)
     weighted = weights * values
@@ -322,49 +383,63 @@
     together = lax.optimization_barrier
     same_core = [[2 * z + c for z in range(layers)] for c in range(2)]
     pairs = [[2 * z, 2 * z + 1] for z in range(layers)]
-    swap = [(i, i ^ 1) for i in range(cols)]
 
     packed = pl.pallas_call(
         pack_kernel,
-        in_specs=[VMEM, VMEM],
-        out_specs=VMEM,
+        in_specs=[HBM, HBM],
+        out_specs=HBM,
         out_shape=jax.ShapeDtypeStruct((layers, depth + PHASE_ROWS, own), BF16),
-        compiler_params=params(),
+        scratch_shapes=[
+            pltpu.VMEM((depth + PHASE_ROWS, own), BF16),
+            pltpu.VMEM((1, own), BF16),
+            pltpu.SemaphoreType.DMA((2 + layers,)),
+        ],
+        compiler_params=params(60),
         name="pack",
     )(inducing_freq, inducing_phase.reshape(1, own))
+    packed, cov = together((packed, visit_cov))
     near_freq = lax.all_to_all(packed, "col", 0, 0, tiled=True, axis_index_groups=same_core)
+    cov = stage(cov, "stage_cov")
+    near_freq, cov = together((near_freq, cov))
 
     half = inducing // 2
     near, sent = pl.pallas_call(
         near_kernel,
         in_specs=[VMEM] * 4,
-        out_specs=[VMEM] * 2,
+        out_specs=[HBM, VMEM],
         out_shape=[
-            jax.ShapeDtypeStruct((rows, half), BF16),
+            jax.ShapeDtypeStruct((SPARE * rows, half), BF16),
             jax.ShapeDtypeStruct((blocks, tall // 2, LANES), F32),
         ],
-        scratch_shapes=[pltpu.VMEM((16, half), F32), pltpu.VMEM((tall // 2, LANES), F32)],
+        scratch_shapes=[
+            pltpu.VMEM((rows, half), BF16),
+            pltpu.VMEM((16, half), F32),
+            pltpu.VMEM((tall // 2, LANES), F32),
+            pltpu.SemaphoreType.DMA((rows // FEATURE_ROWS,)),
+        ],
         compiler_params=params(),
         name="near_features",
-    )(visit_cov, near_freq, weight, size)
+    )(cov, near_freq, weight, size)
     sent, late_freq = together((sent, near_freq))
     arrived = lax.all_to_all(sent, "blk", 0, 0, tiled=True)
-    far_freq = lax.ppermute(late_freq, "col", swap)
-    far = features(visit_cov, (far_freq,), "far_features")
-    arrived, far = together((arrived, far))
+    freq = lax.all_gather(late_freq, "col", axis_index_groups=pairs)
+    far = features(core, cov, freq, (1,), "far_features")
+    by_node = node_cov.transpose(1, 0, 2).reshape(nodes * patients, depth)
+    count = nodes * patients // 2
+    node_covs = (by_node[:count], by_node[count:])
+    arrived, far, node_covs = together((arrived, far, node_covs))
     rhs = jnp.sum(arrived, axis=0) * (1.0 / math.sqrt(rows * blocks))
     halves = lax.all_gather(rhs, "col", axis_index_groups=pairs)
 
-    by_node = node_cov.transpose(1, 0, 2).reshape(nodes * patients, depth)
-    count = nodes * patients // 2
     message = jax.ShapeDtypeStruct((blocks, tall, LANES), F32)
     vector = jax.ShapeDtypeStruct((tall, LANES), F32)
-    scratch = [pltpu.VMEM((16, inducing), F32), pltpu.VMEM((tall, LANES), F32)]
+    fetched = [pltpu.VMEM((rows, half), BF16), pltpu.SemaphoreType.DMA((PARTS,))]
+    scratch = [pltpu.VMEM((16, inducing), F32), pltpu.VMEM((tall, LANES), F32)] + fetched
     work = cost(64 * rows * inducing, 2 * rows * inducing)
 
     sent, before, rhs = pl.pallas_call(
         functools.partial(first_kernel, scale),
-        in_specs=[SMEM] + [VMEM] * 4,
+        in_specs=[SMEM, VMEM, HBM, VMEM, VMEM],
         out_specs=[VMEM] * 3,
         out_shape=[message, jax.ShapeDtypeStruct((1, rows), F32), vector],
         scratch_shapes=scratch,
@@ -372,14 +447,14 @@
         cost_estimate=work,
         name="first_product",
     )(core, halves, near, far, weight)
-    sent, node_cov_now = together((sent, by_node[:count]))
+    sent, node_cov_now = together((sent, node_covs[0]))
     arrived = lax.all_to_all(sent, "blk", 0, 0, tiled=True)
-    node_first = features(node_cov_now, (near_freq, far_freq), "node_features_a")
+    node_first = features(core, node_cov_now, freq, (0, 1), "node_features_a")
     arrived, node_first = together((arrived, node_first))
 
     sent, fit, solution, residual, direction = pl.pallas_call(
         functools.partial(second_kernel, scale),
-        in_specs=[VMEM] * 6,
+        in_specs=[VMEM, VMEM, VMEM, HBM, VMEM, VMEM],
         out_specs=[VMEM] * 5,
         out_shape=[message, jax.ShapeDtypeStruct((2, rows), F32), vector, vector, vector],
         scratch_shapes=scratch,
@@ -387,20 +462,21 @@
         cost_estimate=work,
         name="second_product",
     )(arrived, rhs, before, near, far, weight)
-    sent, node_cov_now = together((sent, by_node[count:]))
+    sent, node_cov_now = together((sent, node_covs[1]))
     arrived = lax.all_to_all(sent, "blk", 0, 0, tiled=True)
-    node_second = features(node_cov_now, (near_freq, far_freq), "node_features_b")
+    node_second = features(core, node_cov_now, freq, (0, 1), "node_features_b")
     arrived, node_second = together((arrived, node_second))
 
     sent, both, norm = pl.pallas_call(
         functools.partial(third_kernel, scale, fit_scale),
-        in_specs=[VMEM] * 11,
+        in_specs=[VMEM] * 5 + [HBM] + [VMEM] * 5,
         out_specs=[VMEM] * 3,
         out_shape=[
             jax.ShapeDtypeStruct((blocks, 4, patients), F32),
             jax.ShapeDtypeStruct((2, tall, LANES), F32),
             jax.ShapeDtypeStruct((8, LANES), F32),
         ],
+        scratch_shapes=fetched,
         compiler_params=params(),
         cost_estimate=work,
         name="third_product",

time: 121 us -> 114 us (0.942)
  local copies, waits for them, and re-layouts: 22.7 us -> 10.4 us
  Pallas kernels: 30.2 us -> 34.4 us
  starting transfers between devices: 39.2 us -> 36.8 us
  blocking collectives: 1.79 us -> 4 us
    unnamed x34 -> x18, local copies, waits for them, and re-layouts: 18.5 us -> 7.93 us
    pallas_call x1, Pallas kernels: 2.27 us -> 4.48 us  [on_device(): pl.pallas_call(nodes_kernel, in_specs=[VMEM] * 3, out_specs=VMEM, out_sha...]
    all_gather x0 -> x1, blocking collectives: none -> 2.2 us  [on_device(): freq = lax.all_gather(late_freq, 'col', axis_index_groups=pairs)]
    ppermute x1 -> x0, starting transfers between devices: 1.91 us -> none  [on_device(): far_freq = lax.ppermute(late_freq, 'col', swap)]
    slice x3, local copies, waits for them, and re-layouts: 2.81 us -> 1.14 us  [on_device(): node_covs = (by_node[:count], by_node[count:])]
    pallas_call x7 -> x8, Pallas kernels: 24.8 us -> 25.7 us  [the longest x3 12.6 us: features(): pl.pallas_call(functools.partial(features_kernel, order), in_specs=[SMEM,...]
  transfers between devices with their start and end apart: 6 -> 5, of which waited for: 5 -> 5; matrix products, arithmetic and copies ran while one was open for 3% -> 2% of each run, Pallas kernels for 14% -> 15%
where the time goes in v2:
time: 114 us; the launch traced here: 113 us
  starting transfers between devices  36.8 us (32%)
  Pallas kernels  34.4 us (30%)
  waiting for transfers between devices  25.8 us (23%)
  local copies, waits for them, and re-layouts  10.4 us (9%)
  blocking collectives  4 us (4%)
    all_to_all x4, starting transfers between devices, on_device(): arrived = lax.all_to_all(sent, 'blk', 0, 0, tiled=True)  26.5 us
    all_to_all x4, waiting for transfers between devices, on_device(): arrived = lax.all_to_all(sent, 'blk', 0, 0, tiled=True)  15.9 us
    pallas_call x3, Pallas kernels, features(): pl.pallas_call(functools.partial(features_kernel, order), in_specs=[SMEM,...  12.6 us
    all_to_all x1, starting transfers between devices, on_device(): lax.all_to_all(packed, 'col', 0, 0, tiled=True, axis_index_groups=same_core)  10.3 us
    all_to_all x1, waiting for transfers between devices, on_device(): lax.all_to_all(packed, 'col', 0, 0, tiled=True, axis_index_groups=same_core)  9.88 us
    unnamed x18, local copies, waits for them, and re-layouts  7.93 us
    pallas_call x1, Pallas kernels, on_device(): pl.pallas_call(nodes_kernel, in_specs=[VMEM] * 3, out_specs=VMEM, out_sha...  4.48 us
    pallas_call x1, Pallas kernels, on_device(): pl.pallas_call(near_kernel, in_specs=[VMEM] * 4, out_specs=[HBM, VMEM], o...  4.23 us
  transfers between devices with their start and end apart: 5, of which 5 were waited for; matrix products, arithmetic and copies ran while one was open for 2% of the time, Pallas kernels for 15%

profile of v2, /device:TPU:8, one launch (start us, length us, event | category | flops | bytes accessed | tf_op | source)
XLA Modules:
  0.0 113.2 jit_solution(9081741072557656077)
XLA Ops:
  0.6 1.6 %pack.1 = bf16[8,136,128]{2,1,0:T(8,128)(2,1)} custom-call(bf16[128,128]{1,0:T(8,128)(2,1)} %freq.1, bf16[1,128]{1,0:T(2,128)(2,1)} %bitcast.25), custom_call_target="tpu_custom_call" | custom-call | tf_op jit(solution)/shard_map/pack/pallas_call | solution.py:387
  2.2 10.3 %all-to-all-start = ((bf16[8,136,128]{2,1,0:T(8,128)(2,1)}), bf16[8,136,128]{2,1,0:T(8,128)(2,1)S(1)}, u32[]{:S(2)}, u32[]{:S(2)}) async-start(bf16[8,136,128]{2,1,0:T(8,128)(2,1)} %pack.1), calls=%async_computation | async-start | bytes 557056 | tf_op jit(solution)/shard_map/all_to_all | solution.py:401
  12.5 0.0 copy-start.3
  12.5 0.9 copy-done.3
  13.5 0.7 reshape.52.weight
  14.2 0.7 reshape.53.size
  14.9 9.9 %all-to-all-done.freq = bf16[8,136,128]{2,1,0:T(8,128)(2,1)S(1)} async-done(((bf16[8,136,128]{2,1,0:T(8,128)(2,1)}), bf16[8,136,128]{2,1,0:T(8,128)(2,1)S(1)}, u32[]{:S(2)}, u32[]{:S(2)}) %all-to-all-start) | async-done | bytes 278560 | tf_op jit(solution)/shard_map/all_to_all | solution.py:401
  24.7 4.2 %near_features.1 = (bf16[9216,1024]{1,0:T(8,128)(2,1)}, f32[32,8,128]{2,1,0:T(8,128)}) custom-call(bf16[1024,128]{1,0:T(8,128)(2,1)S(1)} %stage_cov.1.cov, bf16[8,136,128]{2,1,0:T(8,128)(2,1)S(1)} %all-to-all-done.freq, bf16[1,1024]{1,0:T(2,128)(2,1)S(1)} %reshape.52.weight, bf16[1,1024]{1,0:T(2,128)(2,1)S(1)} %reshape.53.size), custom_call_target="tpu_custom_call" | custom-call | tf_op jit(solution)/shard_map/near_features/pallas_call | solution.py:406
  29.0 10.2 %all-to-all-start.1 = ((f32[32,8,128]{2,1,0:T(8,128)}), f32[32,8,128]{2,1,0:T(8,128)}, u32[]{:S(2)}, u32[]{:S(2)}) async-start(f32[32,8,128]{2,1,0:T(8,128)} %get-tuple-element.44), calls=%async_computation.1 | async-start | bytes 262144 | tf_op jit(solution)/shard_map/all_to_all | solution.py:424
  39.2 1.1 fusion
  40.4 2.2 %all-gather = bf16[16,136,128]{2,1,0:T(8,128)(2,1)S(1)} all-gather(bf16[8,136,128]{2,1,0:T(8,128)(2,1)S(1)} %all-to-all-done.freq), channel_id=2, replica_groups={{0,1},{2,3},{4,5},{6,7},{8,9},{10,11},{12,13},{14,15},{16,17},{18,19},{..., dimensions={0}, use_global_device_ids=true | all-gather | bytes 835584 | tf_op jit(solution)/shard_map/all_gather | solution.py:425
  42.6 2.7 %far_features.1.far = bf16[1024,1024]{1,0:T(8,128)(2,1)S(1)} custom-call(s32[1]{0:T(128)} %bitcast.1.core, bf16[1024,128]{1,0:T(8,128)(2,1)S(1)} %stage_cov.1.cov, bf16[2,8,136,128]{3,2,1,0:T(8,128)(2,1)S(1)} %bitcast.14), custom_call_target="tpu_custom_call" | custom-call | flops 289406976 | bytes 2097152 | tf_op jit(solution)/shard_map/far_features/pallas_call | solution.py:165
  45.3 3.5 %all-to-all-done.1 = f32[32,8,128]{2,1,0:T(8,128)} async-done(((f32[32,8,128]{2,1,0:T(8,128)}), f32[32,8,128]{2,1,0:T(8,128)}, u32[]{:S(2)}, u32[]{:S(2)}) %all-to-all-start.1) | async-done | bytes 131104 | tf_op jit(solution)/shard_map/all_to_all | solution.py:424
  48.8 0.9 reduce_sum.9
  49.8 1.8 %all-gather.1 = f32[16,128]{1,0:T(8,128)S(1)} all-gather(f32[8,128]{1,0:T(8,128)S(1)} %broadcast_multiply_fusion), channel_id=3, replica_groups={{0,1},{2,3},{4,5},{6,7},{8,9},{10,11},{12,13},{14,15},{16,17},{18,19},{..., dimensions={0}, use_global_device_ids=true | all-gather | bytes 12288 | tf_op jit(solution)/shard_map/all_gather | solution.py:432
  51.6 3.3 %first_product.1 = (f32[32,16,128]{2,1,0:T(8,128)S(1)}, f32[1,1024]{1,0:T(1,128)S(1)}, f32[16,128]{1,0:T(8,128)S(1)}) custom-call(s32[1]{0:T(128)} %bitcast.1.core, f32[2,8,128]{2,1,0:T(8,128)S(1)} %bitcast.19, bf16[9216,1024]{1,0:T(8,128)(2,1)} %get-tuple-element.47.near, bf16[1024,1024]{1,0:T(8,128)(2,1)S(1)} %far_features.1.far, ...), custom_call_target="tpu_custom_call" | custom-call | flops 134217728 | bytes 4194304 | tf_op jit(solution)/shard_map/first_product/pallas_call | solution.py:440
  54.8 0.0 copy-start.4
  54.9 0.7 copy-done.4
  55.6 6.3 %all-to-all-start.2 = ((f32[32,16,128]{2,1,0:T(8,128)}), f32[32,16,128]{2,1,0:T(8,128)S(1)}, u32[]{:S(2)}, u32[]{:S(2)}) async-start(f32[32,16,128]{2,1,0:T(8,128)} %copy-done.4), calls=%async_computation.2 | async-start | bytes 524288 | tf_op jit(solution)/shard_map/all_to_all | solution.py:451
  61.9 5.0 %node_features_a.1.first = bf16[1024,2048]{1,0:T(8,128)(2,1)S(1)} custom-call(s32[1]{0:T(128)} %bitcast.1.core, bf16[1024,128]{1,0:T(8,128)(2,1)S(1)} %bitcast.18, bf16[2,8,136,128]{3,2,1,0:T(8,128)(2,1)S(1)} %bitcast.15), custom_call_target="tpu_custom_call" | custom-call | flops 578813952 | bytes 4194304 | tf_op jit(solution)/shard_map/node_features_a/pallas_call | solution.py:165
  66.9 0.0 copy-start
  66.9 2.0 %copy-done = bf16[1024,2048]{1,0:T(8,128)(2,1)} copy-done((bf16[1024,2048]{1,0:T(8,128)(2,1)}, bf16[1024,2048]{1,0:T(8,128)(2,1)S(1)}, u32[]{:S(2)}) %copy-start) | copy-done | bytes 4194328
  68.9 5.5 %all-to-all-done.2.arrived = f32[32,16,128]{2,1,0:T(8,128)S(1)} async-done(((f32[32,16,128]{2,1,0:T(8,128)}), f32[32,16,128]{2,1,0:T(8,128)S(1)}, u32[]{:S(2)}, u32[]{:S(2)}) %all-to-all-start.2) | async-done | bytes 262176 | tf_op jit(solution)/shard_map/all_to_all | solution.py:451
  74.4 4.0 %second_product.1 = (f32[32,16,128]{2,1,0:T(8,128)}, f32[2,1024]{1,0:T(2,128)S(1)}, f32[16,128]{1,0:T(8,128)S(1)}, f32[16,128]{1,0:T(8,128)S(1)}, f32[16,128]{1,0:T(8,128)S(1)}) custom-call(f32[32,16,128]{2,1,0:T(8,128)S(1)} %all-to-all-done.2.arrived, f32[16,128]{1,0:T(8,128)S(1)} %get-tuple-element.54.rhs, f32[1,1024]{1,0:T(1,128)S(1)} %get-tuple-element.55.before, ...), custom_call_target="tpu_custom_call" | custom-call | flops 134217728 | bytes 4194304 | tf_op jit(solution)/shard_map/second_product/pallas_call | solution.py:455
  78.4 0.0 copy-start.5
  78.4 0.0 copy-start.6
  78.4 4.6 %all-to-all-start.3 = ((f32[32,16,128]{2,1,0:T(8,128)}), f32[32,16,128]{2,1,0:T(8,128)S(1)}, u32[]{:S(2)}, u32[]{:S(2)}) async-start(f32[32,16,128]{2,1,0:T(8,128)} %get-tuple-element.58), calls=%async_computation.3 | async-start | bytes 524288 | tf_op jit(solution)/shard_map/all_to_all | solution.py:466
  83.1 5.0 %node_features_b.1.second = bf16[1024,2048]{1,0:T(8,128)(2,1)S(1)} custom-call(s32[1]{0:T(128)} %bitcast.1.core, bf16[1024,128]{1,0:T(8,128)(2,1)S(1)} %bitcast.17, bf16[2,8,136,128]{3,2,1,0:T(8,128)(2,1)S(1)} %bitcast.16), custom_call_target="tpu_custom_call" | custom-call | flops 578813952 | bytes 4194304 | tf_op jit(solution)/shard_map/node_features_b/pallas_call | solution.py:165
  88.0 0.0 copy-start.2
  88.1 2.0 %copy-done.2 = bf16[1024,2048]{1,0:T(8,128)(2,1)} copy-done((bf16[1024,2048]{1,0:T(8,128)(2,1)}, bf16[1024,2048]{1,0:T(8,128)(2,1)S(1)}, u32[]{:S(2)}) %copy-start.2) | copy-done | bytes 4194328
  90.1 4.5 %all-to-all-done.3.arrived = f32[32,16,128]{2,1,0:T(8,128)S(1)} async-done(((f32[32,16,128]{2,1,0:T(8,128)}), f32[32,16,128]{2,1,0:T(8,128)S(1)}, u32[]{:S(2)}, u32[]{:S(2)}) %all-to-all-start.3) | async-done | bytes 262176 | tf_op jit(solution)/shard_map/all_to_all | solution.py:466
  94.6 0.0 copy-done.5
  94.6 0.0 copy-done.6
  94.6 3.5 %third_product.1 = (f32[32,4,128]{2,1,0:T(4,128)}, f32[2,16,128]{2,1,0:T(8,128)S(1)}, f32[8,128]{1,0:T(8,128)S(1)}) custom-call(f32[32,16,128]{2,1,0:T(8,128)S(1)} %all-to-all-done.3.arrived, f32[16,128]{1,0:T(8,128)S(1)} %get-tuple-element.61.solution, f32[16,128]{1,0:T(8,128)S(1)} %get-tuple-element.62.residual, ...), custom_call_target="tpu_custom_call" | custom-call | flops 134217728 | bytes 4194304 | tf_op jit(solution)/shard_map/third_product/pallas_call | solution.py:470
  98.2 5.3 %all-to-all-start.4 = ((f32[32,4,128]{2,1,0:T(4,128)}), f32[32,4,128]{2,1,0:T(4,128)S(1)}, u32[]{:S(2)}, u32[]{:S(2)}) async-start(f32[32,4,128]{2,1,0:T(4,128)} %get-tuple-element.67), calls=%async_computation.4 | async-start | bytes 131072 | tf_op jit(solution)/shard_map/all_to_all | solution.py:485
  103.5 0.0 copy-start.1
  103.5 2.2 %copy-done.1 = bf16[1024,2048]{1,0:T(8,128)(2,1)S(1)} copy-done((bf16[1024,2048]{1,0:T(8,128)(2,1)S(1)}, bf16[1024,2048]{1,0:T(8,128)(2,1)}, u32[]{:S(2)}) %copy-start.1) | copy-done | bytes 4194328
  105.7 0.0 copy-start.7
  105.7 0.0 copy-start.8
  105.7 4.5 %node_values.1 = f32[2,2048]{1,0:T(2,128)S(1)} custom-call(f32[2,16,128]{2,1,0:T(8,128)S(1)} %get-tuple-element.68.both, bf16[1024,2048]{1,0:T(8,128)(2,1)S(1)} %copy-done.1, bf16[1024,2048]{1,0:T(8,128)(2,1)} %copy-done.2), custom_call_target="tpu_custom_call" | custom-call | flops 268435456 | bytes 8388608 | tf_op jit(solution)/shard_map/node_values/pallas_call | solution.py:486
  110.2 2.3 %all-to-all-done.4.arrived = f32[32,4,128]{2,1,0:T(4,128)S(1)} async-done(((f32[32,4,128]{2,1,0:T(4,128)}), f32[32,4,128]{2,1,0:T(4,128)S(1)}, u32[]{:S(2)}, u32[]{:S(2)}) %all-to-all-start.4) | async-done | bytes 65568 | tf_op jit(solution)/shard_map/all_to_all | solution.py:485
  112.5 0.0 copy-done.7
  112.5 0.0 copy-done.8
  112.5 0.7 last.1
  (4 shorter events, 0.1 us)
Async XLA Ops:
  2.2 22.6 %all-to-all-start = ((bf16[8,136,128]{2,1,0:T(8,128)(2,1)}), bf16[8,136,128]{2,1,0:T(8,128)(2,1)S(1)}, u32[]{:S(2)}, u32[]{:S(2)}) async-start(bf16[8,136,128]{2,1,0:T(8,128)(2,1)} %pack.1), calls=%async_computation | async-start | bytes 557056 | tf_op jit(solution)/shard_map/all_to_all | solution.py:401
  12.5 0.9 copy-start.3
  29.0 19.8 %all-to-all-start.1 = ((f32[32,8,128]{2,1,0:T(8,128)}), f32[32,8,128]{2,1,0:T(8,128)}, u32[]{:S(2)}, u32[]{:S(2)}) async-start(f32[32,8,128]{2,1,0:T(8,128)} %get-tuple-element.44), calls=%async_computation.1 | async-start | bytes 262144 | tf_op jit(solution)/shard_map/all_to_all | solution.py:424
  54.8 0.7 copy-start.4
  55.6 18.9 %all-to-all-start.2 = ((f32[32,16,128]{2,1,0:T(8,128)}), f32[32,16,128]{2,1,0:T(8,128)S(1)}, u32[]{:S(2)}, u32[]{:S(2)}) async-start(f32[32,16,128]{2,1,0:T(8,128)} %copy-done.4), calls=%async_computation.2 | async-start | bytes 524288 | tf_op jit(solution)/shard_map/all_to_all | solution.py:451
  66.9 2.0 %copy-start = (bf16[1024,2048]{1,0:T(8,128)(2,1)}, bf16[1024,2048]{1,0:T(8,128)(2,1)S(1)}, u32[]{:S(2)}) copy-start(bf16[1024,2048]{1,0:T(8,128)(2,1)S(1)} %node_features_a.1.first) | copy-start | bytes 12582916
  78.4 16.2 %copy-start.5 = (s32[1024,1]{0,1:T(1,128)S(1)}, s32[1024,1]{0,1:T(1,128)}, u32[]{:S(2)}) copy-start(s32[1024,1]{0,1:T(1,128)} %param.13) | copy-start | bytes 12292
  78.4 16.2 %copy-start.6 = (s32[1024]{0:T(1024)S(1)}, s32[1024]{0:T(1024)}, u32[]{:S(2)}) copy-start(s32[1024]{0:T(1024)} %param.14) | copy-start | bytes 12292
  78.4 16.2 %all-to-all-start.3 = ((f32[32,16,128]{2,1,0:T(8,128)}), f32[32,16,128]{2,1,0:T(8,128)S(1)}, u32[]{:S(2)}, u32[]{:S(2)}) async-start(f32[32,16,128]{2,1,0:T(8,128)} %get-tuple-element.58), calls=%async_computation.3 | async-start | bytes 524288 | tf_op jit(solution)/shard_map/all_to_all | solution.py:466
  88.0 2.0 %copy-start.2 = (bf16[1024,2048]{1,0:T(8,128)(2,1)}, bf16[1024,2048]{1,0:T(8,128)(2,1)S(1)}, u32[]{:S(2)}) copy-start(bf16[1024,2048]{1,0:T(8,128)(2,1)S(1)} %node_features_b.1.second) | copy-start | bytes 12582916
  98.2 14.3 %all-to-all-start.4 = ((f32[32,4,128]{2,1,0:T(4,128)}), f32[32,4,128]{2,1,0:T(4,128)S(1)}, u32[]{:S(2)}, u32[]{:S(2)}) async-start(f32[32,4,128]{2,1,0:T(4,128)} %get-tuple-element.67), calls=%async_computation.4 | async-start | bytes 131072 | tf_op jit(solution)/shard_map/all_to_all | solution.py:485
  103.5 2.2 %copy-start.1 = (bf16[1024,2048]{1,0:T(8,128)(2,1)S(1)}, bf16[1024,2048]{1,0:T(8,128)(2,1)}, u32[]{:S(2)}) copy-start(bf16[1024,2048]{1,0:T(8,128)(2,1)} %copy-done) | copy-start | bytes 12582916
  105.7 6.8 %copy-start.7 = (f32[128]{0:T(128)S(1)}, f32[128]{0:T(128)}, u32[]{:S(2)}) copy-start(f32[128]{0:T(128)} %param.18) | copy-start | bytes 1540
  105.7 6.8 %copy-start.8 = (s32[128]{0:T(128)S(1)}, s32[128]{0:T(128)}, u32[]{:S(2)}) copy-start(s32[128]{0:T(128)} %param.19) | copy-start | bytes 1540

commit v3 on v2

--- a/solution.py
+++ b/solution.py
@@ -69,7 +69,8 @@
 VMEM = pl.BlockSpec(memory_space=pltpu.VMEM)
 SMEM = pl.BlockSpec(memory_space=pltpu.SMEM)
 HBM = pl.BlockSpec(memory_space=pltpu.HBM)
-PARTS = 4
+PARTS = 2
+KEPT = 0.25
 SPARE = 9
 PHASE_ROWS = 8
 
@@ -142,59 +143,117 @@
 FEATURE_ROWS = 256
 
 
-def features_kernel(order, core, cov, freq, out):
-    half = freq.shape[1] * LANES
-
+def half_features(cov, freq, target, base):
     def step(i, carry):
         at = rows_at(i, FEATURE_ROWS)
-        for index, other in enumerate(order):
-            source = 1 - core[0] if other else core[0]
-
-            def store(column, value, base=index * half):
-                out[at, base + column : base + column + value.shape[1]] = value
-
-            feature_block(cov[at, :], freq.at[source], store)
+
+        def store(column, value):
+            target[at, base + column : base + column + value.shape[1]] = value
+
+        feature_block(cov[at, :], freq, store)
         return carry
 
     lax.fori_loop(0, cov.shape[0] // FEATURE_ROWS, step, 0)
 
 
-def features(core, cov, freq, order, name):
+def far_kernel(core, cov, freq, out):
+    half_features(cov, freq.at[1 - core[0]], out, 0)
+
+
+def far_features(core, cov, freq):
     rows, depth = cov.shape
-    columns = len(order) * freq.shape[1] * LANES
+    columns = freq.shape[1] * LANES
     return pl.pallas_call(
-        functools.partial(features_kernel, order),
+        far_kernel,
         in_specs=[SMEM, VMEM, VMEM],
         out_specs=VMEM,
         out_shape=jax.ShapeDtypeStruct((rows, columns), BF16),
         compiler_params=params(),
         cost_estimate=cost(2 * rows * depth * columns + 20 * rows * columns, 2 * rows * columns),
-        name=name,
+        name="far_features",
     )(core, cov, freq)
 
 
-def near_kernel(cov, freq, weight, size, phi_out, out, phi, gathered, tiles, sems):
-    def part(i):
-        at = rows_at(i, FEATURE_ROWS)
-        return pltpu.make_async_copy(phi.at[at], phi_out.at[at], sems.at[i])
+def node_kernel(first, core, cov, freq, *rest):
+    out, held, sems = rest[-3:]
+    half = freq.shape[1] * LANES
+    steps = cov.shape[0] // FEATURE_ROWS
+
+    def leave(i):
+        at, to = rows_at(i, FEATURE_ROWS), rows_at(i + first // FEATURE_ROWS, FEATURE_ROWS)
+        return pltpu.make_async_copy(held.at[at], out.at[to], sems.at[i])
 
     def step(i, carry):
         at = rows_at(i, FEATURE_ROWS)
-
-        def store(column, value):
-            phi[at, column : column + value.shape[1]] = value
-
-        feature_block(cov[at, :], freq, store)
-        part(i).start()
+        for index in range(2):
+            source = core[0] if index == 0 else 1 - core[0]
+
+            def store(column, value, base=index * half):
+                held[at, base + column : base + column + value.shape[1]] = value
+
+            feature_block(cov[at, :], freq.at[source], store)
+        leave(i).start()
         return carry
 
-    steps = cov.shape[0] // FEATURE_ROWS
     lax.fori_loop(0, steps, step, 0)
+    for i in range(steps):
+        leave(i).wait()
+
+
+def node_features(core, cov, freq, before, first, height, name):
+    rows, depth = cov.shape
+    columns = 2 * freq.shape[1] * LANES
+    earlier = () if before is None else (before,)
+    return pl.pallas_call(
+        functools.partial(node_kernel, first),
+        in_specs=[SMEM, VMEM, VMEM] + [HBM] * len(earlier),
+        out_specs=HBM,
+        out_shape=jax.ShapeDtypeStruct((height, columns), BF16),
+        scratch_shapes=[
+            pltpu.VMEM((rows, columns), BF16),
+            pltpu.SemaphoreType.DMA((rows // FEATURE_ROWS,)),
+        ],
+        input_output_aliases={3: 0} if earlier else {},
+        compiler_params=params(),
+        cost_estimate=cost(2 * rows * depth * columns + 20 * rows * columns, 2 * rows * columns),
+        name=name,
+    )(core, cov, freq, *earlier)
+
+
+def near_kernel(
+    core, cov, freq, weight, size, kept, rest_out, out, rest, gathered, tiles, sems
+):
+    first = kept.shape[0]
+
+    def fill(target, base, count, after=None):
+        group = target.shape[0] // count
+
+        def step(i, carry):
+            at = rows_at(i, group)
+
+            def store(column, value):
+                target[at, column : column + value.shape[1]] = value
+
+            rows = cov[pl.ds(pl.multiple_of(base + i * group, 64), group), :]
+            feature_block(rows, freq.at[core[0]], store)
+            if after is not None:
+                after(i, group).start()
+            return carry
+
+        lax.fori_loop(0, count, step, 0)
+
+    def leave(i, group):
+        at = rows_at(i, group)
+        return pltpu.make_async_copy(rest.at[at], rest_out.at[at], sems.at[i])
+
+    fill(rest, first, PARTS, leave)
+    fill(kept, 0, PARTS)
     product = weight[...].astype(F32) * size[...].astype(F32)
-    gathered[...] = dot_nn(stack_rows(split3(product), 16), phi[...])
+    split = stack_rows(split3(product), 16)
+    gathered[...] = dot_nn(split[:, :first], kept[...]) + dot_nn(split[:, first:], rest[...])
     send_whole(gathered, tiles, out)
-    for i in range(steps):
-        part(i).wait()
+    for i in range(PARTS):
+        leave(i, rest.shape[0] // PARTS).wait()
 
 
 def rows_of(vector):
@@ -210,59 +269,59 @@
         out[copy] = whole
 
 
-def fetch(near, held, sems):
+def fetch(rest, held, sems):
     part = held.shape[0] // PARTS
     copies = []
     for k in range(PARTS):
         at = slice(k * part, (k + 1) * part)
-        copy = pltpu.make_async_copy(near.at[at], held.at[at], sems.at[k])
+        copy = pltpu.make_async_copy(rest.at[at], held.at[at], sems.at[k])
         copy.start()
         copies.append((at, copy))
     return copies
 
 
-def forward(direction, held, copies, far):
+def forward(direction, kept, held, copies, far):
     split = rows_of(direction)
     half = far.shape[1]
+    near = split[:, :half]
     total = jnp.sum(dot_nt(split[:, half:], far[...]), axis=0, keepdims=True)
-    values = []
+    values = [jnp.sum(dot_nt(near, kept[...]), axis=0, keepdims=True)]
     for at, copy in copies:
         copy.wait()
-        part = jnp.sum(dot_nt(split[:, :half], held[at]), axis=0, keepdims=True)
-        values.append(part + total[:, at])
-    return jnp.concatenate(values, axis=1)
-
-
-def product(direction, held, copies, far, weight, gathered, tiles, out, scale):
-    values = forward(direction, held, copies, far)
+        values.append(jnp.sum(dot_nt(near, held[at]), axis=0, keepdims=True))
+    return jnp.concatenate(values, axis=1) + total
+
+
+def product(direction, kept, held, copies, far, weight, gathered, tiles, out, scale):
+    values = forward(direction, kept, held, copies, far)
     split = stack_rows(split3(weight[...].astype(F32) * values * scale), 16)
-    half = far.shape[1]
-    gathered[:, :half] = dot_nn(split, held[...])
+    half, first = far.shape[1], kept.shape[0]
     gathered[:, half:] = dot_nn(split, far[...])
+    gathered[:, :half] = dot_nn(split[:, :first], kept[...]) + dot_nn(split[:, first:], held[...])
     send_whole(gathered, tiles, out)
     return values
 
 
 def first_kernel(
-    scale, core, halves, near, far, weight, out, values_out, rhs_out, gathered, tiles, held, sems
+    scale, core, halves, kept, rest, far, weight, out, values_out, rhs_out, gathered, tiles, held, sems
 ):
-    copies = fetch(near, held, sems)
+    copies = fetch(rest, held, sems)
     low, high = halves[0], halves[1]
     swap = core[0] == 1
     half = low.shape[0]
     rhs_out[0:half, :] = jnp.where(swap, high, low)
     rhs_out[half : 2 * half, :] = jnp.where(swap, low, high)
     values_out[...] = product(
-        rhs_out[...], held, copies, far, weight, gathered, tiles, out, scale
+        rhs_out[...], kept, held, copies, far, weight, gathered, tiles, out, scale
     )
 
 
 def second_kernel(
-    scale, arrived, rhs, before, near, far, weight,
+    scale, arrived, rhs, before, kept, rest, far, weight,
     out, fit_out, solution_out, residual_out, direction_out,
     gathered, tiles, held, sems,
 ):
-    copies = fetch(near, held, sems)
+    copies = fetch(rest, held, sems)
     direction = rhs[...]
     norm = total_of(direction * direction)
     image = direction + jnp.sum(arrived[...], axis=0)
@@ -274,16 +333,16 @@
     direction_out[...] = later
     fit_out[0:1, :] = length * before[...]
     fit_out[1:2, :] = product(
-        later, held, copies, far, weight, gathered, tiles, out, scale
+        later, kept, held, copies, far, weight, gathered, tiles, out, scale
     )
 
 
 def third_kernel(
-    scale, fit_scale, arrived, solution, residual, direction, fit, near, far, weight, size, owner, patient,
+    scale, fit_scale, arrived, solution, residual, direction, fit, kept, rest, far, weight, size, owner, patient,
     out, both_out, norm_out,
     held, sems,
 ):
-    copies = fetch(near, held, sems)
+    copies = fetch(rest, held, sems)
     before = direction[...]
     left = residual[...]
     norm = total_of(left * left)
@@ -295,17 +354,17 @@
     both_out[0] = solution[...] + length * before
     both_out[1] = later
     norm_out[...] = jnp.broadcast_to(norm_next, norm_out.shape)
-    values = forward(later, held, copies, far)
+    values = forward(later, kept, held, copies, far)
     fitted = fit[0:1, :] + length * fit[1:2, :]
     weights = weight[...].astype(F32)
     weighted = weights * values
     energy = total_of(weighted * values) * scale
-    rest = weights * (size[...].astype(F32) - fitted * fit_scale)
+    part = weights * (size[...].astype(F32) - fitted * fit_scale)
     owners, patients = out.shape[0], out.shape[2]
     here = values.shape[1]
     to_owner = (owner[...] == lax.broadcasted_iota(jnp.int32, (owners, here), 0)).astype(F32)
     to_patient = (patient[...] == lax.broadcasted_iota(jnp.int32, (patients, here), 0)).astype(F32)
-    parts = split3(rest) + split3(weighted * fit_scale) + (weights,)
+    parts = split3(part) + split3(weighted * fit_scale) + (weights,)
     tall = jnp.concatenate([to_owner * part for part in parts], axis=0).astype(BF16)
     sums = dot_nt(tall, to_patient.astype(BF16))
     part = [sums[i * owners : (i + 1) * owners, :] for i in range(len(parts))]
@@ -315,16 +374,18 @@
     out[:, 3, :] = jnp.broadcast_to(energy, (owners, patients))
 
 
-def nodes_kernel(both, first, second, out):
-    rows = split3(as_row(both[0])) + split3(as_row(both[1]))
-    split = stack_rows(rows, 16)
-    base = 0
-    for phi in (first, second):
-        products = dot_nt(split, phi[...])
-        where = slice(base, base + phi.shape[0])
-        out[0:1, where] = products[0:1] + products[1:2] + products[2:3]
-        out[1:2, where] = products[3:4] + products[4:5] + products[5:6]
-        base += phi.shape[0]
+NODE_ROWS = 512
+
+
+def nodes_kernel(both, phi, out, split):
+    @pl.when(pl.program_id(0) == 0)
+    def _():
+        rows = split3(as_row(both[0])) + split3(as_row(both[1]))
+        split[...] = stack_rows(rows, 16)
+
+    products = dot_nt(split[...], phi[...])
+    out[0:1, :] = products[0:1] + products[1:2] + products[2:3]
+    out[1:2, :] = products[3:4] + products[4:5] + products[5:6]
 
 
 def last_kernel(fit_scale, mine, arrived, both, norm, node_values, time, flag, loglik, weights_out, tiles):
@@ -397,79 +458,82 @@
         compiler_params=params(60),
         name="pack",
     )(inducing_freq, inducing_phase.reshape(1, own))
-    packed, cov = together((packed, visit_cov))
+    packed, cov, turned = together((packed, visit_cov, node_cov))
     near_freq = lax.all_to_all(packed, "col", 0, 0, tiled=True, axis_index_groups=same_core)
     cov = stage(cov, "stage_cov")
-    near_freq, cov = together((near_freq, cov))
+    by_node = turned.transpose(1, 0, 2).reshape(nodes * patients, depth)
+    count = nodes * patients // 2
+    height = (SPARE * nodes * patients) // 4
+    node_covs = (by_node[:count], by_node[count:])
+    near_freq, cov, node_covs = together((near_freq, cov, node_covs))
+    freq = lax.all_gather(near_freq, "col", axis_index_groups=pairs)
 
     half = inducing // 2
-    near, sent = pl.pallas_call(
+    first = int(rows * KEPT)
+    kept, rest, sent = pl.pallas_call(
         near_kernel,
-        in_specs=[VMEM] * 4,
-        out_specs=[HBM, VMEM],
+        in_specs=[SMEM] + [VMEM] * 4,
+        out_specs=[VMEM, HBM, VMEM],
         out_shape=[
+            jax.ShapeDtypeStruct((first, half), BF16),
             jax.ShapeDtypeStruct((SPARE * rows, half), BF16),
             jax.ShapeDtypeStruct((blocks, tall // 2, LANES), F32),
         ],
         scratch_shapes=[
-            pltpu.VMEM((rows, half), BF16),
+            pltpu.VMEM((rows - first, half), BF16),
             pltpu.VMEM((16, half), F32),
             pltpu.VMEM((tall // 2, LANES), F32),
-            pltpu.SemaphoreType.DMA((rows // FEATURE_ROWS,)),
+            pltpu.SemaphoreType.DMA((PARTS,)),
         ],
         compiler_params=params(),
         name="near_features",
-    )(cov, near_freq, weight, size)
-    sent, late_freq = together((sent, near_freq))
+    )(core, cov, freq, weight, size)
+    sent, late_freq = together((sent, freq))
     arrived = lax.all_to_all(sent, "blk", 0, 0, tiled=True)
-    freq = lax.all_gather(late_freq, "col", axis_index_groups=pairs)
-    far = features(core, cov, freq, (1,), "far_features")
-    by_node = node_cov.transpose(1, 0, 2).reshape(nodes * patients, depth)
-    count = nodes * patients // 2
-    node_covs = (by_node[:count], by_node[count:])
-    arrived, far, node_covs = together((arrived, far, node_covs))
+    far = far_features(core, cov, late_freq)
+    arrived, far = together((arrived, far))
     rhs = jnp.sum(arrived, axis=0) * (1.0 / math.sqrt(rows * blocks))
     halves = lax.all_gather(rhs, "col", axis_index_groups=pairs)
 
     message = jax.ShapeDtypeStruct((blocks, tall, LANES), F32)
     vector = jax.ShapeDtypeStruct((tall, LANES), F32)
-    fetched = [pltpu.VMEM((rows, half), BF16), pltpu.SemaphoreType.DMA((PARTS,))]
+    fetched = [pltpu.VMEM((rows - first, half), BF16), pltpu.SemaphoreType.DMA((PARTS,))]
     scratch = [pltpu.VMEM((16, inducing), F32), pltpu.VMEM((tall, LANES), F32)] + fetched
     work = cost(64 * rows * inducing, 2 * rows * inducing)
 
     sent, before, rhs = pl.pallas_call(
         functools.partial(first_kernel, scale),
-        in_specs=[SMEM, VMEM, HBM, VMEM, VMEM],
+        in_specs=[SMEM, VMEM, VMEM, HBM, VMEM, VMEM],
         out_specs=[VMEM] * 3,
         out_shape=[message, jax.ShapeDtypeStruct((1, rows), F32), vector],
         scratch_shapes=scratch,
         compiler_params=params(),
         cost_estimate=work,
         name="first_product",
-    )(core, halves, near, far, weight)
+    )(core, halves, kept, rest, far, weight)
     sent, node_cov_now = together((sent, node_covs[0]))
     arrived = lax.all_to_all(sent, "blk", 0, 0, tiled=True)
-    node_first = features(core, node_cov_now, freq, (0, 1), "node_features_a")
-    arrived, node_first = together((arrived, node_first))
+    node_phi = node_features(core, node_cov_now, freq, None, 0, height, "node_features_a")
+    arrived, node_phi = together((arrived, node_phi))
 
     sent, fit, solution, residual, direction = pl.pallas_call(
         functools.partial(second_kernel, scale),
-        in_specs=[VMEM, VMEM, VMEM, HBM, VMEM, VMEM],
+        in_specs=[VMEM] * 4 + [HBM, VMEM, VMEM],
         out_specs=[VMEM] * 5,
         out_shape=[message, jax.ShapeDtypeStruct((2, rows), F32), vector, vector, vector],
         scratch_shapes=scratch,
         compiler_params=params(),
         cost_estimate=work,
         name="second_product",
-    )(arrived, rhs, before, near, far, weight)
+    )(arrived, rhs, before, kept, rest, far, weight)
     sent, node_cov_now = together((sent, node_covs[1]))
     arrived = lax.all_to_all(sent, "blk", 0, 0, tiled=True)
-    node_second = features(core, node_cov_now, freq, (0, 1), "node_features_b")
-    arrived, node_second = together((arrived, node_second))
+    node_phi = node_features(core, node_cov_now, freq, node_phi, count, height, "node_features_b")
+    arrived, node_phi = together((arrived, node_phi))
 
     sent, both, norm = pl.pallas_call(
         functools.partial(third_kernel, scale, fit_scale),
-        in_specs=[VMEM] * 5 + [HBM] + [VMEM] * 5,
+        in_specs=[VMEM] * 6 + [HBM] + [VMEM] * 5,
         out_specs=[VMEM] * 3,
         out_shape=[
             jax.ShapeDtypeStruct((blocks, 4, patients), F32),
@@ -480,18 +544,23 @@
         compiler_params=params(),
         cost_estimate=work,
         name="third_product",
-    )(arrived, solution, residual, direction, fit, near, far, weight, size, owner, patient)
+    )(arrived, solution, residual, direction, fit, kept, rest, far, weight, size, owner, patient)
     sent, both = together((sent, both))
     arrived = lax.all_to_all(sent, "blk", 0, 0, tiled=True)
     node_values = pl.pallas_call(
         nodes_kernel,
-        in_specs=[VMEM] * 3,
-        out_specs=VMEM,
+        grid=(2 * count // NODE_ROWS,),
+        in_specs=[
+            pl.BlockSpec(both.shape, lambda i: (0, 0, 0)),
+            pl.BlockSpec((NODE_ROWS, inducing), lambda i: (i, 0)),
+        ],
+        out_specs=pl.BlockSpec((2, NODE_ROWS), lambda i: (0, i)),
         out_shape=jax.ShapeDtypeStruct((2, 2 * count), F32),
+        scratch_shapes=[pltpu.VMEM((16, inducing), BF16)],
         compiler_params=params(),
         cost_estimate=cost(64 * 2 * count * inducing, 4 * count * inducing),
         name="node_values",
-    )(both, node_first, node_second)
+    )(both, node_phi)
     arrived, node_values = together((arrived, node_values))
 
     loglik, weights = pl.pallas_call(

time: 114 us -> 116 us (1.018)
  local copies, waits for them, and re-layouts: 10.4 us -> 6.53 us
  waiting for transfers between devices: 25.8 us -> 29.3 us
  Pallas kernels: 34.4 us -> 37.2 us
    all_to_all x4, waiting for transfers between devices: 15.9 us -> 21.9 us  [on_device(): arrived = lax.all_to_all(sent, 'blk', 0, 0, tiled=True)]
    unnamed x18 -> x16, local copies, waits for them, and re-layouts: 7.93 us -> 2.61 us
    all_to_all x1, waiting for transfers between devices: 9.88 us -> 7.32 us  [on_device(): lax.all_to_all(packed, 'col', 0, 0, tiled=True, axis_index_groups=same_core)]
    pallas_call x6, Pallas kernels: 25.3 us -> 27.4 us  [the longest x2 12 us: node_features(): pl.pallas_call(functools.partial(node_kernel, first), in_specs=[SMEM, VME...]
    slice x3, local copies, waits for them, and re-layouts: 1.14 us -> 2.54 us  [on_device(): node_covs = (by_node[:count], by_node[count:])]
  transfers between devices with their start and end apart: 5 -> 5, of which waited for: 5 -> 5; matrix products, arithmetic and copies ran while one was open for 2% -> 3% of each run, Pallas kernels for 15% -> 18%
where the time goes in v3:
time: 116 us; the launch traced here: 115 us
  Pallas kernels  37.2 us (32%)
  starting transfers between devices  35.9 us (31%)
  waiting for transfers between devices  29.3 us (25%)
  local copies, waits for them, and re-layouts  6.53 us (6%)
  blocking collectives  3.99 us (3%)
    all_to_all x4, starting transfers between devices, on_device(): arrived = lax.all_to_all(sent, 'blk', 0, 0, tiled=True)  25.5 us
    all_to_all x4, waiting for transfers between devices, on_device(): arrived = lax.all_to_all(sent, 'blk', 0, 0, tiled=True)  21.9 us
    pallas_call x2, Pallas kernels, node_features(): pl.pallas_call(functools.partial(node_kernel, first), in_specs=[SMEM, VME...  12 us
    all_to_all x1, starting transfers between devices, on_device(): lax.all_to_all(packed, 'col', 0, 0, tiled=True, axis_index_groups=same_core)  10.3 us
    all_to_all x1, waiting for transfers between devices, on_device(): lax.all_to_all(packed, 'col', 0, 0, tiled=True, axis_index_groups=same_core)  7.32 us
    pallas_call x1, Pallas kernels, on_device(): pl.pallas_call(nodes_kernel, grid=(2 * count // NODE_ROWS,), in_specs=[pl...  5.4 us
    pallas_call x1, Pallas kernels, on_device(): pl.pallas_call(functools.partial(third_kernel, scale, fit_scale), in_spec...  4.24 us
    pallas_call x1, Pallas kernels, on_device(): pl.pallas_call(near_kernel, in_specs=[SMEM] + [VMEM] * 4, out_specs=[VMEM...  3.81 us
  transfers between devices with their start and end apart: 5, of which 5 were waited for; matrix products, arithmetic and copies ran while one was open for 3% of the time, Pallas kernels for 18%

profile of v3, /device:TPU:8, one launch (start us, length us, event | category | flops | bytes accessed | tf_op | source)
XLA Modules:
  0.0 114.6 jit_solution(11679313502256220612)
XLA Ops:
  0.6 1.6 %pack.1 = bf16[8,136,128]{2,1,0:T(8,128)(2,1)} custom-call(bf16[128,128]{1,0:T(8,128)(2,1)} %freq.1, bf16[1,128]{1,0:T(2,128)(2,1)} %bitcast.26), custom_call_target="tpu_custom_call" | custom-call | tf_op jit(solution)/shard_map/pack/pallas_call | solution.py:448
  2.2 10.3 %all-to-all-start = ((bf16[8,136,128]{2,1,0:T(8,128)(2,1)}), bf16[8,136,128]{2,1,0:T(8,128)(2,1)S(1)}, u32[]{:S(2)}, u32[]{:S(2)}) async-start(bf16[8,136,128]{2,1,0:T(8,128)(2,1)} %pack.1), calls=%async_computation | async-start | bytes 557056 | tf_op jit(solution)/shard_map/all_to_all | solution.py:462
  12.5 0.0 copy-start.2
  12.5 0.9 copy-done.2
  13.5 0.7 reshape.52.weight
  14.2 0.7 reshape.53.size
  14.9 1.1 fusion
  15.9 0.7 copy.16
  16.7 0.7 copy.15
  17.4 7.3 %all-to-all-done = bf16[8,136,128]{2,1,0:T(8,128)(2,1)S(1)} async-done(((bf16[8,136,128]{2,1,0:T(8,128)(2,1)}), bf16[8,136,128]{2,1,0:T(8,128)(2,1)S(1)}, u32[]{:S(2)}, u32[]{:S(2)}) %all-to-all-start) | async-done | bytes 278560 | tf_op jit(solution)/shard_map/all_to_all | solution.py:462
  24.7 2.2 %all-gather = bf16[16,136,128]{2,1,0:T(8,128)(2,1)S(1)} all-gather(bf16[8,136,128]{2,1,0:T(8,128)(2,1)S(1)} %all-to-all-done), channel_id=2, replica_groups={{0,1},{2,3},{4,5},{6,7},{8,9},{10,11},{12,13},{14,15},{16,17},{18,19},{..., dimensions={0}, use_global_device_ids=true | all-gather | bytes 835584 | tf_op jit(solution)/shard_map/all_gather | solution.py:469
  26.9 3.8 %near_features.1 = (bf16[256,1024]{1,0:T(8,128)(2,1)S(1)}, bf16[9216,1024]{1,0:T(8,128)(2,1)}, f32[32,8,128]{2,1,0:T(8,128)}) custom-call(s32[1]{0:T(128)} %bitcast.1.core, bf16[1024,128]{1,0:T(8,128)(2,1)S(1)} %stage_cov.1.cov, bf16[2,8,136,128]{3,2,1,0:T(8,128)(2,1)S(1)} %bitcast.14, bf16[1,1024]{1,0:T(2,128)(2,1)S(1)} %reshape.52.weight, ...), custom_call_target="tpu_custom_call" | custom-call | tf_op jit(solution)/shard_map/near_features/pallas_call | solution.py:473
  30.8 10.2 %all-to-all-start.1 = ((f32[32,8,128]{2,1,0:T(8,128)}), f32[32,8,128]{2,1,0:T(8,128)}, u32[]{:S(2)}, u32[]{:S(2)}) async-start(f32[32,8,128]{2,1,0:T(8,128)} %get-tuple-element.47), calls=%async_computation.1 | async-start | bytes 262144 | tf_op jit(solution)/shard_map/all_to_all | solution.py:492
  41.0 2.7 %far_features.1.far = bf16[1024,1024]{1,0:T(8,128)(2,1)S(1)} custom-call(s32[1]{0:T(128)} %bitcast.1.core, bf16[1024,128]{1,0:T(8,128)(2,1)S(1)} %stage_cov.1.cov, bf16[2,8,136,128]{3,2,1,0:T(8,128)(2,1)S(1)} %bitcast.15), custom_call_target="tpu_custom_call" | custom-call | flops 289406976 | bytes 2097152 | tf_op jit(solution)/shard_map/far_features/pallas_call | solution.py:166
  43.7 7.2 %all-to-all-done.1 = f32[32,8,128]{2,1,0:T(8,128)} async-done(((f32[32,8,128]{2,1,0:T(8,128)}), f32[32,8,128]{2,1,0:T(8,128)}, u32[]{:S(2)}, u32[]{:S(2)}) %all-to-all-start.1) | async-done | bytes 131104 | tf_op jit(solution)/shard_map/all_to_all | solution.py:492
  50.9 0.9 reduce_sum.9
  51.9 1.8 %all-gather.1 = f32[16,128]{1,0:T(8,128)S(1)} all-gather(f32[8,128]{1,0:T(8,128)S(1)} %broadcast_multiply_fusion), channel_id=3, replica_groups={{0,1},{2,3},{4,5},{6,7},{8,9},{10,11},{12,13},{14,15},{16,17},{18,19},{..., dimensions={0}, use_global_device_ids=true | all-gather | bytes 12288 | tf_op jit(solution)/shard_map/all_gather | solution.py:496
  53.7 3.3 %first_product.1 = (f32[32,16,128]{2,1,0:T(8,128)}, f32[1,1024]{1,0:T(1,128)S(1)}, f32[16,128]{1,0:T(8,128)S(1)}) custom-call(s32[1]{0:T(128)} %bitcast.1.core, f32[2,8,128]{2,1,0:T(8,128)S(1)} %bitcast.20, bf16[256,1024]{1,0:T(8,128)(2,1)S(1)} %get-tuple-element.50.kept, bf16[9216,1024]{1,0:T(8,128)(2,1)} %get-tuple-element.51.rest, ...), custom_call_target="tpu_custom_call" | custom-call | flops 134217728 | bytes 4194304 | tf_op jit(solution)/shard_map/first_product/pallas_call | solution.py:504
  56.9 5.3 %all-to-all-start.2 = ((f32[32,16,128]{2,1,0:T(8,128)}), f32[32,16,128]{2,1,0:T(8,128)}, u32[]{:S(2)}, u32[]{:S(2)}) async-start(f32[32,16,128]{2,1,0:T(8,128)} %get-tuple-element.55), calls=%async_computation.2 | async-start | bytes 524288 | tf_op jit(solution)/shard_map/all_to_all | solution.py:515
  62.3 0.0 copy-start.1
  62.3 0.9 copy-done.1
  63.2 0.0 copy-start
  63.2 6.0 %node_features_a.1.rest_0_ = bf16[4608,2048]{1,0:T(8,128)(2,1)} custom-call(s32[1]{0:T(128)} %bitcast.1.core, bf16[1024,128]{1,0:T(8,128)(2,1)S(1)} %bitcast.19, bf16[2,8,136,128]{3,2,1,0:T(8,128)(2,1)S(1)} %bitcast.16), custom_call_target="tpu_custom_call" | custom-call | flops 578813952 | bytes 4194304 | tf_op jit(solution)/shard_map/node_features_a/pallas_call | solution.py:207
  69.2 6.0 %all-to-all-done.2.arrived = f32[32,16,128]{2,1,0:T(8,128)} async-done(((f32[32,16,128]{2,1,0:T(8,128)}), f32[32,16,128]{2,1,0:T(8,128)}, u32[]{:S(2)}, u32[]{:S(2)}) %all-to-all-start.2) | async-done | bytes 262176 | tf_op jit(solution)/shard_map/all_to_all | solution.py:515
  75.2 3.5 %second_product.1 = (f32[32,16,128]{2,1,0:T(8,128)S(1)}, f32[2,1024]{1,0:T(2,128)S(1)}, f32[16,128]{1,0:T(8,128)S(1)}, f32[16,128]{1,0:T(8,128)S(1)}, f32[16,128]{1,0:T(8,128)S(1)}) custom-call(f32[32,16,128]{2,1,0:T(8,128)} %all-to-all-done.2.arrived, f32[16,128]{1,0:T(8,128)S(1)} %get-tuple-element.58.rhs, f32[1,1024]{1,0:T(1,128)S(1)} %get-tuple-element.59.before, ...), custom_call_target="tpu_custom_call" | custom-call | flops 134217728 | bytes 4194304 | tf_op jit(solution)/shard_map/second_product/pallas_call | solution.py:519
  78.8 0.0 copy-start.3
  78.8 0.7 copy-done.3
  79.5 5.2 %all-to-all-start.3 = ((f32[32,16,128]{2,1,0:T(8,128)}), f32[32,16,128]{2,1,0:T(8,128)}, u32[]{:S(2)}, u32[]{:S(2)}) async-start(f32[32,16,128]{2,1,0:T(8,128)} %copy-done.3), calls=%async_computation.3 | async-start | bytes 524288 | tf_op jit(solution)/shard_map/all_to_all | solution.py:530
  84.7 0.0 copy-done
  84.7 0.0 copy-start.4
  84.7 0.0 copy-start.5
  84.7 6.0 %node_features_b.1.phi = bf16[4608,2048]{1,0:T(8,128)(2,1)} custom-call(s32[1]{0:T(128)} %bitcast.1.core, bf16[1024,128]{1,0:T(8,128)(2,1)S(1)} %bitcast.18, bf16[2,8,136,128]{3,2,1,0:T(8,128)(2,1)S(1)} %bitcast.17, bf16[4608,2048]{1,0:T(8,128)(2,1)} %node_features_a.1.rest_0_), custom_call_target="tpu_custom_call", output_to_operand_aliasing={{}: (3, {})} | custom-call | flops 578813952 | bytes 4194304 | tf_op jit(solution)/shard_map/node_features_b/pallas_call | solution.py:207
  90.7 5.2 %all-to-all-done.3.arrived = f32[32,16,128]{2,1,0:T(8,128)} async-done(((f32[32,16,128]{2,1,0:T(8,128)}), f32[32,16,128]{2,1,0:T(8,128)}, u32[]{:S(2)}, u32[]{:S(2)}) %all-to-all-start.3) | async-done | bytes 262176 | tf_op jit(solution)/shard_map/all_to_all | solution.py:530
  95.9 0.0 copy-done.4
  95.9 0.0 copy-done.5
  96.0 0.0 copy-start.6
  96.0 0.0 copy-start.7
  96.0 4.2 %third_product.1 = (f32[32,4,128]{2,1,0:T(4,128)}, f32[2,16,128]{2,1,0:T(8,128)S(1)}, f32[8,128]{1,0:T(8,128)S(1)}) custom-call(f32[32,16,128]{2,1,0:T(8,128)} %all-to-all-done.3.arrived, f32[16,128]{1,0:T(8,128)S(1)} %get-tuple-element.66.solution, f32[16,128]{1,0:T(8,128)S(1)} %get-tuple-element.67.residual, f32[16,128]{1,0:T(8,128)S(1)} %get-tuple-element.68.direction, ...), custom_call_target="tpu_custom_call" | custom-call | flops 134217728 | bytes 4194304 | tf_op jit(solution)/shard_map/third_product/pallas_call | solution.py:534
  100.2 4.8 %all-to-all-start.4 = ((f32[32,4,128]{2,1,0:T(4,128)}), f32[32,4,128]{2,1,0:T(4,128)S(1)}, u32[]{:S(2)}, u32[]{:S(2)}) async-start(f32[32,4,128]{2,1,0:T(4,128)} %get-tuple-element.72), calls=%async_computation.4 | async-start | bytes 131072 | tf_op jit(solution)/shard_map/all_to_all | solution.py:549
  105.0 5.4 %node_values.1 = f32[2,2048]{1,0:T(2,128)S(1)} custom-call(f32[2,16,128]{2,1,0:T(8,128)S(1)} %get-tuple-element.73.both, bf16[4608,2048]{1,0:T(8,128)(2,1)} %node_features_b.1.phi), custom_call_target="tpu_custom_call" | custom-call | flops 268435456 | bytes 8388608 | tf_op jit(solution)/shard_map/node_values/pallas_call | solution.py:550
  110.4 3.5 %all-to-all-done.4.arrived = f32[32,4,128]{2,1,0:T(4,128)S(1)} async-done(((f32[32,4,128]{2,1,0:T(4,128)}), f32[32,4,128]{2,1,0:T(4,128)S(1)}, u32[]{:S(2)}, u32[]{:S(2)}) %all-to-all-start.4) | async-done | bytes 65568 | tf_op jit(solution)/shard_map/all_to_all | solution.py:549
  113.9 0.0 copy-done.6
  113.9 0.0 copy-done.7
  113.9 0.7 last.1
  (2 shorter events, 0.0 us)
Async XLA Ops:
  2.2 22.6 %all-to-all-start = ((bf16[8,136,128]{2,1,0:T(8,128)(2,1)}), bf16[8,136,128]{2,1,0:T(8,128)(2,1)S(1)}, u32[]{:S(2)}, u32[]{:S(2)}) async-start(bf16[8,136,128]{2,1,0:T(8,128)(2,1)} %pack.1), calls=%async_computation | async-start | bytes 557056 | tf_op jit(solution)/shard_map/all_to_all | solution.py:462
  12.5 0.9 copy-start.2
  30.8 20.2 %all-to-all-start.1 = ((f32[32,8,128]{2,1,0:T(8,128)}), f32[32,8,128]{2,1,0:T(8,128)}, u32[]{:S(2)}, u32[]{:S(2)}) async-start(f32[32,8,128]{2,1,0:T(8,128)} %get-tuple-element.47), calls=%async_computation.1 | async-start | bytes 262144 | tf_op jit(solution)/shard_map/all_to_all | solution.py:492
  56.9 18.3 %all-to-all-start.2 = ((f32[32,16,128]{2,1,0:T(8,128)}), f32[32,16,128]{2,1,0:T(8,128)}, u32[]{:S(2)}, u32[]{:S(2)}) async-start(f32[32,16,128]{2,1,0:T(8,128)} %get-tuple-element.55), calls=%async_computation.2 | async-start | bytes 524288 | tf_op jit(solution)/shard_map/all_to_all | solution.py:515
  62.3 1.0 copy-start.1
  63.2 21.4 %copy-start = (bf16[8,128,128]{2,1,0:T(8,128)(2,1)S(1)}, bf16[8,128,128]{2,1,0:T(8,128)(2,1)}, u32[]{:S(2)}) copy-start(bf16[8,128,128]{2,1,0:T(8,128)(2,1)} %copy.16) | copy-start | bytes 786436
  78.8 0.7 copy-start.3
  79.5 16.5 %all-to-all-start.3 = ((f32[32,16,128]{2,1,0:T(8,128)}), f32[32,16,128]{2,1,0:T(8,128)}, u32[]{:S(2)}, u32[]{:S(2)}) async-start(f32[32,16,128]{2,1,0:T(8,128)} %copy-done.3), calls=%async_computation.3 | async-start | bytes 524288 | tf_op jit(solution)/shard_map/all_to_all | solution.py:530
  84.7 11.3 %copy-start.4 = (s32[1024,1]{0,1:T(1,128)S(1)}, s32[1024,1]{0,1:T(1,128)}, u32[]{:S(2)}) copy-start(s32[1024,1]{0,1:T(1,128)} %param.13) | copy-start | bytes 12292
  84.7 11.3 %copy-start.5 = (s32[1024]{0:T(1024)S(1)}, s32[1024]{0:T(1024)}, u32[]{:S(2)}) copy-start(s32[1024]{0:T(1024)} %param.14) | copy-start | bytes 12292
  96.0 17.9 %copy-start.6 = (f32[128]{0:T(128)S(1)}, f32[128]{0:T(128)}, u32[]{:S(2)}) copy-start(f32[128]{0:T(128)} %param.18) | copy-start | bytes 1540
  96.0 17.9 %copy-start.7 = (s32[128]{0:T(128)S(1)}, s32[128]{0:T(128)}, u32[]{:S(2)}) copy-start(s32[128]{0:T(128)} %param.19) | copy-start | bytes 1540
  100.2 13.7 %all-to-all-start.4 = ((f32[32,4,128]{2,1,0:T(4,128)}), f32[32,4,128]{2,1,0:T(4,128)S(1)}, u32[]{:S(2)}, u32[]{:S(2)}) async-start(f32[32,4,128]{2,1,0:T(4,128)} %get-tuple-element.72), calls=%async_computation.4 | async-start | bytes 131072 | tf_op jit(solution)/shard_map/all_to_all | solution.py:549

commit v4 on v3

--- a/solution.py
+++ b/solution.py
@@ -70,7 +70,7 @@
 SMEM = pl.BlockSpec(memory_space=pltpu.SMEM)
 HBM = pl.BlockSpec(memory_space=pltpu.HBM)
 PARTS = 2
-KEPT = 0.25
+KEPT = 0.5
 SPARE = 9
 PHASE_ROWS = 8
 
@@ -221,7 +221,7 @@
 
 
 def near_kernel(
-    core, cov, freq, weight, size, kept, rest_out, out, rest, gathered, tiles, sems
+    cov, freq, weight, size, kept, rest_out, out, rest, gathered, tiles, sems
 ):
     first = kept.shape[0]
 
@@ -235,7 +235,7 @@
                 target[at, column : column + value.shape[1]] = value
 
             rows = cov[pl.ds(pl.multiple_of(base + i * group, 64), group), :]
-            feature_block(rows, freq.at[core[0]], store)
+            feature_block(rows, freq, store)
             if after is not None:
                 after(i, group).start()
             return carry
@@ -303,10 +303,10 @@
 
 
 def first_kernel(
-    scale, core, halves, kept, rest, far, weight, out, values_out, rhs_out, gathered, tiles, held, sems
+    scale, rhs_scale, core, halves, kept, rest, far, weight, out, values_out, rhs_out, gathered, tiles, held, sems
 ):
     copies = fetch(rest, held, sems)
-    low, high = halves[0], halves[1]
+    low, high = (jnp.sum(halves[h], axis=0) * rhs_scale for h in range(2))
     swap = core[0] == 1
     half = low.shape[0]
     rhs_out[0:half, :] = jnp.where(swap, high, low)
@@ -466,13 +466,12 @@
     height = (SPARE * nodes * patients) // 4
     node_covs = (by_node[:count], by_node[count:])
     near_freq, cov, node_covs = together((near_freq, cov, node_covs))
-    freq = lax.all_gather(near_freq, "col", axis_index_groups=pairs)
 
     half = inducing // 2
     first = int(rows * KEPT)
     kept, rest, sent = pl.pallas_call(
         near_kernel,
-        in_specs=[SMEM] + [VMEM] * 4,
+        in_specs=[VMEM] * 4,
         out_specs=[VMEM, HBM, VMEM],
         out_shape=[
             jax.ShapeDtypeStruct((first, half), BF16),
@@ -487,13 +486,13 @@
         ],
         compiler_params=params(),
         name="near_features",
-    )(core, cov, freq, weight, size)
-    sent, late_freq = together((sent, freq))
+    )(cov, near_freq, weight, size)
+    sent, late_freq = together((sent, near_freq))
     arrived = lax.all_to_all(sent, "blk", 0, 0, tiled=True)
-    far = far_features(core, cov, late_freq)
+    freq = lax.all_gather(late_freq, "col", axis_index_groups=pairs)
+    far = far_features(core, cov, freq)
     arrived, far = together((arrived, far))
-    rhs = jnp.sum(arrived, axis=0) * (1.0 / math.sqrt(rows * blocks))
-    halves = lax.all_gather(rhs, "col", axis_index_groups=pairs)
+    halves = lax.all_gather(arrived, "col", axis_index_groups=pairs)
 
     message = jax.ShapeDtypeStruct((blocks, tall, LANES), F32)
     vector = jax.ShapeDtypeStruct((tall, LANES), F32)
@@ -502,7 +501,7 @@
     work = cost(64 * rows * inducing, 2 * rows * inducing)
 
     sent, before, rhs = pl.pallas_call(
-        functools.partial(first_kernel, scale),
+        functools.partial(first_kernel, scale, 1.0 / math.sqrt(rows * blocks)),
         in_specs=[SMEM, VMEM, VMEM, HBM, VMEM, VMEM],
         out_specs=[VMEM] * 3,
         out_shape=[message, jax.ShapeDtypeStruct((1, rows), F32), vector],

time: 116 us -> 113 us (0.974)
  waiting for transfers between devices: 29.3 us -> 24.1 us
  local copies, waits for them, and re-layouts: 6.53 us -> 9.46 us
    all_to_all x4, waiting for transfers between devices: 21.9 us -> 16.8 us  [on_device(): arrived = lax.all_to_all(sent, 'blk', 0, 0, tiled=True)]
    unnamed x16 -> x22, local copies, waits for them, and re-layouts: 2.61 us -> 5.51 us
  transfers between devices with their start and end apart: 5 -> 5, of which waited for: 5 -> 5; matrix products, arithmetic and copies ran while one was open for 3% -> 4% of each run, Pallas kernels for 18% -> 18%
where the time goes in v4:
time: 113 us; the launch traced here: 112 us
  starting transfers between devices  36.9 us (33%)
  Pallas kernels  36.7 us (32%)
  waiting for transfers between devices  24.1 us (21%)
  local copies, waits for them, and re-layouts  9.46 us (8%)
  blocking collectives  4.19 us (4%)
    all_to_all x4, starting transfers between devices, on_device(): arrived = lax.all_to_all(sent, 'blk', 0, 0, tiled=True)  26.5 us
    all_to_all x4, waiting for transfers between devices, on_device(): arrived = lax.all_to_all(sent, 'blk', 0, 0, tiled=True)  16.8 us
    pallas_call x2, Pallas kernels, node_features(): pl.pallas_call(functools.partial(node_kernel, first), in_specs=[SMEM, VME...  12 us
    all_to_all x1, starting transfers between devices, on_device(): lax.all_to_all(packed, 'col', 0, 0, tiled=True, axis_index_groups=same_core)  10.3 us
    all_to_all x1, waiting for transfers between devices, on_device(): lax.all_to_all(packed, 'col', 0, 0, tiled=True, axis_index_groups=same_core)  7.3 us
    unnamed x22, local copies, waits for them, and re-layouts  5.51 us
    pallas_call x1, Pallas kernels, on_device(): pl.pallas_call(nodes_kernel, grid=(2 * count // NODE_ROWS,), in_specs=[pl...  5.4 us
    pallas_call x1, Pallas kernels, on_device(): pl.pallas_call(functools.partial(third_kernel, scale, fit_scale), in_spec...  3.88 us
  transfers between devices with their start and end apart: 5, of which 5 were waited for; matrix products, arithmetic and copies ran while one was open for 4% of the time, Pallas kernels for 18%

profile of v4, /device:TPU:8, one launch (start us, length us, event | category | flops | bytes accessed | tf_op | source)
XLA Modules:
  0.0 112.1 jit_solution(1987918846452112005)
XLA Ops:
  0.6 1.6 %pack.1 = bf16[8,136,128]{2,1,0:T(8,128)(2,1)} custom-call(bf16[128,128]{1,0:T(8,128)(2,1)} %freq.1, bf16[1,128]{1,0:T(2,128)(2,1)} %bitcast.25), custom_call_target="tpu_custom_call" | custom-call | tf_op jit(solution)/shard_map/pack/pallas_call | solution.py:448
  2.2 10.3 %all-to-all-start = ((bf16[8,136,128]{2,1,0:T(8,128)(2,1)}), bf16[8,136,128]{2,1,0:T(8,128)(2,1)S(1)}, u32[]{:S(2)}, u32[]{:S(2)}) async-start(bf16[8,136,128]{2,1,0:T(8,128)(2,1)} %pack.1), calls=%async_computation | async-start | bytes 557056 | tf_op jit(solution)/shard_map/all_to_all | solution.py:462
  12.5 0.0 copy-start.5
  12.5 0.9 copy-done.5
  13.5 0.7 reshape.43.weight
  14.2 0.7 reshape.44.size
  14.9 1.1 fusion
  15.9 0.8 copy.16
  16.7 0.8 copy.15
  17.4 7.3 %all-to-all-done.freq = bf16[8,136,128]{2,1,0:T(8,128)(2,1)S(1)} async-done(((bf16[8,136,128]{2,1,0:T(8,128)(2,1)}), bf16[8,136,128]{2,1,0:T(8,128)(2,1)S(1)}, u32[]{:S(2)}, u32[]{:S(2)}) %all-to-all-start) | async-done | bytes 278560 | tf_op jit(solution)/shard_map/all_to_all | solution.py:462
  24.7 3.8 %near_features.1 = (bf16[512,1024]{1,0:T(8,128)(2,1)S(1)}, bf16[9216,1024]{1,0:T(8,128)(2,1)}, f32[32,8,128]{2,1,0:T(8,128)}) custom-call(bf16[1024,128]{1,0:T(8,128)(2,1)S(1)} %stage_cov.1.cov, bf16[8,136,128]{2,1,0:T(8,128)(2,1)S(1)} %all-to-all-done.freq, bf16[1,1024]{1,0:T(2,128)(2,1)S(1)} %reshape.43.weight, bf16[1,1024]{1,0:T(2,128)(2,1)S(1)} %reshape.44.size), custom_call_target="tpu_custom_call" | custom-call | tf_op jit(solution)/shard_map/near_features/pallas_call | solution.py:472
  28.6 10.2 %all-to-all-start.1 = ((f32[32,8,128]{2,1,0:T(8,128)}), f32[32,8,128]{2,1,0:T(8,128)S(1)}, u32[]{:S(2)}, u32[]{:S(2)}) async-start(f32[32,8,128]{2,1,0:T(8,128)} %get-tuple-element.47), calls=%async_computation.1 | async-start | bytes 262144 | tf_op jit(solution)/shard_map/all_to_all | solution.py:491
  38.8 2.2 %all-gather = bf16[16,136,128]{2,1,0:T(8,128)(2,1)S(1)} all-gather(bf16[8,136,128]{2,1,0:T(8,128)(2,1)S(1)} %all-to-all-done.freq), channel_id=2, replica_groups={{0,1},{2,3},{4,5},{6,7},{8,9},{10,11},{12,13},{14,15},{16,17},{18,19},{..., dimensions={0}, use_global_device_ids=true | all-gather | bytes 835584 | tf_op jit(solution)/shard_map/all_gather | solution.py:492
  41.0 2.7 %far_features.1.far = bf16[1024,1024]{1,0:T(8,128)(2,1)S(1)} custom-call(s32[1]{0:T(128)} %bitcast.1.core, bf16[1024,128]{1,0:T(8,128)(2,1)S(1)} %stage_cov.1.cov, bf16[2,8,136,128]{3,2,1,0:T(8,128)(2,1)S(1)} %bitcast.14), custom_call_target="tpu_custom_call" | custom-call | flops 289406976 | bytes 2097152 | tf_op jit(solution)/shard_map/far_features/pallas_call | solution.py:166
  43.7 0.0 copy-start
  43.7 0.8 copy-done
  44.5 3.8 %all-to-all-done.1 = f32[32,8,128]{2,1,0:T(8,128)S(1)} async-done(((f32[32,8,128]{2,1,0:T(8,128)}), f32[32,8,128]{2,1,0:T(8,128)S(1)}, u32[]{:S(2)}, u32[]{:S(2)}) %all-to-all-start.1) | async-done | bytes 131104 | tf_op jit(solution)/shard_map/all_to_all | solution.py:491
  48.3 2.0 %all-gather.1 = f32[64,8,128]{2,1,0:T(8,128)S(1)} all-gather(f32[32,8,128]{2,1,0:T(8,128)S(1)} %all-to-all-done.1), channel_id=3, replica_groups={{0,1},{2,3},{4,5},{6,7},{8,9},{10,11},{12,13},{14,15},{16,17},{18,19},{..., dimensions={0}, use_global_device_ids=true | all-gather | bytes 393216 | tf_op jit(solution)/shard_map/all_gather | solution.py:495
  50.3 3.2 %first_product.1 = (f32[32,16,128]{2,1,0:T(8,128)}, f32[1,1024]{1,0:T(1,128)S(1)}, f32[16,128]{1,0:T(8,128)S(1)}) custom-call(s32[1]{0:T(128)} %bitcast.1.core, f32[2,32,8,128]{3,2,1,0:T(8,128)S(1)} %bitcast.19, bf16[512,1024]{1,0:T(8,128)(2,1)S(1)} %get-tuple-element.50.kept, bf16[9216,1024]{1,0:T(8,128)(2,1)} %get-tuple-element.51.rest, ...), custom_call_target="tpu_custom_call" | custom-call | flops 134217728 | bytes 4194304 | tf_op jit(solution)/shard_map/first_product/pallas_call | solution.py:503
  53.5 6.1 %all-to-all-start.2 = ((f32[32,16,128]{2,1,0:T(8,128)}), f32[32,16,128]{2,1,0:T(8,128)}, u32[]{:S(2)}, u32[]{:S(2)}) async-start(f32[32,16,128]{2,1,0:T(8,128)} %get-tuple-element.55), calls=%async_computation.2 | async-start | bytes 524288 | tf_op jit(solution)/shard_map/all_to_all | solution.py:514
  59.5 0.0 copy-start.1
  59.5 1.0 copy-done.1
  60.6 0.0 copy-start.4
  60.6 0.9 copy-done.4
  61.5 0.0 copy-start.3
  61.5 6.0 %node_features_a.1.rest_0_ = bf16[4608,2048]{1,0:T(8,128)(2,1)} custom-call(s32[1]{0:T(128)} %bitcast.1.core, bf16[1024,128]{1,0:T(8,128)(2,1)S(1)} %bitcast.18, bf16[2,8,136,128]{3,2,1,0:T(8,128)(2,1)S(1)} %bitcast.15), custom_call_target="tpu_custom_call" | custom-call | flops 578813952 | bytes 4194304 | tf_op jit(solution)/shard_map/node_features_a/pallas_call | solution.py:207
  67.5 4.5 %all-to-all-done.2.arrived = f32[32,16,128]{2,1,0:T(8,128)} async-done(((f32[32,16,128]{2,1,0:T(8,128)}), f32[32,16,128]{2,1,0:T(8,128)}, u32[]{:S(2)}, u32[]{:S(2)}) %all-to-all-start.2) | async-done | bytes 262176 | tf_op jit(solution)/shard_map/all_to_all | solution.py:514
  72.1 3.5 %second_product.1 = (f32[32,16,128]{2,1,0:T(8,128)S(1)}, f32[2,1024]{1,0:T(2,128)S(1)}, f32[16,128]{1,0:T(8,128)S(1)}, f32[16,128]{1,0:T(8,128)S(1)}, f32[16,128]{1,0:T(8,128)S(1)}) custom-call(f32[32,16,128]{2,1,0:T(8,128)} %all-to-all-done.2.arrived, f32[16,128]{1,0:T(8,128)S(1)} %get-tuple-element.58.rhs, f32[1,1024]{1,0:T(1,128)S(1)} %get-tuple-element.59.before, ...), custom_call_target="tpu_custom_call" | custom-call | flops 134217728 | bytes 4194304 | tf_op jit(solution)/shard_map/second_product/pallas_call | solution.py:518
  75.5 0.0 copy-start.6
  75.5 0.7 copy-done.6
  76.2 5.3 %all-to-all-start.3 = ((f32[32,16,128]{2,1,0:T(8,128)}), f32[32,16,128]{2,1,0:T(8,128)}, u32[]{:S(2)}, u32[]{:S(2)}) async-start(f32[32,16,128]{2,1,0:T(8,128)} %copy-done.6), calls=%async_computation.3 | async-start | bytes 524288 | tf_op jit(solution)/shard_map/all_to_all | solution.py:529
  81.5 0.0 copy-done.3
  81.6 0.0 copy-start.2
  81.6 1.0 copy-done.2
  82.6 0.0 copy-start.7
  82.6 0.0 copy-start.8
  82.6 6.0 %node_features_b.1.phi = bf16[4608,2048]{1,0:T(8,128)(2,1)} custom-call(s32[1]{0:T(128)} %bitcast.1.core, bf16[1024,128]{1,0:T(8,128)(2,1)S(1)} %bitcast.17, bf16[2,8,136,128]{3,2,1,0:T(8,128)(2,1)S(1)} %bitcast.16, bf16[4608,2048]{1,0:T(8,128)(2,1)} %node_features_a.1.rest_0_), custom_call_target="tpu_custom_call", output_to_operand_aliasing={{}: (3, {})} | custom-call | flops 578813952 | bytes 4194304 | tf_op jit(solution)/shard_map/node_features_b/pallas_call | solution.py:207
  88.6 4.8 %all-to-all-done.3.arrived = f32[32,16,128]{2,1,0:T(8,128)} async-done(((f32[32,16,128]{2,1,0:T(8,128)}), f32[32,16,128]{2,1,0:T(8,128)}, u32[]{:S(2)}, u32[]{:S(2)}) %all-to-all-start.3) | async-done | bytes 262176 | tf_op jit(solution)/shard_map/all_to_all | solution.py:529
  93.5 0.0 copy-done.7
  93.5 0.0 copy-done.8
  93.5 0.0 copy-start.9
  93.5 0.0 copy-start.10
  93.5 3.9 %third_product.1 = (f32[32,4,128]{2,1,0:T(4,128)}, f32[2,16,128]{2,1,0:T(8,128)S(1)}, f32[8,128]{1,0:T(8,128)S(1)}) custom-call(f32[32,16,128]{2,1,0:T(8,128)} %all-to-all-done.3.arrived, f32[16,128]{1,0:T(8,128)S(1)} %get-tuple-element.66.solution, f32[16,128]{1,0:T(8,128)S(1)} %get-tuple-element.67.residual, f32[16,128]{1,0:T(8,128)S(1)} %get-tuple-element.68.direction, ...), custom_call_target="tpu_custom_call" | custom-call | flops 134217728 | bytes 4194304 | tf_op jit(solution)/shard_map/third_product/pallas_call | solution.py:533
  97.4 5.0 %all-to-all-start.4 = ((f32[32,4,128]{2,1,0:T(4,128)}), f32[32,4,128]{2,1,0:T(4,128)S(1)}, u32[]{:S(2)}, u32[]{:S(2)}) async-start(f32[32,4,128]{2,1,0:T(4,128)} %get-tuple-element.72), calls=%async_computation.4 | async-start | bytes 131072 | tf_op jit(solution)/shard_map/all_to_all | solution.py:548
  102.4 5.4 %node_values.1 = f32[2,2048]{1,0:T(2,128)S(1)} custom-call(f32[2,16,128]{2,1,0:T(8,128)S(1)} %get-tuple-element.73.both, bf16[4608,2048]{1,0:T(8,128)(2,1)} %node_features_b.1.phi), custom_call_target="tpu_custom_call" | custom-call | flops 268435456 | bytes 8388608 | tf_op jit(solution)/shard_map/node_values/pallas_call | solution.py:549
  107.8 3.6 %all-to-all-done.4.arrived = f32[32,4,128]{2,1,0:T(4,128)S(1)} async-done(((f32[32,4,128]{2,1,0:T(4,128)}), f32[32,4,128]{2,1,0:T(4,128)S(1)}, u32[]{:S(2)}, u32[]{:S(2)}) %all-to-all-start.4) | async-done | bytes 65568 | tf_op jit(solution)/shard_map/all_to_all | solution.py:548
  111.4 0.0 copy-done.9
  111.4 0.0 copy-done.10
  111.4 0.7 last.1
  (1 shorter events, 0.0 us)
Async XLA Ops:
  2.2 22.6 %all-to-all-start = ((bf16[8,136,128]{2,1,0:T(8,128)(2,1)}), bf16[8,136,128]{2,1,0:T(8,128)(2,1)S(1)}, u32[]{:S(2)}, u32[]{:S(2)}) async-start(bf16[8,136,128]{2,1,0:T(8,128)(2,1)} %pack.1), calls=%async_computation | async-start | bytes 557056 | tf_op jit(solution)/shard_map/all_to_all | solution.py:462
  12.5 0.9 copy-start.5
  28.6 19.7 %all-to-all-start.1 = ((f32[32,8,128]{2,1,0:T(8,128)}), f32[32,8,128]{2,1,0:T(8,128)S(1)}, u32[]{:S(2)}, u32[]{:S(2)}) async-start(f32[32,8,128]{2,1,0:T(8,128)} %get-tuple-element.47), calls=%async_computation.1 | async-start | bytes 262144 | tf_op jit(solution)/shard_map/all_to_all | solution.py:491
  43.7 0.8 copy-start
  53.5 18.6 %all-to-all-start.2 = ((f32[32,16,128]{2,1,0:T(8,128)}), f32[32,16,128]{2,1,0:T(8,128)}, u32[]{:S(2)}, u32[]{:S(2)}) async-start(f32[32,16,128]{2,1,0:T(8,128)} %get-tuple-element.55), calls=%async_computation.2 | async-start | bytes 524288 | tf_op jit(solution)/shard_map/all_to_all | solution.py:514
  59.5 1.1 copy-start.1
  60.6 0.9 copy-start.4
  61.5 20.0 %copy-start.3 = (bf16[8,128,128]{2,1,0:T(8,128)(2,1)S(1)}, bf16[8,128,128]{2,1,0:T(8,128)(2,1)}, u32[]{:S(2)}) copy-start(bf16[8,128,128]{2,1,0:T(8,128)(2,1)} %copy.16) | copy-start | bytes 786436
  75.5 0.7 copy-start.6
  76.2 17.2 %all-to-all-start.3 = ((f32[32,16,128]{2,1,0:T(8,128)}), f32[32,16,128]{2,1,0:T(8,128)}, u32[]{:S(2)}, u32[]{:S(2)}) async-start(f32[32,16,128]{2,1,0:T(8,128)} %copy-done.6), calls=%async_computation.3 | async-start | bytes 524288 | tf_op jit(solution)/shard_map/all_to_all | solution.py:529
  81.6 1.1 copy-start.2
  82.6 10.8 %copy-start.7 = (s32[1024,1]{0,1:T(1,128)S(1)}, s32[1024,1]{0,1:T(1,128)}, u32[]{:S(2)}) copy-start(s32[1024,1]{0,1:T(1,128)} %param.13) | copy-start | bytes 12292
  82.6 10.8 %copy-start.8 = (s32[1024]{0:T(1024)S(1)}, s32[1024]{0:T(1024)}, u32[]{:S(2)}) copy-start(s32[1024]{0:T(1024)} %param.14) | copy-start | bytes 12292
  93.5 17.9 %copy-start.9 = (f32[128]{0:T(128)S(1)}, f32[128]{0:T(128)}, u32[]{:S(2)}) copy-start(f32[128]{0:T(128)} %param.18) | copy-start | bytes 1540
  93.5 17.9 %copy-start.10 = (s32[128]{0:T(128)S(1)}, s32[128]{0:T(128)}, u32[]{:S(2)}) copy-start(s32[128]{0:T(128)} %param.19) | copy-start | bytes 1540
  97.4 14.0 %all-to-all-start.4 = ((f32[32,4,128]{2,1,0:T(4,128)}), f32[32,4,128]{2,1,0:T(4,128)S(1)}, u32[]{:S(2)}, u32[]{:S(2)}) async-start(f32[32,4,128]{2,1,0:T(4,128)} %get-tuple-element.72), calls=%async_computation.4 | async-start | bytes 131072 | tf_op jit(solution)/shard_map/all_to_all | solution.py:548

commit v5 on v4

--- a/solution.py
+++ b/solution.py
@@ -214,7 +214,7 @@
             pltpu.SemaphoreType.DMA((rows // FEATURE_ROWS,)),
         ],
         input_output_aliases={3: 0} if earlier else {},
-        compiler_params=params(),
+        compiler_params=params(60),
         cost_estimate=cost(2 * rows * depth * columns + 20 * rows * columns, 2 * rows * columns),
         name=name,
     )(core, cov, freq, *earlier)

time: 113 us -> 111 us (0.982)
  local copies, waits for them, and re-layouts: 9.46 us -> 7.06 us
    unnamed x22 -> x16, local copies, waits for them, and re-layouts: 5.51 us -> 3.13 us
    pallas_call x2, Pallas kernels: 12 us -> 14.3 us  [node_features(): pl.pallas_call(functools.partial(node_kernel, first), in_specs=[SMEM, VME...]
  transfers between devices with their start and end apart: 5 -> 5, of which waited for: 5 -> 5; matrix products, arithmetic and copies ran while one was open for 4% -> 4% of each run, Pallas kernels for 18% -> 20%
where the time goes in v5:
time: 111 us; the launch traced here: 110 us
  Pallas kernels  36.4 us (33%)
  starting transfers between devices  36.4 us (33%)
  waiting for transfers between devices  24.7 us (22%)
  local copies, waits for them, and re-layouts  7.06 us (6%)
  blocking collectives  4.4 us (4%)
    all_to_all x4, starting transfers between devices, on_device(): arrived = lax.all_to_all(sent, 'blk', 0, 0, tiled=True)  26 us
    all_to_all x4, waiting for transfers between devices, on_device(): arrived = lax.all_to_all(sent, 'blk', 0, 0, tiled=True)  17.4 us
    pallas_call x2, Pallas kernels, node_features(): pl.pallas_call(functools.partial(node_kernel, first), in_specs=[SMEM, VME...  14.3 us
    all_to_all x1, starting transfers between devices, on_device(): lax.all_to_all(packed, 'col', 0, 0, tiled=True, axis_index_groups=same_core)  10.3 us
    all_to_all x1, waiting for transfers between devices, on_device(): lax.all_to_all(packed, 'col', 0, 0, tiled=True, axis_index_groups=same_core)  7.33 us
    pallas_call x1, Pallas kernels, on_device(): pl.pallas_call(nodes_kernel, grid=(2 * count // NODE_ROWS,), in_specs=[pl...  5.4 us
    pallas_call x1, Pallas kernels, on_device(): pl.pallas_call(near_kernel, in_specs=[VMEM] * 4, out_specs=[VMEM, HBM, VM...  3.8 us
    unnamed x16, local copies, waits for them, and re-layouts  3.13 us
  transfers between devices with their start and end apart: 5, of which 5 were waited for; matrix products, arithmetic and copies ran while one was open for 4% of the time, Pallas kernels for 20%

profile of v5, /device:TPU:8, one launch (start us, length us, event | category | flops | bytes accessed | tf_op | source)
XLA Modules:
  0.0 109.7 jit_solution(3271551957935275946)
XLA Ops:
  0.6 1.6 %pack.1 = bf16[8,136,128]{2,1,0:T(8,128)(2,1)} custom-call(bf16[128,128]{1,0:T(8,128)(2,1)} %freq.1, bf16[1,128]{1,0:T(2,128)(2,1)} %bitcast.25), custom_call_target="tpu_custom_call" | custom-call | tf_op jit(solution)/shard_map/pack/pallas_call | solution.py:448
  2.2 10.3 %all-to-all-start = ((bf16[8,136,128]{2,1,0:T(8,128)(2,1)}), bf16[8,136,128]{2,1,0:T(8,128)(2,1)S(1)}, u32[]{:S(2)}, u32[]{:S(2)}) async-start(bf16[8,136,128]{2,1,0:T(8,128)(2,1)} %pack.1), calls=%async_computation | async-start | bytes 557056 | tf_op jit(solution)/shard_map/all_to_all | solution.py:462
  12.5 0.0 copy-start.1
  12.5 0.9 copy-done.1
  13.5 0.7 reshape.43.weight
  14.2 0.7 reshape.44.size
  14.9 1.1 fusion
  15.9 0.8 copy.16
  16.7 0.7 copy.15
  17.4 7.3 %all-to-all-done.freq = bf16[8,136,128]{2,1,0:T(8,128)(2,1)S(1)} async-done(((bf16[8,136,128]{2,1,0:T(8,128)(2,1)}), bf16[8,136,128]{2,1,0:T(8,128)(2,1)S(1)}, u32[]{:S(2)}, u32[]{:S(2)}) %all-to-all-start) | async-done | bytes 278560 | tf_op jit(solution)/shard_map/all_to_all | solution.py:462
  24.8 3.8 %near_features.1 = (bf16[512,1024]{1,0:T(8,128)(2,1)S(1)}, bf16[9216,1024]{1,0:T(8,128)(2,1)}, f32[32,8,128]{2,1,0:T(8,128)}) custom-call(bf16[1024,128]{1,0:T(8,128)(2,1)S(1)} %stage_cov.1.cov, bf16[8,136,128]{2,1,0:T(8,128)(2,1)S(1)} %all-to-all-done.freq, bf16[1,1024]{1,0:T(2,128)(2,1)S(1)} %reshape.43.weight, bf16[1,1024]{1,0:T(2,128)(2,1)S(1)} %reshape.44.size), custom_call_target="tpu_custom_call" | custom-call | tf_op jit(solution)/shard_map/near_features/pallas_call | solution.py:472
  28.6 10.2 %all-to-all-start.1 = ((f32[32,8,128]{2,1,0:T(8,128)}), f32[32,8,128]{2,1,0:T(8,128)}, u32[]{:S(2)}, u32[]{:S(2)}) async-start(f32[32,8,128]{2,1,0:T(8,128)} %get-tuple-element.47), calls=%async_computation.1 | async-start | bytes 262144 | tf_op jit(solution)/shard_map/all_to_all | solution.py:491
  38.8 2.2 %all-gather = bf16[16,136,128]{2,1,0:T(8,128)(2,1)S(1)} all-gather(bf16[8,136,128]{2,1,0:T(8,128)(2,1)S(1)} %all-to-all-done.freq), channel_id=2, replica_groups={{0,1},{2,3},{4,5},{6,7},{8,9},{10,11},{12,13},{14,15},{16,17},{18,19},{..., dimensions={0}, use_global_device_ids=true | all-gather | bytes 835584 | tf_op jit(solution)/shard_map/all_gather | solution.py:492
  41.0 2.7 %far_features.1.far = bf16[1024,1024]{1,0:T(8,128)(2,1)S(1)} custom-call(s32[1]{0:T(128)} %bitcast.1.core, bf16[1024,128]{1,0:T(8,128)(2,1)S(1)} %stage_cov.1.cov, bf16[2,8,136,128]{3,2,1,0:T(8,128)(2,1)S(1)} %bitcast.14), custom_call_target="tpu_custom_call" | custom-call | flops 289406976 | bytes 2097152 | tf_op jit(solution)/shard_map/far_features/pallas_call | solution.py:166
  43.8 0.0 copy-start
  43.8 0.8 copy-done
  44.6 3.9 %all-to-all-done.1 = f32[32,8,128]{2,1,0:T(8,128)} async-done(((f32[32,8,128]{2,1,0:T(8,128)}), f32[32,8,128]{2,1,0:T(8,128)}, u32[]{:S(2)}, u32[]{:S(2)}) %all-to-all-start.1) | async-done | bytes 131104 | tf_op jit(solution)/shard_map/all_to_all | solution.py:491
  48.5 2.2 %all-gather.1 = f32[64,8,128]{2,1,0:T(8,128)S(1)} all-gather(f32[32,8,128]{2,1,0:T(8,128)} %all-to-all-done.1), channel_id=3, replica_groups={{0,1},{2,3},{4,5},{6,7},{8,9},{10,11},{12,13},{14,15},{16,17},{18,19},{..., dimensions={0}, use_global_device_ids=true | all-gather | bytes 393216 | tf_op jit(solution)/shard_map/all_gather | solution.py:495
  50.6 2.5 %first_product.1 = (f32[32,16,128]{2,1,0:T(8,128)S(1)}, f32[1,1024]{1,0:T(1,128)S(1)}, f32[16,128]{1,0:T(8,128)S(1)}) custom-call(s32[1]{0:T(128)} %bitcast.1.core, f32[2,32,8,128]{3,2,1,0:T(8,128)S(1)} %bitcast.17, bf16[512,1024]{1,0:T(8,128)(2,1)S(1)} %get-tuple-element.50.kept, bf16[9216,1024]{1,0:T(8,128)(2,1)} %get-tuple-element.51.rest, ...), custom_call_target="tpu_custom_call" | custom-call | flops 134217728 | bytes 4194304 | tf_op jit(solution)/shard_map/first_product/pallas_call | solution.py:503
  53.1 0.0 copy-start.3
  53.2 0.7 copy-done.3
  53.9 5.9 %all-to-all-start.2 = ((f32[32,16,128]{2,1,0:T(8,128)}), f32[32,16,128]{2,1,0:T(8,128)S(1)}, u32[]{:S(2)}, u32[]{:S(2)}) async-start(f32[32,16,128]{2,1,0:T(8,128)} %copy-done.3), calls=%async_computation.2 | async-start | bytes 524288 | tf_op jit(solution)/shard_map/all_to_all | solution.py:514
  59.7 7.1 %node_features_a.1.rest_0_ = bf16[4608,2048]{1,0:T(8,128)(2,1)} custom-call(s32[1]{0:T(128)} %bitcast.1.core, bf16[1024,128]{1,0:T(8,128)(2,1)} %bitcast.23, bf16[2,8,136,128]{3,2,1,0:T(8,128)(2,1)} %bitcast.15), custom_call_target="tpu_custom_call" | custom-call | flops 578813952 | bytes 4194304 | tf_op jit(solution)/shard_map/node_features_a/pallas_call | solution.py:207
  66.9 5.4 %all-to-all-done.2.arrived = f32[32,16,128]{2,1,0:T(8,128)S(1)} async-done(((f32[32,16,128]{2,1,0:T(8,128)}), f32[32,16,128]{2,1,0:T(8,128)S(1)}, u32[]{:S(2)}, u32[]{:S(2)}) %all-to-all-start.2) | async-done | bytes 262176 | tf_op jit(solution)/shard_map/all_to_all | solution.py:514
  72.2 2.5 %second_product.1 = (f32[32,16,128]{2,1,0:T(8,128)S(1)}, f32[2,1024]{1,0:T(2,128)S(1)}, f32[16,128]{1,0:T(8,128)S(1)}, f32[16,128]{1,0:T(8,128)S(1)}, f32[16,128]{1,0:T(8,128)S(1)}) custom-call(f32[32,16,128]{2,1,0:T(8,128)S(1)} %all-to-all-done.2.arrived, f32[16,128]{1,0:T(8,128)S(1)} %get-tuple-element.58.rhs, f32[1,1024]{1,0:T(1,128)S(1)} %get-tuple-element.59.before, ...), custom_call_target="tpu_custom_call" | custom-call | flops 134217728 | bytes 4194304 | tf_op jit(solution)/shard_map/second_product/pallas_call | solution.py:518
  74.7 0.0 copy-start.2
  74.7 0.7 copy-done.2
  75.4 4.6 %all-to-all-start.3 = ((f32[32,16,128]{2,1,0:T(8,128)}), f32[32,16,128]{2,1,0:T(8,128)S(1)}, u32[]{:S(2)}, u32[]{:S(2)}) async-start(f32[32,16,128]{2,1,0:T(8,128)} %copy-done.2), calls=%async_computation.3 | async-start | bytes 524288 | tf_op jit(solution)/shard_map/all_to_all | solution.py:529
  80.0 0.0 copy-start.4
  80.1 0.0 copy-start.5
  80.1 7.1 %node_features_b.1.phi = bf16[4608,2048]{1,0:T(8,128)(2,1)} custom-call(s32[1]{0:T(128)} %bitcast.1.core, bf16[1024,128]{1,0:T(8,128)(2,1)} %bitcast.22, bf16[2,8,136,128]{3,2,1,0:T(8,128)(2,1)} %bitcast.16, bf16[4608,2048]{1,0:T(8,128)(2,1)} %node_features_a.1.rest_0_), custom_call_target="tpu_custom_call", output_to_operand_aliasing={{}: (3, {})} | custom-call | flops 578813952 | bytes 4194304 | tf_op jit(solution)/shard_map/node_features_b/pallas_call | solution.py:207
  87.2 4.5 %all-to-all-done.3.arrived = f32[32,16,128]{2,1,0:T(8,128)S(1)} async-done(((f32[32,16,128]{2,1,0:T(8,128)}), f32[32,16,128]{2,1,0:T(8,128)S(1)}, u32[]{:S(2)}, u32[]{:S(2)}) %all-to-all-start.3) | async-done | bytes 262176 | tf_op jit(solution)/shard_map/all_to_all | solution.py:529
  91.7 0.0 copy-done.4
  91.7 0.0 copy-done.5
  91.7 0.0 copy-start.6
  91.7 0.0 copy-start.7
  91.8 2.9 %third_product.1 = (f32[32,4,128]{2,1,0:T(4,128)}, f32[2,16,128]{2,1,0:T(8,128)S(1)}, f32[8,128]{1,0:T(8,128)S(1)}) custom-call(f32[32,16,128]{2,1,0:T(8,128)S(1)} %all-to-all-done.3.arrived, f32[16,128]{1,0:T(8,128)S(1)} %get-tuple-element.66.solution, f32[16,128]{1,0:T(8,128)S(1)} %get-tuple-element.67.residual, ...), custom_call_target="tpu_custom_call" | custom-call | flops 134217728 | bytes 4194304 | tf_op jit(solution)/shard_map/third_product/pallas_call | solution.py:533
  94.7 5.3 %all-to-all-start.4 = ((f32[32,4,128]{2,1,0:T(4,128)}), f32[32,4,128]{2,1,0:T(4,128)S(1)}, u32[]{:S(2)}, u32[]{:S(2)}) async-start(f32[32,4,128]{2,1,0:T(4,128)} %get-tuple-element.72), calls=%async_computation.4 | async-start | bytes 131072 | tf_op jit(solution)/shard_map/all_to_all | solution.py:548
  100.0 5.4 %node_values.1 = f32[2,2048]{1,0:T(2,128)S(1)} custom-call(f32[2,16,128]{2,1,0:T(8,128)S(1)} %get-tuple-element.73.both, bf16[4608,2048]{1,0:T(8,128)(2,1)} %node_features_b.1.phi), custom_call_target="tpu_custom_call" | custom-call | flops 268435456 | bytes 8388608 | tf_op jit(solution)/shard_map/node_values/pallas_call | solution.py:549
  105.4 3.6 %all-to-all-done.4.arrived = f32[32,4,128]{2,1,0:T(4,128)S(1)} async-done(((f32[32,4,128]{2,1,0:T(4,128)}), f32[32,4,128]{2,1,0:T(4,128)S(1)}, u32[]{:S(2)}, u32[]{:S(2)}) %all-to-all-start.4) | async-done | bytes 65568 | tf_op jit(solution)/shard_map/all_to_all | solution.py:548
  109.0 0.0 copy-done.6
  109.0 0.0 copy-done.7
  109.0 0.7 last.1
  (1 shorter events, 0.0 us)
Async XLA Ops:
  2.2 22.6 %all-to-all-start = ((bf16[8,136,128]{2,1,0:T(8,128)(2,1)}), bf16[8,136,128]{2,1,0:T(8,128)(2,1)S(1)}, u32[]{:S(2)}, u32[]{:S(2)}) async-start(bf16[8,136,128]{2,1,0:T(8,128)(2,1)} %pack.1), calls=%async_computation | async-start | bytes 557056 | tf_op jit(solution)/shard_map/all_to_all | solution.py:462
  12.5 0.9 copy-start.1
  28.6 19.9 %all-to-all-start.1 = ((f32[32,8,128]{2,1,0:T(8,128)}), f32[32,8,128]{2,1,0:T(8,128)}, u32[]{:S(2)}, u32[]{:S(2)}) async-start(f32[32,8,128]{2,1,0:T(8,128)} %get-tuple-element.47), calls=%async_computation.1 | async-start | bytes 262144 | tf_op jit(solution)/shard_map/all_to_all | solution.py:491
  43.8 0.8 copy-start
  53.1 0.7 copy-start.3
  53.9 18.4 %all-to-all-start.2 = ((f32[32,16,128]{2,1,0:T(8,128)}), f32[32,16,128]{2,1,0:T(8,128)S(1)}, u32[]{:S(2)}, u32[]{:S(2)}) async-start(f32[32,16,128]{2,1,0:T(8,128)} %copy-done.3), calls=%async_computation.2 | async-start | bytes 524288 | tf_op jit(solution)/shard_map/all_to_all | solution.py:514
  74.7 0.7 copy-start.2
  75.4 16.3 %all-to-all-start.3 = ((f32[32,16,128]{2,1,0:T(8,128)}), f32[32,16,128]{2,1,0:T(8,128)S(1)}, u32[]{:S(2)}, u32[]{:S(2)}) async-start(f32[32,16,128]{2,1,0:T(8,128)} %copy-done.2), calls=%async_computation.3 | async-start | bytes 524288 | tf_op jit(solution)/shard_map/all_to_all | solution.py:529
  80.0 11.7 %copy-start.4 = (s32[1024,1]{0,1:T(1,128)S(1)}, s32[1024,1]{0,1:T(1,128)}, u32[]{:S(2)}) copy-start(s32[1024,1]{0,1:T(1,128)} %param.13) | copy-start | bytes 12292
  80.1 11.7 %copy-start.5 = (s32[1024]{0:T(1024)S(1)}, s32[1024]{0:T(1024)}, u32[]{:S(2)}) copy-start(s32[1024]{0:T(1024)} %param.14) | copy-start | bytes 12292
  91.7 17.3 %copy-start.6 = (f32[128]{0:T(128)S(1)}, f32[128]{0:T(128)}, u32[]{:S(2)}) copy-start(f32[128]{0:T(128)} %param.18) | copy-start | bytes 1540
  91.7 17.3 %copy-start.7 = (s32[128]{0:T(128)S(1)}, s32[128]{0:T(128)}, u32[]{:S(2)}) copy-start(s32[128]{0:T(128)} %param.19) | copy-start | bytes 1540
  94.7 14.4 %all-to-all-start.4 = ((f32[32,4,128]{2,1,0:T(4,128)}), f32[32,4,128]{2,1,0:T(4,128)S(1)}, u32[]{:S(2)}, u32[]{:S(2)}) async-start(f32[32,4,128]{2,1,0:T(4,128)} %get-tuple-element.72), calls=%async_computation.4 | async-start | bytes 131072 | tf_op jit(solution)/shard_map/all_to_all | solution.py:548

commit v6 on v5

--- a/solution.py
+++ b/solution.py
@@ -72,7 +72,7 @@
 PARTS = 2
 KEPT = 0.5
 SPARE = 9
-PHASE_ROWS = 8
+PHASE_ROWS = 16
 
 
 def rows_at(index, size):
@@ -91,26 +91,27 @@
     return pl.CostEstimate(flops=flops, bytes_accessed=size, transcendentals=hard)
 
 
-def pack_kernel(freq, phase, out, packed, row, sems):
+def pack_kernel(freq, phase, out, row, last, sems):
     depth = freq.shape[0]
-    loads = [
-        pltpu.make_async_copy(freq, packed.at[0:depth], sems.at[0]),
-        pltpu.make_async_copy(phase, row, sems.at[1]),
-    ]
-    for load in loads:
-        load.start()
-    for load in loads:
-        load.wait()
-    packed[depth : depth + PHASE_ROWS, :] = jnp.broadcast_to(
-        row[...], (PHASE_ROWS, row.shape[1])
-    )
+    copies = out.shape[0]
+    load = pltpu.make_async_copy(phase, row, sems.at[2 * copies])
+    load.start()
     stores = [
-        pltpu.make_async_copy(packed, out.at[copy], sems.at[2 + copy])
-        for copy in range(out.shape[0])
+        pltpu.make_async_copy(freq, out.at[copy, 0:depth], sems.at[copy]) for copy in range(copies)
     ]
     for store in stores:
         store.start()
-    for store in stores:
+    load.wait()
+    last[...] = jnp.broadcast_to(row[...], last.shape)
+    tails = [
+        pltpu.make_async_copy(
+            last, out.at[copy, depth : depth + PHASE_ROWS], sems.at[copies + copy]
+        )
+        for copy in range(copies)
+    ]
+    for tail in tails:
+        tail.start()
+    for store in stores + tails:
         store.wait()
 
 
@@ -246,14 +247,13 @@
         at = rows_at(i, group)
         return pltpu.make_async_copy(rest.at[at], rest_out.at[at], sems.at[i])
 
-    fill(rest, first, PARTS, leave)
-    fill(kept, 0, PARTS)
+    fill(rest, first, 1, leave)
+    fill(kept, 0, 1)
     product = weight[...].astype(F32) * size[...].astype(F32)
     split = stack_rows(split3(product), 16)
     gathered[...] = dot_nn(split[:, :first], kept[...]) + dot_nn(split[:, first:], rest[...])
     send_whole(gathered, tiles, out)
-    for i in range(PARTS):
-        leave(i, rest.shape[0] // PARTS).wait()
+    leave(0, rest.shape[0]).wait()
 
 
 def rows_of(vector):
@@ -364,13 +364,13 @@
     here = values.shape[1]
     to_owner = (owner[...] == lax.broadcasted_iota(jnp.int32, (owners, here), 0)).astype(F32)
     to_patient = (patient[...] == lax.broadcasted_iota(jnp.int32, (patients, here), 0)).astype(F32)
-    parts = split3(part) + split3(weighted * fit_scale) + (weights,)
+    parts = split3(part)[:2] + split3(weighted * fit_scale)[:2] + (weights,)
     tall = jnp.concatenate([to_owner * part for part in parts], axis=0).astype(BF16)
     sums = dot_nt(tall, to_patient.astype(BF16))
     part = [sums[i * owners : (i + 1) * owners, :] for i in range(len(parts))]
-    out[:, 0, :] = part[0] + part[1] + part[2]
-    out[:, 1, :] = part[3] + part[4] + part[5]
-    out[:, 2, :] = part[6]
+    out[:, 0, :] = part[0] + part[1]
+    out[:, 1, :] = part[2] + part[3]
+    out[:, 2, :] = part[4]
     out[:, 3, :] = jnp.broadcast_to(energy, (owners, patients))
 
 
@@ -451,9 +451,9 @@
         out_specs=HBM,
         out_shape=jax.ShapeDtypeStruct((layers, depth + PHASE_ROWS, own), BF16),
         scratch_shapes=[
-            pltpu.VMEM((depth + PHASE_ROWS, own), BF16),
             pltpu.VMEM((1, own), BF16),
-            pltpu.SemaphoreType.DMA((2 + layers,)),
+            pltpu.VMEM((PHASE_ROWS, own), BF16),
+            pltpu.SemaphoreType.DMA((2 * layers + 1,)),
         ],
         compiler_params=params(60),
         name="pack",
@@ -482,7 +482,7 @@
             pltpu.VMEM((rows - first, half), BF16),
             pltpu.VMEM((16, half), F32),
             pltpu.VMEM((tall // 2, LANES), F32),
-            pltpu.SemaphoreType.DMA((PARTS,)),
+            pltpu.SemaphoreType.DMA((1,)),
         ],
         compiler_params=params(),
         name="near_features",

time: 111 us -> 119 us (1.072)
  Pallas kernels: 36.4 us -> 44.3 us
    pallas_call x1, Pallas kernels: 1.57 us -> 9.21 us  [on_device(): pl.pallas_call(pack_kernel, in_specs=[HBM, HBM], out_specs=HBM, out_shape...]
  transfers between devices with their start and end apart: 5 -> 5, of which waited for: 5 -> 5; matrix products, arithmetic and copies ran while one was open for 4% -> 3% of each run, Pallas kernels for 20% -> 19%
where the time goes in v6:
time: 119 us; the launch traced here: 118 us
  Pallas kernels  44.3 us (37%)
  starting transfers between devices  36.5 us (31%)
  waiting for transfers between devices  25 us (21%)
  local copies, waits for them, and re-layouts  7.07 us (6%)
  blocking collectives  4.42 us (4%)
    all_to_all x4, starting transfers between devices, on_device(): arrived = lax.all_to_all(sent, 'blk', 0, 0, tiled=True)  26.1 us
    all_to_all x4, waiting for transfers between devices, on_device(): arrived = lax.all_to_all(sent, 'blk', 0, 0, tiled=True)  17.3 us
    pallas_call x2, Pallas kernels, node_features(): pl.pallas_call(functools.partial(node_kernel, first), in_specs=[SMEM, VME...  14.3 us
    all_to_all x1, starting transfers between devices, on_device(): lax.all_to_all(packed, 'col', 0, 0, tiled=True, axis_index_groups=same_core)  10.3 us
    pallas_call x1, Pallas kernels, on_device(): pl.pallas_call(pack_kernel, in_specs=[HBM, HBM], out_specs=HBM, out_shape...  9.21 us
    all_to_all x1, waiting for transfers between devices, on_device(): lax.all_to_all(packed, 'col', 0, 0, tiled=True, axis_index_groups=same_core)  7.68 us
    pallas_call x1, Pallas kernels, on_device(): pl.pallas_call(nodes_kernel, grid=(2 * count // NODE_ROWS,), in_specs=[pl...  5.4 us
    pallas_call x1, Pallas kernels, on_device(): pl.pallas_call(near_kernel, in_specs=[VMEM] * 4, out_specs=[VMEM, HBM, VM...  4.11 us
  transfers between devices with their start and end apart: 5, of which 5 were waited for; matrix products, arithmetic and copies ran while one was open for 3% of the time, Pallas kernels for 19%

profile of v6, /device:TPU:8, one launch (start us, length us, event | category | flops | bytes accessed | tf_op | source)
XLA Modules:
  0.0 118.1 jit_solution(6619215552394224194)
XLA Ops:
  0.6 9.2 %pack.1 = bf16[8,144,128]{2,1,0:T(8,128)(2,1)} custom-call(bf16[128,128]{1,0:T(8,128)(2,1)} %freq.1, bf16[1,128]{1,0:T(2,128)(2,1)} %bitcast.25), custom_call_target="tpu_custom_call" | custom-call | tf_op jit(solution)/shard_map/pack/pallas_call | solution.py:448
  9.8 10.3 %all-to-all-start = ((bf16[8,144,128]{2,1,0:T(8,128)(2,1)}), bf16[8,144,128]{2,1,0:T(8,128)(2,1)S(1)}, u32[]{:S(2)}, u32[]{:S(2)}) async-start(bf16[8,144,128]{2,1,0:T(8,128)(2,1)} %pack.1), calls=%async_computation | async-start | bytes 589824 | tf_op jit(solution)/shard_map/all_to_all | solution.py:462
  20.2 0.0 copy-start.1
  20.2 0.9 copy-done.1
  21.1 0.7 reshape.43.weight
  21.8 0.7 reshape.44.size
  22.5 1.1 fusion
  23.6 0.7 copy.16
  24.3 0.7 copy.15
  25.1 7.7 %all-to-all-done.freq = bf16[8,144,128]{2,1,0:T(8,128)(2,1)S(1)} async-done(((bf16[8,144,128]{2,1,0:T(8,128)(2,1)}), bf16[8,144,128]{2,1,0:T(8,128)(2,1)S(1)}, u32[]{:S(2)}, u32[]{:S(2)}) %all-to-all-start) | async-done | bytes 294944 | tf_op jit(solution)/shard_map/all_to_all | solution.py:462
  32.8 4.1 %near_features.1 = (bf16[512,1024]{1,0:T(8,128)(2,1)S(1)}, bf16[9216,1024]{1,0:T(8,128)(2,1)}, f32[32,8,128]{2,1,0:T(8,128)}) custom-call(bf16[1024,128]{1,0:T(8,128)(2,1)S(1)} %stage_cov.1.cov, bf16[8,144,128]{2,1,0:T(8,128)(2,1)S(1)} %all-to-all-done.freq, bf16[1,1024]{1,0:T(2,128)(2,1)S(1)} %reshape.43.weight, bf16[1,1024]{1,0:T(2,128)(2,1)S(1)} %reshape.44.size), custom_call_target="tpu_custom_call" | custom-call | tf_op jit(solution)/shard_map/near_features/pallas_call | solution.py:472
  36.9 10.2 %all-to-all-start.1 = ((f32[32,8,128]{2,1,0:T(8,128)}), f32[32,8,128]{2,1,0:T(8,128)}, u32[]{:S(2)}, u32[]{:S(2)}) async-start(f32[32,8,128]{2,1,0:T(8,128)} %get-tuple-element.47), calls=%async_computation.1 | async-start | bytes 262144 | tf_op jit(solution)/shard_map/all_to_all | solution.py:491
  47.1 2.2 %all-gather = bf16[16,144,128]{2,1,0:T(8,128)(2,1)S(1)} all-gather(bf16[8,144,128]{2,1,0:T(8,128)(2,1)S(1)} %all-to-all-done.freq), channel_id=2, replica_groups={{0,1},{2,3},{4,5},{6,7},{8,9},{10,11},{12,13},{14,15},{16,17},{18,19},{..., dimensions={0}, use_global_device_ids=true | all-gather | bytes 884736 | tf_op jit(solution)/shard_map/all_gather | solution.py:492
  49.3 2.7 %far_features.1.far = bf16[1024,1024]{1,0:T(8,128)(2,1)S(1)} custom-call(s32[1]{0:T(128)} %bitcast.1.core, bf16[1024,128]{1,0:T(8,128)(2,1)S(1)} %stage_cov.1.cov, bf16[2,8,144,128]{3,2,1,0:T(8,128)(2,1)S(1)} %bitcast.14), custom_call_target="tpu_custom_call" | custom-call | flops 289406976 | bytes 2097152 | tf_op jit(solution)/shard_map/far_features/pallas_call | solution.py:167
  52.1 0.0 copy-start
  52.1 0.8 copy-done
  52.9 3.8 %all-to-all-done.1 = f32[32,8,128]{2,1,0:T(8,128)} async-done(((f32[32,8,128]{2,1,0:T(8,128)}), f32[32,8,128]{2,1,0:T(8,128)}, u32[]{:S(2)}, u32[]{:S(2)}) %all-to-all-start.1) | async-done | bytes 131104 | tf_op jit(solution)/shard_map/all_to_all | solution.py:491
  56.7 2.2 %all-gather.1 = f32[64,8,128]{2,1,0:T(8,128)S(1)} all-gather(f32[32,8,128]{2,1,0:T(8,128)} %all-to-all-done.1), channel_id=3, replica_groups={{0,1},{2,3},{4,5},{6,7},{8,9},{10,11},{12,13},{14,15},{16,17},{18,19},{..., dimensions={0}, use_global_device_ids=true | all-gather | bytes 393216 | tf_op jit(solution)/shard_map/all_gather | solution.py:495
  58.9 2.5 %first_product.1 = (f32[32,16,128]{2,1,0:T(8,128)S(1)}, f32[1,1024]{1,0:T(1,128)S(1)}, f32[16,128]{1,0:T(8,128)S(1)}) custom-call(s32[1]{0:T(128)} %bitcast.1.core, f32[2,32,8,128]{3,2,1,0:T(8,128)S(1)} %bitcast.17, bf16[512,1024]{1,0:T(8,128)(2,1)S(1)} %get-tuple-element.50.kept, bf16[9216,1024]{1,0:T(8,128)(2,1)} %get-tuple-element.51.rest, ...), custom_call_target="tpu_custom_call" | custom-call | flops 134217728 | bytes 4194304 | tf_op jit(solution)/shard_map/first_product/pallas_call | solution.py:503
  61.4 0.0 copy-start.3
  61.4 0.7 copy-done.3
  62.1 6.0 %all-to-all-start.2 = ((f32[32,16,128]{2,1,0:T(8,128)}), f32[32,16,128]{2,1,0:T(8,128)S(1)}, u32[]{:S(2)}, u32[]{:S(2)}) async-start(f32[32,16,128]{2,1,0:T(8,128)} %copy-done.3), calls=%async_computation.2 | async-start | bytes 524288 | tf_op jit(solution)/shard_map/all_to_all | solution.py:514
  68.1 7.1 %node_features_a.1.rest_0_ = bf16[4608,2048]{1,0:T(8,128)(2,1)} custom-call(s32[1]{0:T(128)} %bitcast.1.core, bf16[1024,128]{1,0:T(8,128)(2,1)} %bitcast.23, bf16[2,8,144,128]{3,2,1,0:T(8,128)(2,1)} %bitcast.15), custom_call_target="tpu_custom_call" | custom-call | flops 578813952 | bytes 4194304 | tf_op jit(solution)/shard_map/node_features_a/pallas_call | solution.py:208
  75.2 5.3 %all-to-all-done.2.arrived = f32[32,16,128]{2,1,0:T(8,128)S(1)} async-done(((f32[32,16,128]{2,1,0:T(8,128)}), f32[32,16,128]{2,1,0:T(8,128)S(1)}, u32[]{:S(2)}, u32[]{:S(2)}) %all-to-all-start.2) | async-done | bytes 262176 | tf_op jit(solution)/shard_map/all_to_all | solution.py:514
  80.6 2.5 %second_product.1 = (f32[32,16,128]{2,1,0:T(8,128)S(1)}, f32[2,1024]{1,0:T(2,128)S(1)}, f32[16,128]{1,0:T(8,128)S(1)}, f32[16,128]{1,0:T(8,128)S(1)}, f32[16,128]{1,0:T(8,128)S(1)}) custom-call(f32[32,16,128]{2,1,0:T(8,128)S(1)} %all-to-all-done.2.arrived, f32[16,128]{1,0:T(8,128)S(1)} %get-tuple-element.58.rhs, f32[1,1024]{1,0:T(1,128)S(1)} %get-tuple-element.59.before, ...), custom_call_target="tpu_custom_call" | custom-call | flops 134217728 | bytes 4194304 | tf_op jit(solution)/shard_map/second_product/pallas_call | solution.py:518
  83.1 0.0 copy-start.2
  83.1 0.7 copy-done.2
  83.8 4.6 %all-to-all-start.3 = ((f32[32,16,128]{2,1,0:T(8,128)}), f32[32,16,128]{2,1,0:T(8,128)S(1)}, u32[]{:S(2)}, u32[]{:S(2)}) async-start(f32[32,16,128]{2,1,0:T(8,128)} %copy-done.2), calls=%async_computation.3 | async-start | bytes 524288 | tf_op jit(solution)/shard_map/all_to_all | solution.py:529
  88.4 0.0 copy-start.4
  88.4 0.0 copy-start.5
  88.4 7.2 %node_features_b.1.phi = bf16[4608,2048]{1,0:T(8,128)(2,1)} custom-call(s32[1]{0:T(128)} %bitcast.1.core, bf16[1024,128]{1,0:T(8,128)(2,1)} %bitcast.22, bf16[2,8,144,128]{3,2,1,0:T(8,128)(2,1)} %bitcast.16, bf16[4608,2048]{1,0:T(8,128)(2,1)} %node_features_a.1.rest_0_), custom_call_target="tpu_custom_call", output_to_operand_aliasing={{}: (3, {})} | custom-call | flops 578813952 | bytes 4194304 | tf_op jit(solution)/shard_map/node_features_b/pallas_call | solution.py:208
  95.6 4.5 %all-to-all-done.3.arrived = f32[32,16,128]{2,1,0:T(8,128)S(1)} async-done(((f32[32,16,128]{2,1,0:T(8,128)}), f32[32,16,128]{2,1,0:T(8,128)S(1)}, u32[]{:S(2)}, u32[]{:S(2)}) %all-to-all-start.3) | async-done | bytes 262176 | tf_op jit(solution)/shard_map/all_to_all | solution.py:529
  100.1 0.0 copy-done.4
  100.1 0.0 copy-done.5
  100.1 0.0 copy-start.6
  100.1 0.0 copy-start.7
  100.1 2.9 %third_product.1 = (f32[32,4,128]{2,1,0:T(4,128)}, f32[2,16,128]{2,1,0:T(8,128)S(1)}, f32[8,128]{1,0:T(8,128)S(1)}) custom-call(f32[32,16,128]{2,1,0:T(8,128)S(1)} %all-to-all-done.3.arrived, f32[16,128]{1,0:T(8,128)S(1)} %get-tuple-element.66.solution, f32[16,128]{1,0:T(8,128)S(1)} %get-tuple-element.67.residual, ...), custom_call_target="tpu_custom_call" | custom-call | flops 134217728 | bytes 4194304 | tf_op jit(solution)/shard_map/third_product/pallas_call | solution.py:533
  103.0 5.3 %all-to-all-start.4 = ((f32[32,4,128]{2,1,0:T(4,128)}), f32[32,4,128]{2,1,0:T(4,128)S(1)}, u32[]{:S(2)}, u32[]{:S(2)}) async-start(f32[32,4,128]{2,1,0:T(4,128)} %get-tuple-element.72), calls=%async_computation.4 | async-start | bytes 131072 | tf_op jit(solution)/shard_map/all_to_all | solution.py:548
  108.3 5.4 %node_values.1 = f32[2,2048]{1,0:T(2,128)S(1)} custom-call(f32[2,16,128]{2,1,0:T(8,128)S(1)} %get-tuple-element.73.both, bf16[4608,2048]{1,0:T(8,128)(2,1)} %node_features_b.1.phi), custom_call_target="tpu_custom_call" | custom-call | flops 268435456 | bytes 8388608 | tf_op jit(solution)/shard_map/node_values/pallas_call | solution.py:549
  113.7 3.6 %all-to-all-done.4.arrived = f32[32,4,128]{2,1,0:T(4,128)S(1)} async-done(((f32[32,4,128]{2,1,0:T(4,128)}), f32[32,4,128]{2,1,0:T(4,128)S(1)}, u32[]{:S(2)}, u32[]{:S(2)}) %all-to-all-start.4) | async-done | bytes 65568 | tf_op jit(solution)/shard_map/all_to_all | solution.py:548
  117.4 0.0 copy-done.6
  117.4 0.0 copy-done.7
  117.4 0.7 last.1
  (1 shorter events, 0.0 us)
Async XLA Ops:
  9.8 22.9 %all-to-all-start = ((bf16[8,144,128]{2,1,0:T(8,128)(2,1)}), bf16[8,144,128]{2,1,0:T(8,128)(2,1)S(1)}, u32[]{:S(2)}, u32[]{:S(2)}) async-start(bf16[8,144,128]{2,1,0:T(8,128)(2,1)} %pack.1), calls=%async_computation | async-start | bytes 589824 | tf_op jit(solution)/shard_map/all_to_all | solution.py:462
  20.2 0.9 copy-start.1
  36.9 19.8 %all-to-all-start.1 = ((f32[32,8,128]{2,1,0:T(8,128)}), f32[32,8,128]{2,1,0:T(8,128)}, u32[]{:S(2)}, u32[]{:S(2)}) async-start(f32[32,8,128]{2,1,0:T(8,128)} %get-tuple-element.47), calls=%async_computation.1 | async-start | bytes 262144 | tf_op jit(solution)/shard_map/all_to_all | solution.py:491
  52.1 0.8 copy-start
  61.4 0.7 copy-start.3
  62.1 18.4 %all-to-all-start.2 = ((f32[32,16,128]{2,1,0:T(8,128)}), f32[32,16,128]{2,1,0:T(8,128)S(1)}, u32[]{:S(2)}, u32[]{:S(2)}) async-start(f32[32,16,128]{2,1,0:T(8,128)} %copy-done.3), calls=%async_computation.2 | async-start | bytes 524288 | tf_op jit(solution)/shard_map/all_to_all | solution.py:514
  83.1 0.7 copy-start.2
  83.8 16.3 %all-to-all-start.3 = ((f32[32,16,128]{2,1,0:T(8,128)}), f32[32,16,128]{2,1,0:T(8,128)S(1)}, u32[]{:S(2)}, u32[]{:S(2)}) async-start(f32[32,16,128]{2,1,0:T(8,128)} %copy-done.2), calls=%async_computation.3 | async-start | bytes 524288 | tf_op jit(solution)/shard_map/all_to_all | solution.py:529
  88.4 11.7 %copy-start.4 = (s32[1024,1]{0,1:T(1,128)S(1)}, s32[1024,1]{0,1:T(1,128)}, u32[]{:S(2)}) copy-start(s32[1024,1]{0,1:T(1,128)} %param.13) | copy-start | bytes 12292
  88.4 11.7 %copy-start.5 = (s32[1024]{0:T(1024)S(1)}, s32[1024]{0:T(1024)}, u32[]{:S(2)}) copy-start(s32[1024]{0:T(1024)} %param.14) | copy-start | bytes 12292
  100.1 17.3 %copy-start.6 = (f32[128]{0:T(128)S(1)}, f32[128]{0:T(128)}, u32[]{:S(2)}) copy-start(f32[128]{0:T(128)} %param.18) | copy-start | bytes 1540
  100.1 17.3 %copy-start.7 = (s32[128]{0:T(128)S(1)}, s32[128]{0:T(128)}, u32[]{:S(2)}) copy-start(s32[128]{0:T(128)} %param.19) | copy-start | bytes 1540
  103.0 14.4 %all-to-all-start.4 = ((f32[32,4,128]{2,1,0:T(4,128)}), f32[32,4,128]{2,1,0:T(4,128)S(1)}, u32[]{:S(2)}, u32[]{:S(2)}) async-start(f32[32,4,128]{2,1,0:T(4,128)} %get-tuple-element.72), calls=%async_computation.4 | async-start | bytes 131072 | tf_op jit(solution)/shard_map/all_to_all | solution.py:548

commit v7 on v5

--- a/solution.py
+++ b/solution.py
@@ -292,18 +292,34 @@
     return jnp.concatenate(values, axis=1) + total
 
 
-def product(direction, kept, held, copies, far, weight, gathered, tiles, out, scale):
+def product(direction, kept, held, copies, far, weight, staged, tiles, sends, out, scale):
     values = forward(direction, kept, held, copies, far)
     split = stack_rows(split3(weight[...].astype(F32) * values * scale), 16)
-    half, first = far.shape[1], kept.shape[0]
-    gathered[:, half:] = dot_nn(split, far[...])
-    gathered[:, :half] = dot_nn(split[:, :first], kept[...]) + dot_nn(split[:, first:], held[...])
-    send_whole(gathered, tiles, out)
+    first, layers = kept.shape[0], tiles.shape[0]
+
+    def leave(half, sums):
+        total = jnp.sum(sums, axis=0, keepdims=True)
+        for j in range(layers):
+            tiles[j : j + 1, :] = total[:, j * LANES : (j + 1) * LANES]
+        whole = tiles[...]
+        for copy in range(out.shape[0]):
+            staged[half, copy] = whole
+        send = pltpu.make_async_copy(
+            staged.at[half], out.at[:, half * layers : (half + 1) * layers], sends.at[half]
+        )
+        send.start()
+        return send
+
+    late = leave(1, dot_nn(split, far[...]))
+    near = dot_nn(split[:, :first], kept[...]) + dot_nn(split[:, first:], held[...])
+    early = leave(0, near)
+    late.wait()
+    early.wait()
     return values
 
 
 def first_kernel(
-    scale, rhs_scale, core, halves, kept, rest, far, weight, out, values_out, rhs_out, gathered, tiles, held, sems
+    scale, rhs_scale, core, halves, kept, rest, far, weight, out, values_out, rhs_out, staged, tiles, sends, held, sems
 ):
     copies = fetch(rest, held, sems)
     low, high = (jnp.sum(halves[h], axis=0) * rhs_scale for h in range(2))
@@ -312,14 +328,14 @@
     rhs_out[0:half, :] = jnp.where(swap, high, low)
     rhs_out[half : 2 * half, :] = jnp.where(swap, low, high)
     values_out[...] = product(
-        rhs_out[...], kept, held, copies, far, weight, gathered, tiles, out, scale
+        rhs_out[...], kept, held, copies, far, weight, staged, tiles, sends, out, scale
     )
 
 
 def second_kernel(
     scale, arrived, rhs, before, kept, rest, far, weight,
     out, fit_out, solution_out, residual_out, direction_out,
-    gathered, tiles, held, sems,
+    staged, tiles, sends, held, sems,
 ):
     copies = fetch(rest, held, sems)
     direction = rhs[...]
@@ -333,7 +349,7 @@
     direction_out[...] = later
     fit_out[0:1, :] = length * before[...]
     fit_out[1:2, :] = product(
-        later, kept, held, copies, far, weight, gathered, tiles, out, scale
+        later, kept, held, copies, far, weight, staged, tiles, sends, out, scale
     )
 
 
@@ -494,16 +510,20 @@
     arrived, far = together((arrived, far))
     halves = lax.all_gather(arrived, "col", axis_index_groups=pairs)
 
-    message = jax.ShapeDtypeStruct((blocks, tall, LANES), F32)
+    message = pltpu.HBM((blocks, tall, LANES), F32)
     vector = jax.ShapeDtypeStruct((tall, LANES), F32)
     fetched = [pltpu.VMEM((rows - first, half), BF16), pltpu.SemaphoreType.DMA((PARTS,))]
-    scratch = [pltpu.VMEM((16, inducing), F32), pltpu.VMEM((tall, LANES), F32)] + fetched
+    scratch = [
+        pltpu.VMEM((2, blocks, tall // 2, LANES), F32),
+        pltpu.VMEM((tall // 2, LANES), F32),
+        pltpu.SemaphoreType.DMA((2,)),
+    ] + fetched
     work = cost(64 * rows * inducing, 2 * rows * inducing)
 
     sent, before, rhs = pl.pallas_call(
         functools.partial(first_kernel, scale, 1.0 / math.sqrt(rows * blocks)),
         in_specs=[SMEM, VMEM, VMEM, HBM, VMEM, VMEM],
-        out_specs=[VMEM] * 3,
+        out_specs=[HBM, VMEM, VMEM],
         out_shape=[message, jax.ShapeDtypeStruct((1, rows), F32), vector],
         scratch_shapes=scratch,
         compiler_params=params(),
@@ -518,7 +538,7 @@
     sent, fit, solution, residual, direction = pl.pallas_call(
         functools.partial(second_kernel, scale),
         in_specs=[VMEM] * 4 + [HBM, VMEM, VMEM],
-        out_specs=[VMEM] * 5,
+        out_specs=[HBM] + [VMEM] * 4,
         out_shape=[message, jax.ShapeDtypeStruct((2, rows), F32), vector, vector, vector],
         scratch_shapes=scratch,
         compiler_params=params(),

time: 111 us -> 110 us (level)
  Pallas kernels: 36.4 us -> 37.8 us
  local copies, waits for them, and re-layouts: 7.06 us -> 5.7 us
    unnamed x16 -> x12, local copies, waits for them, and re-layouts: 3.13 us -> 1.76 us
where the time goes in v7:
time: 110 us
  Pallas kernels  37.8 us (34%)
  starting transfers between devices  36.5 us (33%)
  waiting for transfers between devices  24.4 us (22%)
  local copies, waits for them, and re-layouts  5.7 us (5%)
  blocking collectives  4.4 us (4%)
    all_to_all x4, starting transfers between devices, on_device(): arrived = lax.all_to_all(sent, 'blk', 0, 0, tiled=True)  26.2 us
    all_to_all x4, waiting for transfers between devices, on_device(): arrived = lax.all_to_all(sent, 'blk', 0, 0, tiled=True)  17.1 us
    pallas_call x2, Pallas kernels, node_features(): pl.pallas_call(functools.partial(node_kernel, first), in_specs=[SMEM, VME...  14.3 us
    all_to_all x1, starting transfers between devices, on_device(): lax.all_to_all(packed, 'col', 0, 0, tiled=True, axis_index_groups=same_core)  10.3 us
    all_to_all x1, waiting for transfers between devices, on_device(): lax.all_to_all(packed, 'col', 0, 0, tiled=True, axis_index_groups=same_core)  7.31 us
    pallas_call x1, Pallas kernels, on_device(): pl.pallas_call(nodes_kernel, grid=(2 * count // NODE_ROWS,), in_specs=[pl...  5.4 us
    pallas_call x1, Pallas kernels, on_device(): pl.pallas_call(near_kernel, in_specs=[VMEM] * 4, out_specs=[VMEM, HBM, VM...  3.79 us
    pallas_call x1, Pallas kernels, on_device(): pl.pallas_call(functools.partial(second_kernel, scale), in_specs=[VMEM] *...  3.19 us
  transfers between devices with their start and end apart: 5, of which 5 were waited for; matrix products, arithmetic and copies ran while one was open for 4% of the time, Pallas kernels for 20%

profile of v7, /device:TPU:8, one launch (start us, length us, event | category | flops | bytes accessed | tf_op | source)
XLA Modules:
  0.0 109.5 jit_solution(5279586550834419543)
XLA Ops:
  0.6 1.6 %pack.1 = bf16[8,136,128]{2,1,0:T(8,128)(2,1)} custom-call(bf16[128,128]{1,0:T(8,128)(2,1)} %freq.1, bf16[1,128]{1,0:T(2,128)(2,1)} %bitcast.25), custom_call_target="tpu_custom_call" | custom-call | tf_op jit(solution)/shard_map/pack/pallas_call | solution.py:464
  2.2 10.3 %all-to-all-start = ((bf16[8,136,128]{2,1,0:T(8,128)(2,1)}), bf16[8,136,128]{2,1,0:T(8,128)(2,1)S(1)}, u32[]{:S(2)}, u32[]{:S(2)}) async-start(bf16[8,136,128]{2,1,0:T(8,128)(2,1)} %pack.1), calls=%async_computation | async-start | bytes 557056 | tf_op jit(solution)/shard_map/all_to_all | solution.py:478
  12.5 0.0 copy-start.1
  12.5 0.9 copy-done.1
  13.5 0.7 reshape.43.weight
  14.2 0.7 reshape.44.size
  14.9 1.1 fusion
  15.9 0.8 copy.16
  16.7 0.7 copy.15
  17.4 7.3 %all-to-all-done.freq = bf16[8,136,128]{2,1,0:T(8,128)(2,1)S(1)} async-done(((bf16[8,136,128]{2,1,0:T(8,128)(2,1)}), bf16[8,136,128]{2,1,0:T(8,128)(2,1)S(1)}, u32[]{:S(2)}, u32[]{:S(2)}) %all-to-all-start) | async-done | bytes 278560 | tf_op jit(solution)/shard_map/all_to_all | solution.py:478
  24.7 3.8 %near_features.1 = (bf16[512,1024]{1,0:T(8,128)(2,1)S(1)}, bf16[9216,1024]{1,0:T(8,128)(2,1)}, f32[32,8,128]{2,1,0:T(8,128)}) custom-call(bf16[1024,128]{1,0:T(8,128)(2,1)S(1)} %stage_cov.1.cov, bf16[8,136,128]{2,1,0:T(8,128)(2,1)S(1)} %all-to-all-done.freq, bf16[1,1024]{1,0:T(2,128)(2,1)S(1)} %reshape.43.weight, bf16[1,1024]{1,0:T(2,128)(2,1)S(1)} %reshape.44.size), custom_call_target="tpu_custom_call" | custom-call | tf_op jit(solution)/shard_map/near_features/pallas_call | solution.py:488
  28.5 10.2 %all-to-all-start.1 = ((f32[32,8,128]{2,1,0:T(8,128)}), f32[32,8,128]{2,1,0:T(8,128)}, u32[]{:S(2)}, u32[]{:S(2)}) async-start(f32[32,8,128]{2,1,0:T(8,128)} %get-tuple-element.47), calls=%async_computation.1 | async-start | bytes 262144 | tf_op jit(solution)/shard_map/all_to_all | solution.py:507
  38.8 2.2 %all-gather = bf16[16,136,128]{2,1,0:T(8,128)(2,1)S(1)} all-gather(bf16[8,136,128]{2,1,0:T(8,128)(2,1)S(1)} %all-to-all-done.freq), channel_id=2, replica_groups={{0,1},{2,3},{4,5},{6,7},{8,9},{10,11},{12,13},{14,15},{16,17},{18,19},{..., dimensions={0}, use_global_device_ids=true | all-gather | bytes 835584 | tf_op jit(solution)/shard_map/all_gather | solution.py:508
  41.0 2.8 %far_features.1.far = bf16[1024,1024]{1,0:T(8,128)(2,1)S(1)} custom-call(s32[1]{0:T(128)} %bitcast.1.core, bf16[1024,128]{1,0:T(8,128)(2,1)S(1)} %stage_cov.1.cov, bf16[2,8,136,128]{3,2,1,0:T(8,128)(2,1)S(1)} %bitcast.14), custom_call_target="tpu_custom_call" | custom-call | flops 289406976 | bytes 2097152 | tf_op jit(solution)/shard_map/far_features/pallas_call | solution.py:166
  43.8 0.0 copy-start
  43.8 0.8 copy-done
  44.6 3.8 %all-to-all-done.1 = f32[32,8,128]{2,1,0:T(8,128)} async-done(((f32[32,8,128]{2,1,0:T(8,128)}), f32[32,8,128]{2,1,0:T(8,128)}, u32[]{:S(2)}, u32[]{:S(2)}) %all-to-all-start.1) | async-done | bytes 131104 | tf_op jit(solution)/shard_map/all_to_all | solution.py:507
  48.4 2.2 %all-gather.1 = f32[64,8,128]{2,1,0:T(8,128)S(1)} all-gather(f32[32,8,128]{2,1,0:T(8,128)} %all-to-all-done.1), channel_id=3, replica_groups={{0,1},{2,3},{4,5},{6,7},{8,9},{10,11},{12,13},{14,15},{16,17},{18,19},{..., dimensions={0}, use_global_device_ids=true | all-gather | bytes 393216 | tf_op jit(solution)/shard_map/all_gather | solution.py:511
  50.6 3.2 %first_product.1 = (f32[32,16,128]{2,1,0:T(8,128)}, f32[1,1024]{1,0:T(1,128)S(1)}, f32[16,128]{1,0:T(8,128)S(1)}) custom-call(s32[1]{0:T(128)} %bitcast.1.core, f32[2,32,8,128]{3,2,1,0:T(8,128)S(1)} %bitcast.17, bf16[512,1024]{1,0:T(8,128)(2,1)S(1)} %get-tuple-element.50.kept, bf16[9216,1024]{1,0:T(8,128)(2,1)} %get-tuple-element.51.rest, ...), custom_call_target="tpu_custom_call" | custom-call | flops 134217728 | bytes 4194304 | tf_op jit(solution)/shard_map/first_product/pallas_call | solution.py:523
  53.8 6.0 %all-to-all-start.2 = ((f32[32,16,128]{2,1,0:T(8,128)}), f32[32,16,128]{2,1,0:T(8,128)S(1)}, u32[]{:S(2)}, u32[]{:S(2)}) async-start(f32[32,16,128]{2,1,0:T(8,128)} %get-tuple-element.55), calls=%async_computation.2 | async-start | bytes 524288 | tf_op jit(solution)/shard_map/all_to_all | solution.py:534
  59.8 7.1 %node_features_a.1.rest_0_ = bf16[4608,2048]{1,0:T(8,128)(2,1)} custom-call(s32[1]{0:T(128)} %bitcast.1.core, bf16[1024,128]{1,0:T(8,128)(2,1)} %bitcast.23, bf16[2,8,136,128]{3,2,1,0:T(8,128)(2,1)} %bitcast.15), custom_call_target="tpu_custom_call" | custom-call | flops 578813952 | bytes 4194304 | tf_op jit(solution)/shard_map/node_features_a/pallas_call | solution.py:207
  66.9 5.3 %all-to-all-done.2.arrived = f32[32,16,128]{2,1,0:T(8,128)S(1)} async-done(((f32[32,16,128]{2,1,0:T(8,128)}), f32[32,16,128]{2,1,0:T(8,128)S(1)}, u32[]{:S(2)}, u32[]{:S(2)}) %all-to-all-start.2) | async-done | bytes 262176 | tf_op jit(solution)/shard_map/all_to_all | solution.py:534
  72.2 3.2 %second_product.1 = (f32[32,16,128]{2,1,0:T(8,128)}, f32[2,1024]{1,0:T(2,128)S(1)}, f32[16,128]{1,0:T(8,128)S(1)}, f32[16,128]{1,0:T(8,128)S(1)}, f32[16,128]{1,0:T(8,128)S(1)}) custom-call(f32[32,16,128]{2,1,0:T(8,128)S(1)} %all-to-all-done.2.arrived, f32[16,128]{1,0:T(8,128)S(1)} %get-tuple-element.58.rhs, f32[1,1024]{1,0:T(1,128)S(1)} %get-tuple-element.59.before, ...), custom_call_target="tpu_custom_call" | custom-call | flops 134217728 | bytes 4194304 | tf_op jit(solution)/shard_map/second_product/pallas_call | solution.py:538
  75.4 4.6 %all-to-all-start.3 = ((f32[32,16,128]{2,1,0:T(8,128)}), f32[32,16,128]{2,1,0:T(8,128)S(1)}, u32[]{:S(2)}, u32[]{:S(2)}) async-start(f32[32,16,128]{2,1,0:T(8,128)} %get-tuple-element.62), calls=%async_computation.3 | async-start | bytes 524288 | tf_op jit(solution)/shard_map/all_to_all | solution.py:549
  80.1 0.0 copy-start.2
  80.1 0.0 copy-start.3
  80.1 7.1 %node_features_b.1.phi = bf16[4608,2048]{1,0:T(8,128)(2,1)} custom-call(s32[1]{0:T(128)} %bitcast.1.core, bf16[1024,128]{1,0:T(8,128)(2,1)} %bitcast.22, bf16[2,8,136,128]{3,2,1,0:T(8,128)(2,1)} %bitcast.16, bf16[4608,2048]{1,0:T(8,128)(2,1)} %node_features_a.1.rest_0_), custom_call_target="tpu_custom_call", output_to_operand_aliasing={{}: (3, {})} | custom-call | flops 578813952 | bytes 4194304 | tf_op jit(solution)/shard_map/node_features_b/pallas_call | solution.py:207
  87.2 4.5 %all-to-all-done.3.arrived = f32[32,16,128]{2,1,0:T(8,128)S(1)} async-done(((f32[32,16,128]{2,1,0:T(8,128)}), f32[32,16,128]{2,1,0:T(8,128)S(1)}, u32[]{:S(2)}, u32[]{:S(2)}) %all-to-all-start.3) | async-done | bytes 262176 | tf_op jit(solution)/shard_map/all_to_all | solution.py:549
  91.7 0.0 copy-done.2
  91.8 0.0 copy-done.3
  91.8 0.0 copy-start.4
  91.8 0.0 copy-start.5
  91.8 2.9 %third_product.1 = (f32[32,4,128]{2,1,0:T(4,128)}, f32[2,16,128]{2,1,0:T(8,128)S(1)}, f32[8,128]{1,0:T(8,128)S(1)}) custom-call(f32[32,16,128]{2,1,0:T(8,128)S(1)} %all-to-all-done.3.arrived, f32[16,128]{1,0:T(8,128)S(1)} %get-tuple-element.66.solution, f32[16,128]{1,0:T(8,128)S(1)} %get-tuple-element.67.residual, ...), custom_call_target="tpu_custom_call" | custom-call | flops 134217728 | bytes 4194304 | tf_op jit(solution)/shard_map/third_product/pallas_call | solution.py:553
  94.7 5.3 %all-to-all-start.4 = ((f32[32,4,128]{2,1,0:T(4,128)}), f32[32,4,128]{2,1,0:T(4,128)S(1)}, u32[]{:S(2)}, u32[]{:S(2)}) async-start(f32[32,4,128]{2,1,0:T(4,128)} %get-tuple-element.72), calls=%async_computation.4 | async-start | bytes 131072 | tf_op jit(solution)/shard_map/all_to_all | solution.py:568
  100.0 5.4 %node_values.1 = f32[2,2048]{1,0:T(2,128)S(1)} custom-call(f32[2,16,128]{2,1,0:T(8,128)S(1)} %get-tuple-element.73.both, bf16[4608,2048]{1,0:T(8,128)(2,1)} %node_features_b.1.phi), custom_call_target="tpu_custom_call" | custom-call | flops 268435456 | bytes 8388608 | tf_op jit(solution)/shard_map/node_values/pallas_call | solution.py:569
  105.4 3.4 %all-to-all-done.4.arrived = f32[32,4,128]{2,1,0:T(4,128)S(1)} async-done(((f32[32,4,128]{2,1,0:T(4,128)}), f32[32,4,128]{2,1,0:T(4,128)S(1)}, u32[]{:S(2)}, u32[]{:S(2)}) %all-to-all-start.4) | async-done | bytes 65568 | tf_op jit(solution)/shard_map/all_to_all | solution.py:568
  108.8 0.0 copy-done.4
  108.8 0.0 copy-done.5
  108.8 0.7 last.1
  (1 shorter events, 0.0 us)
Async XLA Ops:
  2.2 22.6 %all-to-all-start = ((bf16[8,136,128]{2,1,0:T(8,128)(2,1)}), bf16[8,136,128]{2,1,0:T(8,128)(2,1)S(1)}, u32[]{:S(2)}, u32[]{:S(2)}) async-start(bf16[8,136,128]{2,1,0:T(8,128)(2,1)} %pack.1), calls=%async_computation | async-start | bytes 557056 | tf_op jit(solution)/shard_map/all_to_all | solution.py:478
  12.5 0.9 copy-start.1
  28.5 19.8 %all-to-all-start.1 = ((f32[32,8,128]{2,1,0:T(8,128)}), f32[32,8,128]{2,1,0:T(8,128)}, u32[]{:S(2)}, u32[]{:S(2)}) async-start(f32[32,8,128]{2,1,0:T(8,128)} %get-tuple-element.47), calls=%async_computation.1 | async-start | bytes 262144 | tf_op jit(solution)/shard_map/all_to_all | solution.py:507
  43.8 0.8 copy-start
  53.8 18.5 %all-to-all-start.2 = ((f32[32,16,128]{2,1,0:T(8,128)}), f32[32,16,128]{2,1,0:T(8,128)S(1)}, u32[]{:S(2)}, u32[]{:S(2)}) async-start(f32[32,16,128]{2,1,0:T(8,128)} %get-tuple-element.55), calls=%async_computation.2 | async-start | bytes 524288 | tf_op jit(solution)/shard_map/all_to_all | solution.py:534
  75.4 16.3 %all-to-all-start.3 = ((f32[32,16,128]{2,1,0:T(8,128)}), f32[32,16,128]{2,1,0:T(8,128)S(1)}, u32[]{:S(2)}, u32[]{:S(2)}) async-start(f32[32,16,128]{2,1,0:T(8,128)} %get-tuple-element.62), calls=%async_computation.3 | async-start | bytes 524288 | tf_op jit(solution)/shard_map/all_to_all | solution.py:549
  80.1 11.7 %copy-start.2 = (s32[1024,1]{0,1:T(1,128)S(1)}, s32[1024,1]{0,1:T(1,128)}, u32[]{:S(2)}) copy-start(s32[1024,1]{0,1:T(1,128)} %param.13) | copy-start | bytes 12292
  80.1 11.7 %copy-start.3 = (s32[1024]{0:T(1024)S(1)}, s32[1024]{0:T(1024)}, u32[]{:S(2)}) copy-start(s32[1024]{0:T(1024)} %param.14) | copy-start | bytes 12292
  91.8 17.1 %copy-start.4 = (f32[128]{0:T(128)S(1)}, f32[128]{0:T(128)}, u32[]{:S(2)}) copy-start(f32[128]{0:T(128)} %param.18) | copy-start | bytes 1540
  91.8 17.1 %copy-start.5 = (s32[128]{0:T(128)S(1)}, s32[128]{0:T(128)}, u32[]{:S(2)}) copy-start(s32[128]{0:T(128)} %param.19) | copy-start | bytes 1540
  94.7 14.1 %all-to-all-start.4 = ((f32[32,4,128]{2,1,0:T(4,128)}), f32[32,4,128]{2,1,0:T(4,128)S(1)}, u32[]{:S(2)}, u32[]{:S(2)}) async-start(f32[32,4,128]{2,1,0:T(4,128)} %get-tuple-element.72), calls=%async_computation.4 | async-start | bytes 131072 | tf_op jit(solution)/shard_map/all_to_all | solution.py:568

commit v8 on v5

--- a/solution.py
+++ b/solution.py
@@ -396,7 +396,8 @@
     tiles[...] = both[0] + length * direction
     weights_out[...] = tiles[pl.ds(mine[0], 1), :]
     effect = (sums[0:1, :] - length * sums[1:2, :]) / (1.0 + sums[2:3, :])
-    values = (node_values[0:1, :] + length * node_values[1:2, :]) * fit_scale
+    halves = [node_values[h, 0:1, :] + length * node_values[h, 1:2, :] for h in range(2)]
+    values = jnp.concatenate(halves, axis=1) * fit_scale
     patients = loglik.shape[1]
     nodes = values.shape[1] // patients
     total = jnp.zeros_like(effect)
@@ -464,8 +465,8 @@
     by_node = turned.transpose(1, 0, 2).reshape(nodes * patients, depth)
     count = nodes * patients // 2
     height = (SPARE * nodes * patients) // 4
-    node_covs = (by_node[:count], by_node[count:])
-    near_freq, cov, node_covs = together((near_freq, cov, node_covs))
+    by_node = lax.dynamic_slice_in_dim(by_node, core[0] * count, count, 0)
+    near_freq, cov, by_node = together((near_freq, cov, by_node))
 
     half = inducing // 2
     first = int(rows * KEPT)
@@ -510,7 +511,7 @@
         cost_estimate=work,
         name="first_product",
     )(core, halves, kept, rest, far, weight)
-    sent, node_cov_now = together((sent, node_covs[0]))
+    sent, node_cov_now = together((sent, by_node))
     arrived = lax.all_to_all(sent, "blk", 0, 0, tiled=True)
     node_phi = node_features(core, node_cov_now, freq, None, 0, height, "node_features_a")
     arrived, node_phi = together((arrived, node_phi))
@@ -525,11 +526,7 @@
         cost_estimate=work,
         name="second_product",
     )(arrived, rhs, before, kept, rest, far, weight)
-    sent, node_cov_now = together((sent, node_covs[1]))
     arrived = lax.all_to_all(sent, "blk", 0, 0, tiled=True)
-    node_phi = node_features(core, node_cov_now, freq, node_phi, count, height, "node_features_b")
-    arrived, node_phi = together((arrived, node_phi))
-
     sent, both, norm = pl.pallas_call(
         functools.partial(third_kernel, scale, fit_scale),
         in_specs=[VMEM] * 6 + [HBM] + [VMEM] * 5,
@@ -548,18 +545,19 @@
     arrived = lax.all_to_all(sent, "blk", 0, 0, tiled=True)
     node_values = pl.pallas_call(
         nodes_kernel,
-        grid=(2 * count // NODE_ROWS,),
+        grid=(count // NODE_ROWS,),
         in_specs=[
             pl.BlockSpec(both.shape, lambda i: (0, 0, 0)),
             pl.BlockSpec((NODE_ROWS, inducing), lambda i: (i, 0)),
         ],
         out_specs=pl.BlockSpec((2, NODE_ROWS), lambda i: (0, i)),
-        out_shape=jax.ShapeDtypeStruct((2, 2 * count), F32),
+        out_shape=jax.ShapeDtypeStruct((2, count), F32),
         scratch_shapes=[pltpu.VMEM((16, inducing), BF16)],
         compiler_params=params(),
         cost_estimate=cost(64 * 2 * count * inducing, 4 * count * inducing),
         name="node_values",
     )(both, node_phi)
+    node_values = lax.all_gather(node_values, "col", axis_index_groups=pairs)
     arrived, node_values = together((arrived, node_values))
 
     loglik, weights = pl.pallas_call(

time: 111 us -> 108 us (0.973)
  blocking collectives: 4.4 us -> 22.2 us
  Pallas kernels: 36.4 us -> 26.9 us
  starting transfers between devices: 36.4 us -> 31.1 us
  waiting for transfers between devices: 24.7 us -> 21 us
  local copies, waits for them, and re-layouts: 7.06 us -> 5.73 us
    all_to_all x0 -> x1, blocking collectives: none -> 16.1 us  [on_device(): arrived = lax.all_to_all(sent, 'blk', 0, 0, tiled=True)]
    pallas_call x2 -> x1, Pallas kernels: 14.3 us -> 7.15 us  [node_features(): pl.pallas_call(functools.partial(node_kernel, first), in_specs=[SMEM, VME...]
    all_to_all x4 -> x3, starting transfers between devices: 26 us -> 20.8 us  [on_device(): arrived = lax.all_to_all(sent, 'blk', 0, 0, tiled=True)]
    all_to_all x4 -> x3, waiting for transfers between devices: 17.4 us -> 13.1 us  [on_device(): arrived = lax.all_to_all(sent, 'blk', 0, 0, tiled=True)]
    slice x3 -> x0, local copies, waits for them, and re-layouts: 2.55 us -> none  [on_device(): node_covs = (by_node[:count], by_node[count:])]
    pallas_call x1, Pallas kernels: 5.4 us -> 2.98 us  [on_device(): pl.pallas_call(nodes_kernel, grid=(count // NODE_ROWS,), in_specs=[pl.Blo...]
    all_gather x0 -> x1, blocking collectives: none -> 1.82 us  [on_device(): node_values = lax.all_gather(node_values, 'col', axis_index_groups=pairs)]
    transpose x0 -> x1, local copies, waits for them, and re-layouts: none -> 1.18 us  [on_device(): by_node = turned.transpose(1, 0, 2).reshape(nodes * patients, depth)]
  transfers between devices with their start and end apart: 5 -> 4, of which waited for: 5 -> 4; matrix products, arithmetic and copies ran while one was open for 4% -> 3% of each run, Pallas kernels for 20% -> 12%
where the time goes in v8:
time: 108 us
  starting transfers between devices  31.1 us (29%)
  Pallas kernels  26.9 us (25%)
  blocking collectives  22.2 us (21%)
  waiting for transfers between devices  21 us (19%)
  local copies, waits for them, and re-layouts  5.73 us (5%)
    all_to_all x3, starting transfers between devices, on_device(): arrived = lax.all_to_all(sent, 'blk', 0, 0, tiled=True)  20.8 us
    all_to_all x1, blocking collectives, on_device(): arrived = lax.all_to_all(sent, 'blk', 0, 0, tiled=True)  16.1 us
    all_to_all x3, waiting for transfers between devices, on_device(): arrived = lax.all_to_all(sent, 'blk', 0, 0, tiled=True)  13.1 us
    all_to_all x1, starting transfers between devices, on_device(): lax.all_to_all(packed, 'col', 0, 0, tiled=True, axis_index_groups=same_core)  10.3 us
    all_to_all x1, waiting for transfers between devices, on_device(): lax.all_to_all(packed, 'col', 0, 0, tiled=True, axis_index_groups=same_core)  7.95 us
    pallas_call x1, Pallas kernels, node_features(): pl.pallas_call(functools.partial(node_kernel, first), in_specs=[SMEM, VME...  7.15 us
    pallas_call x1, Pallas kernels, on_device(): pl.pallas_call(near_kernel, in_specs=[VMEM] * 4, out_specs=[VMEM, HBM, VM...  3.79 us
    pallas_call x1, Pallas kernels, on_device(): pl.pallas_call(nodes_kernel, grid=(count // NODE_ROWS,), in_specs=[pl.Blo...  2.98 us
  transfers between devices with their start and end apart: 4, of which 4 were waited for; matrix products, arithmetic and copies ran while one was open for 3% of the time, Pallas kernels for 12%

profile of v8, /device:TPU:8, one launch (start us, length us, event | category | flops | bytes accessed | tf_op | source)
XLA Modules:
  0.0 107.7 jit_solution(17042126552757406934)
XLA Ops:
  0.6 1.6 %pack.1 = bf16[8,136,128]{2,1,0:T(8,128)(2,1)} custom-call(bf16[128,128]{1,0:T(8,128)(2,1)} %freq.1, bf16[1,128]{1,0:T(2,128)(2,1)} %bitcast.24), custom_call_target="tpu_custom_call" | custom-call | tf_op jit(solution)/shard_map/pack/pallas_call | solution.py:449
  2.2 10.3 %all-to-all-start = ((bf16[8,136,128]{2,1,0:T(8,128)(2,1)}), bf16[8,136,128]{2,1,0:T(8,128)(2,1)S(1)}, u32[]{:S(2)}, u32[]{:S(2)}) async-start(bf16[8,136,128]{2,1,0:T(8,128)(2,1)} %pack.1), calls=%async_computation | async-start | bytes 557056 | tf_op jit(solution)/shard_map/all_to_all | solution.py:463
  12.5 0.0 copy-start.1
  12.5 0.9 copy-done.1
  13.5 0.7 reshape.44.weight
  14.2 0.7 reshape.45.size
  14.9 1.2 %copy.13 = bf16[16,128,128]{2,1,0:T(8,128)(2,1)S(1)} copy(bf16[16,128,128]{2,0,1:T(8,128)(2,1)} %bitcast.23) | data formatting | bytes 1048576 | tf_op jit(solution)/shard_map/transpose | solution.py:465
  16.1 0.7 constant_dynamic-slice_fusion.cov
  16.8 8.0 %all-to-all-done.freq = bf16[8,136,128]{2,1,0:T(8,128)(2,1)S(1)} async-done(((bf16[8,136,128]{2,1,0:T(8,128)(2,1)}), bf16[8,136,128]{2,1,0:T(8,128)(2,1)S(1)}, u32[]{:S(2)}, u32[]{:S(2)}) %all-to-all-start) | async-done | bytes 278560 | tf_op jit(solution)/shard_map/all_to_all | solution.py:463
  24.7 3.8 %near_features.1 = (bf16[512,1024]{1,0:T(8,128)(2,1)S(1)}, bf16[9216,1024]{1,0:T(8,128)(2,1)}, f32[32,8,128]{2,1,0:T(8,128)}) custom-call(bf16[1024,128]{1,0:T(8,128)(2,1)S(1)} %stage_cov.1.cov, bf16[8,136,128]{2,1,0:T(8,128)(2,1)S(1)} %all-to-all-done.freq, bf16[1,1024]{1,0:T(2,128)(2,1)S(1)} %reshape.44.weight, bf16[1,1024]{1,0:T(2,128)(2,1)S(1)} %reshape.45.size), custom_call_target="tpu_custom_call" | custom-call | tf_op jit(solution)/shard_map/near_features/pallas_call | solution.py:473
  28.6 10.2 %all-to-all-start.1 = ((f32[32,8,128]{2,1,0:T(8,128)}), f32[32,8,128]{2,1,0:T(8,128)S(1)}, u32[]{:S(2)}, u32[]{:S(2)}) async-start(f32[32,8,128]{2,1,0:T(8,128)} %get-tuple-element.42), calls=%async_computation.1 | async-start | bytes 262144 | tf_op jit(solution)/shard_map/all_to_all | solution.py:492
  38.7 2.2 %all-gather = bf16[16,136,128]{2,1,0:T(8,128)(2,1)S(1)} all-gather(bf16[8,136,128]{2,1,0:T(8,128)(2,1)S(1)} %all-to-all-done.freq), channel_id=2, replica_groups={{0,1},{2,3},{4,5},{6,7},{8,9},{10,11},{12,13},{14,15},{16,17},{18,19},{..., dimensions={0}, use_global_device_ids=true | all-gather | bytes 835584 | tf_op jit(solution)/shard_map/all_gather | solution.py:493
  40.9 2.7 %far_features.1.far = bf16[1024,1024]{1,0:T(8,128)(2,1)S(1)} custom-call(s32[1]{0:T(128)} %bitcast.1.core, bf16[1024,128]{1,0:T(8,128)(2,1)S(1)} %stage_cov.1.cov, bf16[2,8,136,128]{3,2,1,0:T(8,128)(2,1)S(1)} %bitcast.14), custom_call_target="tpu_custom_call" | custom-call | flops 289406976 | bytes 2097152 | tf_op jit(solution)/shard_map/far_features/pallas_call | solution.py:166
  43.7 0.0 copy-start
  43.7 0.8 copy-done
  44.5 3.8 %all-to-all-done.1 = f32[32,8,128]{2,1,0:T(8,128)S(1)} async-done(((f32[32,8,128]{2,1,0:T(8,128)}), f32[32,8,128]{2,1,0:T(8,128)S(1)}, u32[]{:S(2)}, u32[]{:S(2)}) %all-to-all-start.1) | async-done | bytes 131104 | tf_op jit(solution)/shard_map/all_to_all | solution.py:492
  48.3 2.0 %all-gather.1 = f32[64,8,128]{2,1,0:T(8,128)S(1)} all-gather(f32[32,8,128]{2,1,0:T(8,128)S(1)} %all-to-all-done.1), channel_id=3, replica_groups={{0,1},{2,3},{4,5},{6,7},{8,9},{10,11},{12,13},{14,15},{16,17},{18,19},{..., dimensions={0}, use_global_device_ids=true | all-gather | bytes 393216 | tf_op jit(solution)/shard_map/all_gather | solution.py:496
  50.3 2.5 %first_product.1 = (f32[32,16,128]{2,1,0:T(8,128)S(1)}, f32[1,1024]{1,0:T(1,128)S(1)}, f32[16,128]{1,0:T(8,128)S(1)}) custom-call(s32[1]{0:T(128)} %bitcast.1.core, f32[2,32,8,128]{3,2,1,0:T(8,128)S(1)} %bitcast.16, bf16[512,1024]{1,0:T(8,128)(2,1)S(1)} %get-tuple-element.45.kept, bf16[9216,1024]{1,0:T(8,128)(2,1)} %get-tuple-element.46.rest, ...), custom_call_target="tpu_custom_call" | custom-call | flops 134217728 | bytes 4194304 | tf_op jit(solution)/shard_map/first_product/pallas_call | solution.py:504
  52.8 0.0 copy-start.2
  52.8 0.7 copy-done.2
  53.5 6.0 %all-to-all-start.2 = ((f32[32,16,128]{2,1,0:T(8,128)}), f32[32,16,128]{2,1,0:T(8,128)S(1)}, u32[]{:S(2)}, u32[]{:S(2)}) async-start(f32[32,16,128]{2,1,0:T(8,128)} %copy-done.2), calls=%async_computation.2 | async-start | bytes 524288 | tf_op jit(solution)/shard_map/all_to_all | solution.py:515
  59.4 0.0 copy-start.3
  59.4 0.0 copy-start.4
  59.5 7.1 %node_features_a.1.phi = bf16[4608,2048]{1,0:T(8,128)(2,1)} custom-call(s32[1]{0:T(128)} %bitcast.1.core, bf16[1024,128]{1,0:T(8,128)(2,1)} %constant_dynamic-slice_fusion.cov, bf16[2,8,136,128]{3,2,1,0:T(8,128)(2,1)} %bitcast.15), custom_call_target="tpu_custom_call" | custom-call | flops 578813952 | bytes 4194304 | tf_op jit(solution)/shard_map/node_features_a/pallas_call | solution.py:207
  66.6 5.3 %all-to-all-done.2.arrived = f32[32,16,128]{2,1,0:T(8,128)S(1)} async-done(((f32[32,16,128]{2,1,0:T(8,128)}), f32[32,16,128]{2,1,0:T(8,128)S(1)}, u32[]{:S(2)}, u32[]{:S(2)}) %all-to-all-start.2) | async-done | bytes 262176 | tf_op jit(solution)/shard_map/all_to_all | solution.py:515
  71.9 2.5 %second_product.1 = (f32[32,16,128]{2,1,0:T(8,128)S(1)}, f32[2,1024]{1,0:T(2,128)S(1)}, f32[16,128]{1,0:T(8,128)S(1)}, f32[16,128]{1,0:T(8,128)S(1)}, f32[16,128]{1,0:T(8,128)S(1)}) custom-call(f32[32,16,128]{2,1,0:T(8,128)S(1)} %all-to-all-done.2.arrived, f32[16,128]{1,0:T(8,128)S(1)} %get-tuple-element.53.rhs, f32[1,1024]{1,0:T(1,128)S(1)} %get-tuple-element.54.before, ...), custom_call_target="tpu_custom_call" | custom-call | flops 134217728 | bytes 4194304 | tf_op jit(solution)/shard_map/second_product/pallas_call | solution.py:519
  74.4 16.1 %all_to_all.25.arrived = f32[32,16,128]{2,1,0:T(8,128)S(1)} all-to-all(f32[32,16,128]{2,1,0:T(8,128)S(1)} %get-tuple-element.55), channel_id=1, replica_groups=mesh['blk'=32,'col'=16] {'blk'}, dimensions={0} | all-to-all | bytes 524288 | tf_op jit(solution)/shard_map/all_to_all | solution.py:529
  90.6 0.0 copy-done.3
  90.6 0.0 copy-done.4
  90.6 0.0 copy-start.5
  90.6 0.0 copy-start.6
  90.6 2.9 %third_product.1 = (f32[32,4,128]{2,1,0:T(4,128)}, f32[2,16,128]{2,1,0:T(8,128)S(1)}, f32[8,128]{1,0:T(8,128)S(1)}) custom-call(f32[32,16,128]{2,1,0:T(8,128)S(1)} %all_to_all.25.arrived, f32[16,128]{1,0:T(8,128)S(1)} %get-tuple-element.56.solution, f32[16,128]{1,0:T(8,128)S(1)} %get-tuple-element.57.residual, f32[16,128]{1,0:T(8,128)S(1)} %get-tuple-element.58.direction, ...), custom_call_target="tpu_custom_call" | custom-call | flops 134217728 | bytes 4194304 | tf_op jit(solution)/shard_map/third_product/pallas_call | solution.py:530
  93.5 4.7 %all-to-all-start.4 = ((f32[32,4,128]{2,1,0:T(4,128)}), f32[32,4,128]{2,1,0:T(4,128)S(1)}, u32[]{:S(2)}, u32[]{:S(2)}) async-start(f32[32,4,128]{2,1,0:T(4,128)} %get-tuple-element.62), calls=%async_computation.4 | async-start | bytes 131072 | tf_op jit(solution)/shard_map/all_to_all | solution.py:545
  98.2 3.0 %node_values.1 = f32[2,1024]{1,0:T(2,128)S(1)} custom-call(f32[2,16,128]{2,1,0:T(8,128)S(1)} %get-tuple-element.63.both, bf16[4608,2048]{1,0:T(8,128)(2,1)} %node_features_a.1.phi), custom_call_target="tpu_custom_call" | custom-call | flops 268435456 | bytes 8388608 | tf_op jit(solution)/shard_map/node_values/pallas_call | solution.py:546
  101.2 1.8 %all-gather.3.node_values = f32[2,2,1024]{2,1,0:T(2,128)S(1)} all-gather(f32[1,2,1024]{2,1,0:T(2,128)S(1)} %bitcast.17), channel_id=4, replica_groups={{0,1},{2,3},{4,5},{6,7},{8,9},{10,11},{12,13},{14,15},{16,17},{18,19},{..., dimensions={0}, use_global_device_ids=true | all-gather | bytes 24576 | tf_op jit(solution)/shard_map/all_gather | solution.py:560
  103.0 4.0 %all-to-all-done.4.arrived = f32[32,4,128]{2,1,0:T(4,128)S(1)} async-done(((f32[32,4,128]{2,1,0:T(4,128)}), f32[32,4,128]{2,1,0:T(4,128)S(1)}, u32[]{:S(2)}, u32[]{:S(2)}) %all-to-all-start.4) | async-done | bytes 65568 | tf_op jit(solution)/shard_map/all_to_all | solution.py:545
  107.0 0.0 copy-done.5
  107.0 0.0 copy-done.6
  107.0 0.7 last.1
  (1 shorter events, 0.0 us)
Async XLA Ops:
  2.2 22.6 %all-to-all-start = ((bf16[8,136,128]{2,1,0:T(8,128)(2,1)}), bf16[8,136,128]{2,1,0:T(8,128)(2,1)S(1)}, u32[]{:S(2)}, u32[]{:S(2)}) async-start(bf16[8,136,128]{2,1,0:T(8,128)(2,1)} %pack.1), calls=%async_computation | async-start | bytes 557056 | tf_op jit(solution)/shard_map/all_to_all | solution.py:463
  12.5 0.9 copy-start.1
  28.6 19.7 %all-to-all-start.1 = ((f32[32,8,128]{2,1,0:T(8,128)}), f32[32,8,128]{2,1,0:T(8,128)S(1)}, u32[]{:S(2)}, u32[]{:S(2)}) async-start(f32[32,8,128]{2,1,0:T(8,128)} %get-tuple-element.42), calls=%async_computation.1 | async-start | bytes 262144 | tf_op jit(solution)/shard_map/all_to_all | solution.py:492
  43.7 0.8 copy-start
  52.8 0.7 copy-start.2
  53.5 18.4 %all-to-all-start.2 = ((f32[32,16,128]{2,1,0:T(8,128)}), f32[32,16,128]{2,1,0:T(8,128)S(1)}, u32[]{:S(2)}, u32[]{:S(2)}) async-start(f32[32,16,128]{2,1,0:T(8,128)} %copy-done.2), calls=%async_computation.2 | async-start | bytes 524288 | tf_op jit(solution)/shard_map/all_to_all | solution.py:515
  59.4 31.1 %copy-start.3 = (s32[1024,1]{0,1:T(1,128)S(1)}, s32[1024,1]{0,1:T(1,128)}, u32[]{:S(2)}) copy-start(s32[1024,1]{0,1:T(1,128)} %param.13) | copy-start | bytes 12292
  59.4 31.1 %copy-start.4 = (s32[1024]{0:T(1024)S(1)}, s32[1024]{0:T(1024)}, u32[]{:S(2)}) copy-start(s32[1024]{0:T(1024)} %param.14) | copy-start | bytes 12292
  90.6 16.4 %copy-start.5 = (f32[128]{0:T(128)S(1)}, f32[128]{0:T(128)}, u32[]{:S(2)}) copy-start(f32[128]{0:T(128)} %param.18) | copy-start | bytes 1540
  90.6 16.4 %copy-start.6 = (s32[128]{0:T(128)S(1)}, s32[128]{0:T(128)}, u32[]{:S(2)}) copy-start(s32[128]{0:T(128)} %param.19) | copy-start | bytes 1540
  93.5 13.5 %all-to-all-start.4 = ((f32[32,4,128]{2,1,0:T(4,128)}), f32[32,4,128]{2,1,0:T(4,128)S(1)}, u32[]{:S(2)}, u32[]{:S(2)}) async-start(f32[32,4,128]{2,1,0:T(4,128)} %get-tuple-element.62), calls=%async_computation.4 | async-start | bytes 131072 | tf_op jit(solution)/shard_map/all_to_all | solution.py:545

commit v9 on v8

--- a/solution.py
+++ b/solution.py
@@ -270,9 +270,9 @@
 
 
 def fetch(rest, held, sems):
-    part = held.shape[0] // PARTS
+    part = held.shape[0]
     copies = []
-    for k in range(PARTS):
+    for k in range(1):
         at = slice(k * part, (k + 1) * part)
         copy = pltpu.make_async_copy(rest.at[at], held.at[at], sems.at[k])
         copy.start()

time: 108 us -> 108 us (level)
  no operation moved by 1% of the time
where the time goes in v9:
time: 108 us; the launch traced here: 107 us
  starting transfers between devices  31.1 us (29%)
  Pallas kernels  26.1 us (24%)
  blocking collectives  22.2 us (21%)
  waiting for transfers between devices  21 us (19%)
  local copies, waits for them, and re-layouts  5.73 us (5%)
    all_to_all x3, starting transfers between devices, on_device(): arrived = lax.all_to_all(sent, 'blk', 0, 0, tiled=True)  20.8 us
    all_to_all x1, blocking collectives, on_device(): arrived = lax.all_to_all(sent, 'blk', 0, 0, tiled=True)  16.1 us
    all_to_all x3, waiting for transfers between devices, on_device(): arrived = lax.all_to_all(sent, 'blk', 0, 0, tiled=True)  13.1 us
    all_to_all x1, starting transfers between devices, on_device(): lax.all_to_all(packed, 'col', 0, 0, tiled=True, axis_index_groups=same_core)  10.3 us
    all_to_all x1, waiting for transfers between devices, on_device(): lax.all_to_all(packed, 'col', 0, 0, tiled=True, axis_index_groups=same_core)  7.95 us
    pallas_call x1, Pallas kernels, node_features(): pl.pallas_call(functools.partial(node_kernel, first), in_specs=[SMEM, VME...  7.15 us
    pallas_call x1, Pallas kernels, on_device(): pl.pallas_call(near_kernel, in_specs=[VMEM] * 4, out_specs=[VMEM, HBM, VM...  3.79 us
    pallas_call x1, Pallas kernels, on_device(): pl.pallas_call(nodes_kernel, grid=(count // NODE_ROWS,), in_specs=[pl.Blo...  2.98 us
  transfers between devices with their start and end apart: 4, of which 4 were waited for; matrix products, arithmetic and copies ran while one was open for 3% of the time, Pallas kernels for 12%

profile of v9, /device:TPU:8, one launch (start us, length us, event | category | flops | bytes accessed | tf_op | source)
XLA Modules:
  0.0 106.9 jit_solution(11516236803729945150)
XLA Ops:
  0.6 1.6 %pack.1 = bf16[8,136,128]{2,1,0:T(8,128)(2,1)} custom-call(bf16[128,128]{1,0:T(8,128)(2,1)} %freq.1, bf16[1,128]{1,0:T(2,128)(2,1)} %bitcast.24), custom_call_target="tpu_custom_call" | custom-call | tf_op jit(solution)/shard_map/pack/pallas_call | solution.py:449
  2.2 10.3 %all-to-all-start = ((bf16[8,136,128]{2,1,0:T(8,128)(2,1)}), bf16[8,136,128]{2,1,0:T(8,128)(2,1)S(1)}, u32[]{:S(2)}, u32[]{:S(2)}) async-start(bf16[8,136,128]{2,1,0:T(8,128)(2,1)} %pack.1), calls=%async_computation | async-start | bytes 557056 | tf_op jit(solution)/shard_map/all_to_all | solution.py:463
  12.5 0.0 copy-start.1
  12.5 0.9 copy-done.1
  13.5 0.7 reshape.44.weight
  14.2 0.7 reshape.45.size
  14.9 1.2 %copy.13 = bf16[16,128,128]{2,1,0:T(8,128)(2,1)S(1)} copy(bf16[16,128,128]{2,0,1:T(8,128)(2,1)} %bitcast.23) | data formatting | bytes 1048576 | tf_op jit(solution)/shard_map/transpose | solution.py:465
  16.1 0.7 constant_dynamic-slice_fusion.cov
  16.8 8.0 %all-to-all-done.freq = bf16[8,136,128]{2,1,0:T(8,128)(2,1)S(1)} async-done(((bf16[8,136,128]{2,1,0:T(8,128)(2,1)}), bf16[8,136,128]{2,1,0:T(8,128)(2,1)S(1)}, u32[]{:S(2)}, u32[]{:S(2)}) %all-to-all-start) | async-done | bytes 278560 | tf_op jit(solution)/shard_map/all_to_all | solution.py:463
  24.7 3.8 %near_features.1 = (bf16[512,1024]{1,0:T(8,128)(2,1)S(1)}, bf16[9216,1024]{1,0:T(8,128)(2,1)}, f32[32,8,128]{2,1,0:T(8,128)}) custom-call(bf16[1024,128]{1,0:T(8,128)(2,1)S(1)} %stage_cov.1.cov, bf16[8,136,128]{2,1,0:T(8,128)(2,1)S(1)} %all-to-all-done.freq, bf16[1,1024]{1,0:T(2,128)(2,1)S(1)} %reshape.44.weight, bf16[1,1024]{1,0:T(2,128)(2,1)S(1)} %reshape.45.size), custom_call_target="tpu_custom_call" | custom-call | tf_op jit(solution)/shard_map/near_features/pallas_call | solution.py:473
  28.6 10.2 %all-to-all-start.1 = ((f32[32,8,128]{2,1,0:T(8,128)}), f32[32,8,128]{2,1,0:T(8,128)S(1)}, u32[]{:S(2)}, u32[]{:S(2)}) async-start(f32[32,8,128]{2,1,0:T(8,128)} %get-tuple-element.42), calls=%async_computation.1 | async-start | bytes 262144 | tf_op jit(solution)/shard_map/all_to_all | solution.py:492
  38.7 2.2 %all-gather = bf16[16,136,128]{2,1,0:T(8,128)(2,1)S(1)} all-gather(bf16[8,136,128]{2,1,0:T(8,128)(2,1)S(1)} %all-to-all-done.freq), channel_id=2, replica_groups={{0,1},{2,3},{4,5},{6,7},{8,9},{10,11},{12,13},{14,15},{16,17},{18,19},{..., dimensions={0}, use_global_device_ids=true | all-gather | bytes 835584 | tf_op jit(solution)/shard_map/all_gather | solution.py:493
  40.9 2.7 %far_features.1.far = bf16[1024,1024]{1,0:T(8,128)(2,1)S(1)} custom-call(s32[1]{0:T(128)} %bitcast.1.core, bf16[1024,128]{1,0:T(8,128)(2,1)S(1)} %stage_cov.1.cov, bf16[2,8,136,128]{3,2,1,0:T(8,128)(2,1)S(1)} %bitcast.14), custom_call_target="tpu_custom_call" | custom-call | flops 289406976 | bytes 2097152 | tf_op jit(solution)/shard_map/far_features/pallas_call | solution.py:166
  43.7 0.0 copy-start
  43.7 0.8 copy-done
  44.5 3.8 %all-to-all-done.1 = f32[32,8,128]{2,1,0:T(8,128)S(1)} async-done(((f32[32,8,128]{2,1,0:T(8,128)}), f32[32,8,128]{2,1,0:T(8,128)S(1)}, u32[]{:S(2)}, u32[]{:S(2)}) %all-to-all-start.1) | async-done | bytes 131104 | tf_op jit(solution)/shard_map/all_to_all | solution.py:492
  48.3 2.0 %all-gather.1 = f32[64,8,128]{2,1,0:T(8,128)S(1)} all-gather(f32[32,8,128]{2,1,0:T(8,128)S(1)} %all-to-all-done.1), channel_id=3, replica_groups={{0,1},{2,3},{4,5},{6,7},{8,9},{10,11},{12,13},{14,15},{16,17},{18,19},{..., dimensions={0}, use_global_device_ids=true | all-gather | bytes 393216 | tf_op jit(solution)/shard_map/all_gather | solution.py:496
  50.3 2.3 %first_product.1 = (f32[32,16,128]{2,1,0:T(8,128)S(1)}, f32[1,1024]{1,0:T(1,128)S(1)}, f32[16,128]{1,0:T(8,128)S(1)}) custom-call(s32[1]{0:T(128)} %bitcast.1.core, f32[2,32,8,128]{3,2,1,0:T(8,128)S(1)} %bitcast.16, bf16[512,1024]{1,0:T(8,128)(2,1)S(1)} %get-tuple-element.45.kept, bf16[9216,1024]{1,0:T(8,128)(2,1)} %get-tuple-element.46.rest, ...), custom_call_target="tpu_custom_call" | custom-call | flops 134217728 | bytes 4194304 | tf_op jit(solution)/shard_map/first_product/pallas_call | solution.py:504
  52.6 0.0 copy-start.2
  52.6 0.7 copy-done.2
  53.3 6.0 %all-to-all-start.2 = ((f32[32,16,128]{2,1,0:T(8,128)}), f32[32,16,128]{2,1,0:T(8,128)S(1)}, u32[]{:S(2)}, u32[]{:S(2)}) async-start(f32[32,16,128]{2,1,0:T(8,128)} %copy-done.2), calls=%async_computation.2 | async-start | bytes 524288 | tf_op jit(solution)/shard_map/all_to_all | solution.py:515
  59.2 0.0 copy-start.3
  59.2 0.0 copy-start.4
  59.3 7.1 %node_features_a.1.phi = bf16[4608,2048]{1,0:T(8,128)(2,1)} custom-call(s32[1]{0:T(128)} %bitcast.1.core, bf16[1024,128]{1,0:T(8,128)(2,1)} %constant_dynamic-slice_fusion.cov, bf16[2,8,136,128]{3,2,1,0:T(8,128)(2,1)} %bitcast.15), custom_call_target="tpu_custom_call" | custom-call | flops 578813952 | bytes 4194304 | tf_op jit(solution)/shard_map/node_features_a/pallas_call | solution.py:207
  66.4 5.3 %all-to-all-done.2.arrived = f32[32,16,128]{2,1,0:T(8,128)S(1)} async-done(((f32[32,16,128]{2,1,0:T(8,128)}), f32[32,16,128]{2,1,0:T(8,128)S(1)}, u32[]{:S(2)}, u32[]{:S(2)}) %all-to-all-start.2) | async-done | bytes 262176 | tf_op jit(solution)/shard_map/all_to_all | solution.py:515
  71.7 2.3 %second_product.1 = (f32[32,16,128]{2,1,0:T(8,128)S(1)}, f32[2,1024]{1,0:T(2,128)S(1)}, f32[16,128]{1,0:T(8,128)S(1)}, f32[16,128]{1,0:T(8,128)S(1)}, f32[16,128]{1,0:T(8,128)S(1)}) custom-call(f32[32,16,128]{2,1,0:T(8,128)S(1)} %all-to-all-done.2.arrived, f32[16,128]{1,0:T(8,128)S(1)} %get-tuple-element.53.rhs, f32[1,1024]{1,0:T(1,128)S(1)} %get-tuple-element.54.before, ...), custom_call_target="tpu_custom_call" | custom-call | flops 134217728 | bytes 4194304 | tf_op jit(solution)/shard_map/second_product/pallas_call | solution.py:519
  74.0 16.1 %all_to_all.25.arrived = f32[32,16,128]{2,1,0:T(8,128)S(1)} all-to-all(f32[32,16,128]{2,1,0:T(8,128)S(1)} %get-tuple-element.55), channel_id=1, replica_groups=mesh['blk'=32,'col'=16] {'blk'}, dimensions={0} | all-to-all | bytes 524288 | tf_op jit(solution)/shard_map/all_to_all | solution.py:529
  90.1 0.0 copy-done.3
  90.1 0.0 copy-done.4
  90.1 0.0 copy-start.5
  90.1 0.0 copy-start.6
  90.1 2.6 %third_product.1 = (f32[32,4,128]{2,1,0:T(4,128)}, f32[2,16,128]{2,1,0:T(8,128)S(1)}, f32[8,128]{1,0:T(8,128)S(1)}) custom-call(f32[32,16,128]{2,1,0:T(8,128)S(1)} %all_to_all.25.arrived, f32[16,128]{1,0:T(8,128)S(1)} %get-tuple-element.56.solution, f32[16,128]{1,0:T(8,128)S(1)} %get-tuple-element.57.residual, f32[16,128]{1,0:T(8,128)S(1)} %get-tuple-element.58.direction, ...), custom_call_target="tpu_custom_call" | custom-call | flops 134217728 | bytes 4194304 | tf_op jit(solution)/shard_map/third_product/pallas_call | solution.py:530
  92.7 4.7 %all-to-all-start.4 = ((f32[32,4,128]{2,1,0:T(4,128)}), f32[32,4,128]{2,1,0:T(4,128)S(1)}, u32[]{:S(2)}, u32[]{:S(2)}) async-start(f32[32,4,128]{2,1,0:T(4,128)} %get-tuple-element.62), calls=%async_computation.4 | async-start | bytes 131072 | tf_op jit(solution)/shard_map/all_to_all | solution.py:545
  97.4 3.0 %node_values.1 = f32[2,1024]{1,0:T(2,128)S(1)} custom-call(f32[2,16,128]{2,1,0:T(8,128)S(1)} %get-tuple-element.63.both, bf16[4608,2048]{1,0:T(8,128)(2,1)} %node_features_a.1.phi), custom_call_target="tpu_custom_call" | custom-call | flops 268435456 | bytes 8388608 | tf_op jit(solution)/shard_map/node_values/pallas_call | solution.py:546
  100.4 1.8 %all-gather.3.node_values = f32[2,2,1024]{2,1,0:T(2,128)S(1)} all-gather(f32[1,2,1024]{2,1,0:T(2,128)S(1)} %bitcast.17), channel_id=4, replica_groups={{0,1},{2,3},{4,5},{6,7},{8,9},{10,11},{12,13},{14,15},{16,17},{18,19},{..., dimensions={0}, use_global_device_ids=true | all-gather | bytes 24576 | tf_op jit(solution)/shard_map/all_gather | solution.py:560
  102.2 4.0 %all-to-all-done.4.arrived = f32[32,4,128]{2,1,0:T(4,128)S(1)} async-done(((f32[32,4,128]{2,1,0:T(4,128)}), f32[32,4,128]{2,1,0:T(4,128)S(1)}, u32[]{:S(2)}, u32[]{:S(2)}) %all-to-all-start.4) | async-done | bytes 65568 | tf_op jit(solution)/shard_map/all_to_all | solution.py:545
  106.2 0.0 copy-done.5
  106.2 0.0 copy-done.6
  106.2 0.7 last.1
  (1 shorter events, 0.0 us)
Async XLA Ops:
  2.2 22.6 %all-to-all-start = ((bf16[8,136,128]{2,1,0:T(8,128)(2,1)}), bf16[8,136,128]{2,1,0:T(8,128)(2,1)S(1)}, u32[]{:S(2)}, u32[]{:S(2)}) async-start(bf16[8,136,128]{2,1,0:T(8,128)(2,1)} %pack.1), calls=%async_computation | async-start | bytes 557056 | tf_op jit(solution)/shard_map/all_to_all | solution.py:463
  12.5 0.9 copy-start.1
  28.6 19.7 %all-to-all-start.1 = ((f32[32,8,128]{2,1,0:T(8,128)}), f32[32,8,128]{2,1,0:T(8,128)S(1)}, u32[]{:S(2)}, u32[]{:S(2)}) async-start(f32[32,8,128]{2,1,0:T(8,128)} %get-tuple-element.42), calls=%async_computation.1 | async-start | bytes 262144 | tf_op jit(solution)/shard_map/all_to_all | solution.py:492
  43.7 0.8 copy-start
  52.6 0.7 copy-start.2
  53.3 18.4 %all-to-all-start.2 = ((f32[32,16,128]{2,1,0:T(8,128)}), f32[32,16,128]{2,1,0:T(8,128)S(1)}, u32[]{:S(2)}, u32[]{:S(2)}) async-start(f32[32,16,128]{2,1,0:T(8,128)} %copy-done.2), calls=%async_computation.2 | async-start | bytes 524288 | tf_op jit(solution)/shard_map/all_to_all | solution.py:515
  59.2 30.9 %copy-start.3 = (s32[1024,1]{0,1:T(1,128)S(1)}, s32[1024,1]{0,1:T(1,128)}, u32[]{:S(2)}) copy-start(s32[1024,1]{0,1:T(1,128)} %param.13) | copy-start | bytes 12292
  59.2 30.9 %copy-start.4 = (s32[1024]{0:T(1024)S(1)}, s32[1024]{0:T(1024)}, u32[]{:S(2)}) copy-start(s32[1024]{0:T(1024)} %param.14) | copy-start | bytes 12292
  90.1 16.1 %copy-start.5 = (f32[128]{0:T(128)S(1)}, f32[128]{0:T(128)}, u32[]{:S(2)}) copy-start(f32[128]{0:T(128)} %param.18) | copy-start | bytes 1540
  90.1 16.1 %copy-start.6 = (s32[128]{0:T(128)S(1)}, s32[128]{0:T(128)}, u32[]{:S(2)}) copy-start(s32[128]{0:T(128)} %param.19) | copy-start | bytes 1540
  92.7 13.5 %all-to-all-start.4 = ((f32[32,4,128]{2,1,0:T(4,128)}), f32[32,4,128]{2,1,0:T(4,128)S(1)}, u32[]{:S(2)}, u32[]{:S(2)}) async-start(f32[32,4,128]{2,1,0:T(4,128)} %get-tuple-element.62), calls=%async_computation.4 | async-start | bytes 131072 | tf_op jit(solution)/shard_map/all_to_all | solution.py:545
